TPU v7x, 32 devices: a whole 2x2x4 slice. The times are simulated.
32 devices in a mesh: group: 2 (over x), clus: 16 (over z, y, core).
Axes of the slice: x: 2, y: 2, z: 4, core: 2. Of those that a mesh axis runs over, the one named last changes fastest.
Arguments:
- block_vectors: float32 [512, 32, 256], P(('group', 'clus')), parts along dimension 0, may hold values from -6 to 6
- prior_vectors: float32 [512, 32, 256], P(('group', 'clus')), parts along dimension 0, may hold values from -6 to 6
- prior_beta: float32 [64, 32], P('group'), parts along dimension 0, may hold values from -1.2 to 1.2
- points: bfloat16 [512, 3, 256], P(('group', 'clus')), parts along dimension 0, may hold values from 0 to 1.3
- basis: bfloat16 [512, 32, 256], P(('group', 'clus')), parts along dimension 0, may hold values from -0.375 to 0.375
- scales: float32 [512, 32], P(('group', 'clus')), parts along dimension 0, may hold values from 0.5 to 2
- skeleton: bfloat16 [512, 3, 32], P(('group', 'clus')), parts along dimension 0, may hold values from 0 to 1.3
- near_pairs: int32 [32, 16, 3, 2], P(('group', 'clus')), parts along dimension 0, may hold values from -1 to 15, as said below
- far_ids: int32 [512, 64], P(('group', 'clus')), parts along dimension 0, may hold values from 0 to 255
Outputs:
- next_vectors: float32 [512, 32, 256], P(('group', 'clus')), parts along dimension 0
- alpha_block: float32 [64, 32], P('group'), parts along dimension 0
- beta_block: float32 [64, 32], P('group'), parts along dimension 0
There are 2 independent parts, one for each index of `group`. A program takes and returns all parts, laid end to end along the dimension named above; each array names one. Nothing has to cross between parts.
Inputs may be any that keep to these rules, and one draw needn't show every extreme that they name: near_pairs[o, p, t, 0] is -1 for an empty entry, else a row cluster index local to device o; near_pairs[o, p, t, 1] is a cluster index local to device p and differs from near_pairs[o, p, t, 0]. The share of live entries differs from device to device; in every draw all entries of some device are live.
All inputs are finite; a program needn't handle non-finite values.
Results may differ from a plain program's by a relative error of at most 0.0045.
Values may be sent and summed in bfloat16 or wider, within the bound.
No kernel may reach another device: no remote copies, remote signals or barrier semaphores. Data moves between devices by JAX's collectives and lax.ppermute only.
A program may use at most 128 MiB of HBM per device.

v0:
```python
import jax
import jax.numpy as jnp
from jax import lax
from jax.sharding import PartitionSpec as P

root_three = 1.7320508075688772
length_scale = 0.15


def kernel_tile(left_points, right_points):
    left_wide = left_points.astype(jnp.float32)
    right_wide = right_points.astype(jnp.float32)
    difference = left_wide[..., 0, :, None] - right_wide[..., 0, None, :]
    squared = difference * difference
    for coordinate in range(1, 3):
        difference = left_wide[..., coordinate, :, None] - right_wide[..., coordinate, None, :]
        squared = squared + difference * difference
    scaled = jnp.sqrt(squared) * (root_three / length_scale)
    return (1.0 + scaled) * jnp.exp(-scaled)


def inner_products(first_block, second_block):
    return jnp.einsum("cub,cvb->uv", first_block, second_block, precision=lax.Precision.HIGHEST)


def local(
    block_vectors, prior_vectors, prior_beta, points, basis, scales, skeleton, near_pairs, far_ids
):
    highest = lax.Precision.HIGHEST
    clusters, vec_count, cluster_size = block_vectors.shape
    devices_count = lax.axis_size("clus")
    total_points = devices_count * clusters * cluster_size
    slot_count = near_pairs.shape[2]
    per_turn = 8 * slot_count
    turn_count = devices_count // 8
    half_vectors = block_vectors.astype(jnp.bfloat16)
    pair_rows = near_pairs[0, :, :, 0]
    pair_partners = near_pairs[0, :, :, 1]
    rank_count = basis.shape[1]
    far_count = far_ids.shape[1]
    projected = jnp.einsum("crb,cvb->crv", basis, half_vectors, preferred_element_type=jnp.float32)
    sources = (
        (scales[:, :, None] * projected)
        .astype(jnp.bfloat16)
        .reshape(clusters, rank_count * vec_count)
    )
    all_sources, all_skeleton = (
        lax.all_gather(sources, "clus", axis=0, tiled=True),
        lax.all_gather(skeleton, "clus", axis=0, tiled=True),
    )
    far_flat = far_ids.reshape(-1)
    far_sources = jnp.take(all_sources, far_flat, axis=0).reshape(
        clusters, far_count, rank_count, vec_count
    )
    far_skeleton = jnp.take(all_skeleton, far_flat, axis=0).reshape(
        clusters, far_count, 3, rank_count
    )
    coupling = kernel_tile(skeleton[:, None], far_skeleton).astype(jnp.bfloat16)
    gathered = jnp.einsum(
        "cfab,cfbv->cav", coupling, far_sources, preferred_element_type=jnp.float32
    )
    lifted = (scales[:, :, None] * gathered).astype(jnp.bfloat16)
    far_term = jnp.einsum("crv,crb->cvb", lifted, basis, preferred_element_type=jnp.float32)
    self_tiles = kernel_tile(points, points).astype(jnp.bfloat16)
    applied = far_term + jnp.einsum(
        "cvb,cba->cva", half_vectors, self_tiles, preferred_element_type=jnp.float32
    )
    live_mask = pair_rows >= 0
    safe_rows = jnp.maximum(pair_rows, 0)
    drop_rows = jnp.where(live_mask, pair_rows, clusters)

    def in_turns(values):
        return values.reshape((turn_count, per_turn) + values.shape[2:])

    def direct_part(applied, batch_items):
        safe_ids, drop_ids, live_now, partner_vectors, partner_points = batch_items
        own_points = jnp.take(points, safe_ids, axis=0)
        kernel_tiles = kernel_tile(partner_points, own_points).astype(jnp.bfloat16)
        direct = jnp.einsum(
            "gvb,gba->gva", partner_vectors, kernel_tiles, preferred_element_type=jnp.float32
        )
        return (applied.at[drop_ids].add(direct, mode="drop"), kernel_tiles)

    def paired_turn(applied, batch_items):
        applied, kernel_tiles = direct_part(applied, batch_items)
        own_vectors = jnp.take(half_vectors, batch_items[0], axis=0)
        mirror = jnp.einsum(
            "gva,gba->gvb", own_vectors, kernel_tiles, preferred_element_type=jnp.float32
        )
        return (applied, jnp.where(batch_items[2][:, None, None], mirror, 0.0).astype(jnp.bfloat16))

    served = lax.all_to_all(pair_partners, "clus", split_axis=0, concat_axis=0, tiled=True)
    served_flat = served.reshape(-1)
    served_vectors = jnp.take(half_vectors, served_flat, axis=0).reshape(
        served.shape + (vec_count, cluster_size)
    )
    served_points = jnp.take(points, served_flat, axis=0).reshape(served.shape + (3, cluster_size))
    served_vectors, served_points = (served_vectors, served_points)
    fetched_vectors, fetched_points = (
        lax.all_to_all(served_vectors, "clus", split_axis=0, concat_axis=0, tiled=True),
        lax.all_to_all(served_points, "clus", split_axis=0, concat_axis=0, tiled=True),
    )
    applied, mirrors = lax.scan(
        paired_turn,
        applied,
        (
            in_turns(safe_rows),
            in_turns(drop_rows),
            in_turns(live_mask),
            in_turns(fetched_vectors),
            in_turns(fetched_points),
        ),
    )
    returned = lax.all_to_all(
        mirrors.reshape(served.shape + (vec_count, cluster_size)),
        "clus",
        split_axis=0,
        concat_axis=0,
        tiled=True,
    )
    applied = applied.at[served.reshape(-1)].add(
        returned.reshape(-1, vec_count, cluster_size).astype(jnp.float32)
    )
    alpha_block = lax.psum(inner_products(block_vectors, applied), "clus") / total_points
    residual = applied - jnp.einsum("uv,cub->cvb", alpha_block, block_vectors, precision=highest)
    residual = residual - jnp.einsum("vu,cub->cvb", prior_beta, prior_vectors, precision=highest)
    gram_matrix = lax.psum(inner_products(residual, residual), "clus") / total_points
    factor = jnp.linalg.cholesky(gram_matrix)
    inverse = lax.linalg.triangular_solve(
        factor, jnp.eye(vec_count, dtype=jnp.float32), left_side=True, lower=True
    )
    next_vectors = jnp.einsum("uv,cvb->cub", inverse, residual, precision=highest)
    return (next_vectors, alpha_block, factor.T)


def solution(mesh):
    placed = (
        P(("group", "clus"), None, None),
        P(("group", "clus"), None, None),
        P("group", None),
        P(("group", "clus"), None, None),
        P(("group", "clus"), None, None),
        P(("group", "clus"), None),
        P(("group", "clus"), None, None),
        P(("group", "clus"), None, None, None),
        P(("group", "clus"), None),
    )
    return jax.shard_map(
        local,
        mesh=mesh,
        in_specs=placed,
        out_specs=(P(("group", "clus"), None, None), P("group", None), P("group", None)),
        check_vma=False,
    )
```

profile of v0, /device:TPU:0, one launch (start us, length us, event | category | flops | bytes accessed | tf_op | source)
XLA Modules:
  0.0 329.5 jit_solution(5952822724726559660)
XLA Ops:
  2.1 7.4 %all-to-all-start = ((s32[16,1,3]{2,1,0:T(1,128)}), s32[16,1,3]{2,1,0:T(1,128)S(1)}, u32[]{:S(2)}, u32[]{:S(2)}) async-start(s32[16,1,3]{2,1,0:T(1,128)} %copy.56), calls=%async_computation | async-start | bytes 16384 | tf_op jit(solution)/shard_map/all_to_all | solution.py:92
  11.0 23.9 %all_gather.6 = bf16[256,3,32]{2,0,1:T(8,128)(2,1)} all-gather(bf16[16,3,32]{2,0,1:T(8,128)(2,1)} %param.17), channel_id=1, replica_groups=mesh['group'=2,'clus'=16] {'clus'}, dimensions={0}, use_global_device_ids=true | all-gather | bytes 52224 | tf_op jit(solution)/shard_map/all_gather | solution.py:49
  39.3 18.9 %all_gather.7 = bf16[256,1024]{1,0:T(8,128)(2,1)S(1)} all-gather(bf16[16,1024]{1,0:T(8,128)(2,1)S(1)} %reshape.213), channel_id=1, replica_groups=mesh['group'=2,'clus'=16] {'clus'}, dimensions={0}, use_global_device_ids=true | all-gather | bytes 557056 | tf_op jit(solution)/shard_map/all_gather | solution.py:48
  58.2 4.1 %gather_fusion.3 = bf16[1024,1024]{1,0:T(8,128)(2,1)S(1)} fusion(bf16[256,1024]{1,0:T(8,128)(2,1)S(1)} %all_gather.7, s32[1024]{0:T(1024)S(1)} %broadcast_clamp_fusion), kind=kCustom, calls=%fused_computation.3 | custom fusion | bytes 4198400 | tf_op jit(solution)/shard_map/jit(_take)/gather | solution.py:52
  62.3 2.6 copy.52
  64.9 6.4 %gather.35 = bf16[16,64,32,32]{1,0,3,2:T(8,128)(2,1)} reshape(bf16[1024,1024]{0,1:T(8,128)(2,1)} %copy.52) | data formatting | bytes 4194304 | tf_op jit(solution)/shard_map/jit(_take)/gather | solution.py:52
  71.4 3.6 %gather_fusion.2 = bf16[1024,3,32]{2,1,0:T(4,128)(2,1)S(1)} fusion(bf16[256,3,32]{2,1,0:T(4,128)(2,1)S(1)} %copy.51, s32[1024]{0:T(1024)S(1)} %broadcast_clamp_fusion), kind=kCustom, calls=%fused_computation.2 | custom fusion | bytes 397312 | tf_op jit(solution)/shard_map/jit(_take)/gather | solution.py:55
  75.1 4.6 %broadcast_select_fusion = bf16[16,64,32,32]{1,0,3,2:T(8,128)(2,1)} fusion(bf16[16,64,32,32]{1,0,3,2:T(8,128)(2,1)} %gather.35, pred[16,64]{1,0:T(8,128)(4,1)S(1)} %compare_and_fusion.1), kind=kLoop, calls=%fused_computation.56 | loop fusion | flops 1048576 | bytes 4195328 | tf_op jit(solution)/shard_map/jit(_take)/select_n | solution.py:52
  79.6 1.4 select_convert_fusion.1
  81.0 2.1 fusion.51
  83.3 4.4 %fusion.30 = f32[16,32,256]{2,1,0:T(8,128)} fusion(bf16[16,32,256]{2,1,0:T(8,128)(2,1)S(1)} %convert_element_type.54, f32[16,256]{1,0:T(8,128)S(1)} %copy-done.7, f32[16,256]{1,0:T(8,128)S(1)} %copy-done.8, f32[16,256]{1,0:T(8,128)S(1)} %copy-done.6), kind=kOutput, calls=%fused_computation.58 | convolution fusion | flops 80740352 | bytes 835584 | tf_op jit(solution)/shard_map/cvb,cba->cva/dot_general | solution.py:65
  87.8 10.0 %copy.53 = bf16[16,64,32,32]{3,2,1,0:T(8,128)(2,1)} copy(bf16[16,64,32,32]{1,0,3,2:T(8,128)(2,1)} %broadcast_select_fusion) | data formatting | bytes 4194304 | tf_op jit(solution)/shard_map/jit(_take)/select_n | solution.py:52
  101.7 3.5 %all-to-all-start.2 = ((bf16[16,3,3,256]{3,1,2,0:T(4,128)(2,1)}), bf16[16,3,3,256]{3,1,2,0:T(4,128)(2,1)S(1)}, u32[]{:S(2)}, u32[]{:S(2)}) async-start(bf16[16,3,3,256]{3,1,2,0:T(4,128)(2,1)} %copy.60), calls=%async_computation.2 | async-start | bytes 196608 | tf_op jit(solution)/shard_map/all_to_all | solution.py:101
  106.2 6.3 %all-to-all-done.2 = bf16[16,3,3,256]{3,1,2,0:T(4,128)(2,1)S(1)} async-done(((bf16[16,3,3,256]{3,1,2,0:T(4,128)(2,1)}), bf16[16,3,3,256]{3,1,2,0:T(4,128)(2,1)S(1)}, u32[]{:S(2)}, u32[]{:S(2)}) %all-to-all-start.2) | async-done | bytes 73760 | tf_op jit(solution)/shard_map/all_to_all | solution.py:101
  112.5 3.8 %all-to-all-start.1 = ((bf16[16,3,32,256]{3,2,1,0:T(8,128)(2,1)}), bf16[16,3,32,256]{3,2,1,0:T(8,128)(2,1)S(1)}, u32[]{:S(2)}, u32[]{:S(2)}) async-start(bf16[16,3,32,256]{3,2,1,0:T(8,128)(2,1)} %broadcast_select_fusion.1), calls=%async_computation.1 | async-start | bytes 1572864 | tf_op jit(solution)/shard_map/all_to_all | solution.py:100
  116.4 15.9 %convolution_add_fusion = f32[16,32,256]{2,1,0:T(8,128)S(1)} fusion(f32[16,32,256]{2,1,0:T(8,128)} %fusion.30, bf16[16,32,256]{2,1,0:T(8,128)(2,1)S(1)} %copy-done.4, bf16[16,64,32,32]{3,2,1,0:T(8,128)(2,1)} %copy.53, f32[16,64,32]{2,1,0:T(8,128)} %bitcast.179, f32[16,32]{1,0:T(8,128)S(1)} %get-tuple-element.135, f32[16,64,32]{2,1,0:T(8,128)} %bitcast.180, ...), kind=kOutput, calls=%fused_computation.64 | convolution fusion | flops 89292800 | bytes 3809280 | tf_op jit(solution)/shard_map/crv,crb->cvb/dot_general | solution.py:63
  132.4 2.5 all-to-all-done.1
  134.8 34.4 %while.12 = (s32[]{:T(128)}, f32[16,32,256]{2,1,0:T(8,128)S(1)}, bf16[2,24,32,256]{3,2,1,0:T(8,128)(2,1)}, s32[2,24]{1,0:T(2,128)S(1)}, bf16[2,24,32,256]{3,2,1,...) while((s32[]{:T(128)}, f32[16,32,256]{2,1,0:T(8,128)S(1)}, ...), condition=%wide.region_2.3_spmd, body=%wide.region_0.0_spmd.sunk | while | flops 243064096 | bytes 6149745 | solution.py:103
  136.3 6.8 %fusion.76 = bf16[2,24,32,256]{3,2,1,0:T(8,128)(2,1)} fusion(bf16[2,24,32,256]{3,2,1,0:T(8,128)(2,1)} %get-tuple-element.233, s32[]{:T(128)} %get-tuple-element.231, f32[24,256]{1,0:T(8,128)S(1)} %bitcast.172, f32[24,256]{1,0:T(8,128)S(1)} %get-tuple-element.215, f32[24,256]{1,0:T(8,128)S(1)} %bitcast.174, f32[24,256]{1,0:T(8,128)S(1)} %get-tuple-element.217, ...), kind=kOutput, calls=%fused_computation.14.clone.1 | convolution fusion | flops 121700352 | bytes 934448 | tf_op jit(solution)/shard_map/while/body/eval_jaxpr/gva,gba->gvb/dot_general | solution.py:87
  143.1 6.7 %fusion.75 = f32[24,32,256]{2,1,0:T(8,128)S(1)} fusion(f32[24,256]{1,0:T(8,128)S(1)} %bitcast.173, f32[24,256]{1,0:T(8,128)S(1)} %get-tuple-element.215, f32[24,256]{1,0:T(8,128)S(1)} %bitcast.175, f32[24,256]{1,0:T(8,128)S(1)} %get-tuple-element.217, f32[24,256]{1,0:T(8,128)S(1)} %bitcast.177, f32[24,256]{1,0:T(8,128)S(1)} %get-tuple-element.219, ...), kind=kOutput, calls=%fused_computation.10.clone.1 | convolution fusion | flops 121110528 | bytes 1327108 | tf_op jit(solution)/shard_map/while/body/eval_jaxpr/gvb,gba->gva/dot_general | solution.py:79
  149.9 2.1 scatter_fusion
  153.5 6.8 %fusion.76 = bf16[2,24,32,256]{3,2,1,0:T(8,128)(2,1)} fusion(bf16[2,24,32,256]{3,2,1,0:T(8,128)(2,1)} %get-tuple-element.233, s32[]{:T(128)} %get-tuple-element.231, f32[24,256]{1,0:T(8,128)S(1)} %bitcast.172, f32[24,256]{1,0:T(8,128)S(1)} %get-tuple-element.215, f32[24,256]{1,0:T(8,128)S(1)} %bitcast.174, f32[24,256]{1,0:T(8,128)S(1)} %get-tuple-element.217, ...), kind=kOutput, calls=%fused_computation.14.clone.1 | convolution fusion | flops 121700352 | bytes 934448 | tf_op jit(solution)/shard_map/while/body/eval_jaxpr/gva,gba->gvb/dot_general | solution.py:87
  160.3 6.7 %fusion.75 = f32[24,32,256]{2,1,0:T(8,128)S(1)} fusion(f32[24,256]{1,0:T(8,128)S(1)} %bitcast.173, f32[24,256]{1,0:T(8,128)S(1)} %get-tuple-element.215, f32[24,256]{1,0:T(8,128)S(1)} %bitcast.175, f32[24,256]{1,0:T(8,128)S(1)} %get-tuple-element.217, f32[24,256]{1,0:T(8,128)S(1)} %bitcast.177, f32[24,256]{1,0:T(8,128)S(1)} %get-tuple-element.219, ...), kind=kOutput, calls=%fused_computation.10.clone.1 | convolution fusion | flops 121110528 | bytes 1327108 | tf_op jit(solution)/shard_map/while/body/eval_jaxpr/gvb,gba->gva/dot_general | solution.py:79
  167.1 2.1 scatter_fusion
  169.2 5.6 %all-to-all-start.3 = ((bf16[16,3,32,256]{3,2,1,0:T(8,128)(2,1)}), bf16[16,3,32,256]{3,2,1,0:T(8,128)(2,1)}, u32[]{:S(2)}, u32[]{:S(2)}) async-start(bf16[16,3,32,256]{3,2,1,0:T(8,128)(2,1)} %bitcast.171), calls=%async_computation.3 | async-start | bytes 1572864 | tf_op jit(solution)/shard_map/all_to_all | solution.py:114
  176.2 17.4 %all-to-all-done.3 = bf16[16,3,32,256]{3,2,1,0:T(8,128)(2,1)} async-done(((bf16[16,3,32,256]{3,2,1,0:T(8,128)(2,1)}), bf16[16,3,32,256]{3,2,1,0:T(8,128)(2,1)}, u32[]{:S(2)}, u32[]{:S(2)}) %all-to-all-start.3) | async-done | bytes 786464 | tf_op jit(solution)/shard_map/all_to_all | solution.py:114
  194.9 2.9 scatter_fusion.1
  198.4 61.5 %psum.14 = f32[32,32]{0,1:T(8,128)S(1)} all-reduce(f32[32,32]{0,1:T(8,128)S(1)} %convolution_bitcast_fusion.5), channel_id=1, replica_groups=mesh['group'=2,'clus'=16] {'clus'}, use_global_device_ids=true, to_apply=%region_4.5 | all-reduce | flops 1024 | bytes 8192 | tf_op jit(solution)/shard_map/psum | solution.py:124
  260.0 1.6 fusion.32
  262.2 57.6 %psum.15 = f32[32,32]{0,1:T(8,128)S(1)} all-reduce(f32[32,32]{0,1:T(8,128)S(1)} %convolution_bitcast_fusion.4), channel_id=1, replica_groups=mesh['group'=2,'clus'=16] {'clus'}, use_global_device_ids=true, to_apply=%region_5.6 | all-reduce | flops 1024 | bytes 8192 | tf_op jit(solution)/shard_map/psum | solution.py:127
  319.9 2.9 cholesky.17
  324.1 2.4 custom-call.6
  (98 shorter events, 23.8 us)
Async XLA Ops:
  0.6 174.2 %copy-start = (f32[16,32,256]{2,1,0:T(8,128)S(1)}, f32[16,32,256]{2,1,0:T(8,128)}, u32[]{:S(2)}) copy-start(f32[16,32,256]{2,1,0:T(8,128)} %param.12) | copy-start | bytes 1572868
  2.1 95.7 %all-to-all-start = ((s32[16,1,3]{2,1,0:T(1,128)}), s32[16,1,3]{2,1,0:T(1,128)S(1)}, u32[]{:S(2)}, u32[]{:S(2)}) async-start(s32[16,1,3]{2,1,0:T(1,128)} %copy.56), calls=%async_computation | async-start | bytes 16384 | tf_op jit(solution)/shard_map/all_to_all | solution.py:92
  62.3 9.0 %copy-start.3 = (bf16[256,3,32]{2,0,1:T(8,128)(2,1)S(1)}, bf16[256,3,32]{2,0,1:T(8,128)(2,1)}, u32[]{:S(2)}) copy-start(bf16[256,3,32]{2,0,1:T(8,128)(2,1)} %all_gather.6) | copy-start | bytes 147460
  75.0 8.3 %copy-start.6 = (f32[16,256]{1,0:T(8,128)S(1)}, f32[16,256]{1,0:T(8,128)}, u32[]{:S(2)}) copy-start(f32[16,256]{1,0:T(8,128)} %get-tuple-element.131) | copy-start | bytes 49156
  75.0 8.3 %copy-start.7 = (f32[16,256]{1,0:T(8,128)S(1)}, f32[16,256]{1,0:T(8,128)}, u32[]{:S(2)}) copy-start(f32[16,256]{1,0:T(8,128)} %get-tuple-element.132) | copy-start | bytes 49156
  75.0 8.3 %copy-start.8 = (f32[16,256]{1,0:T(8,128)S(1)}, f32[16,256]{1,0:T(8,128)}, u32[]{:S(2)}) copy-start(f32[16,256]{1,0:T(8,128)} %get-tuple-element.133) | copy-start | bytes 49156
  83.3 4.4 %copy-start.1 = (bf16[16,3,256]{2,0,1:T(8,128)(2,1)S(1)}, bf16[16,3,256]{2,0,1:T(8,128)(2,1)}, u32[]{:S(2)}) copy-start(bf16[16,3,256]{2,0,1:T(8,128)(2,1)} %param.14) | copy-start | bytes 73732
  97.8 18.5 %copy-start.4 = (bf16[16,32,256]{2,1,0:T(8,128)(2,1)S(1)}, bf16[16,32,256]{2,1,0:T(8,128)(2,1)}, u32[]{:S(2)}) copy-start(bf16[16,32,256]{2,1,0:T(8,128)(2,1)} %param.15) | copy-start | bytes 786436
  97.8 18.5 %copy-start.9 = (f32[16,32]{1,0:T(8,128)S(1)}, f32[16,32]{1,0:T(8,128)}, u32[]{:S(2)}) copy-start(f32[16,32]{1,0:T(8,128)} %param.16) | copy-start | bytes 6148
  101.7 10.9 %all-to-all-start.2 = ((bf16[16,3,3,256]{3,1,2,0:T(4,128)(2,1)}), bf16[16,3,3,256]{3,1,2,0:T(4,128)(2,1)S(1)}, u32[]{:S(2)}, u32[]{:S(2)}) async-start(bf16[16,3,3,256]{3,1,2,0:T(4,128)(2,1)} %copy.60), calls=%async_computation.2 | async-start | bytes 196608 | tf_op jit(solution)/shard_map/all_to_all | solution.py:101
  112.5 22.3 %all-to-all-start.1 = ((bf16[16,3,32,256]{3,2,1,0:T(8,128)(2,1)}), bf16[16,3,32,256]{3,2,1,0:T(8,128)(2,1)S(1)}, u32[]{:S(2)}, u32[]{:S(2)}) async-start(bf16[16,3,32,256]{3,2,1,0:T(8,128)(2,1)} %broadcast_select_fusion.1), calls=%async_computation.1 | async-start | bytes 1572864 | tf_op jit(solution)/shard_map/all_to_all | solution.py:100
  134.8 40.0 %copy-start.5 = (f32[32,32]{1,0:T(8,128)S(1)}, f32[32,32]{1,0:T(8,128)}, u32[]{:S(2)}) copy-start(f32[32,32]{1,0:T(8,128)} %param.13) | copy-start | bytes 12292
  169.2 28.6 %copy-start.2 = (f32[16,32,256]{2,1,0:T(8,128)S(1)}, f32[16,32,256]{2,1,0:T(8,128)}, u32[]{:S(2)}) copy-start(f32[16,32,256]{2,1,0:T(8,128)} %param.11) | copy-start | bytes 1572868
  169.2 24.4 %all-to-all-start.3 = ((bf16[16,3,32,256]{3,2,1,0:T(8,128)(2,1)}), bf16[16,3,32,256]{3,2,1,0:T(8,128)(2,1)}, u32[]{:S(2)}, u32[]{:S(2)}) async-start(bf16[16,3,32,256]{3,2,1,0:T(8,128)(2,1)} %bitcast.171), calls=%async_computation.3 | async-start | bytes 1572864 | tf_op jit(solution)/shard_map/all_to_all | solution.py:114
where the time goes:
time: 331 us; the launch traced here: 330 us
  blocking collectives  162 us (49%)
  matrix products  54.2 us (16%)
  local copies, waits for them, and re-layouts  39.2 us (12%)
  other arithmetic  26.6 us (8%)
  waiting for transfers between devices  26.1 us (8%)
  starting transfers between devices  20.3 us (6%)
    psum x1, blocking collectives, local(): lax.psum(inner_products(block_vectors, applied), 'clus') / total_points  61.5 us
    psum x1, blocking collectives, local(): lax.psum(inner_products(residual, residual), 'clus') / total_points  57.6 us
    all_gather x1, blocking collectives, local(): lax.all_gather(skeleton, 'clus', axis=0, tiled=True)  23.9 us
    all_gather x1, blocking collectives, local(): lax.all_gather(sources, 'clus', axis=0, tiled=True)  18.9 us
    all_to_all x1, waiting for transfers between devices, local(): lax.all_to_all(mirrors.reshape(served.shape + (vec_count, cluster_size)),...  17.4 us
    dot_general x1, matrix products, local(): jnp.einsum('crv,crb->cvb', lifted, basis, preferred_element_type=jnp.floa...  15.9 us
    dot_general x2, matrix products, paired_turn(): jnp.einsum('gva,gba->gvb', own_vectors, kernel_tiles, preferred_element_t...  13.6 us
    dot_general x2, matrix products, direct_part(): jnp.einsum('gvb,gba->gva', partner_vectors, kernel_tiles, preferred_eleme...  13.5 us
  transfers between devices with their start and end apart: 4, of which 3 were waited for; matrix products, arithmetic and copies ran while one was open for 19% of the time, Pallas kernels for 0%

commit v1 on v0

v1 whole, which is shorter than its diff:
```python
import functools
import math

import jax
import jax.numpy as jnp
from jax import lax
from jax.experimental import pallas as pl
from jax.experimental.pallas import tpu as pltpu
from jax.sharding import PartitionSpec as P

root_three = 1.7320508075688772
length_scale = 0.15
steepness = root_three / length_scale
feature_count = 16
vmem_limit = 56 * 1024 * 1024
NT = (((1,), (1,)), ((), ()))


def kernel_values(squared):
    squared = jnp.maximum(squared, 1e-12)
    distance = squared * lax.rsqrt(squared)
    decay = jnp.exp2(distance * (-steepness * math.log2(math.e)))
    return (1.0 + distance * steepness) * decay


def dot_nt(left, right):
    return lax.dot_general(left, right, NT, preferred_element_type=jnp.float32)


def dot_exact(left, right, dims=(((1,), (0,)), ((), ()))):
    return lax.dot_general(
        left, right, dims, precision=lax.Precision.HIGHEST, preferred_element_type=jnp.float32
    )


def squared_distances(left_features, right_features):
    return jnp.dot(left_features, right_features, preferred_element_type=jnp.float32)


def tile_of(left_features, right_features):
    return kernel_values(squared_distances(left_features, right_features)).astype(jnp.bfloat16)


def features_of(coordinates):
    wide = coordinates.astype(jnp.float32)
    norm = jnp.sum(wide * wide, axis=-2, keepdims=True)
    high = lax.reduce_precision(norm, 8, 7)
    middle = lax.reduce_precision(norm - high, 8, 7)
    low = lax.reduce_precision(norm - high - middle, 8, 7)
    pieces = jnp.concatenate([high, middle, low], axis=-2)
    ones = jnp.ones_like(pieces)
    blank = jnp.zeros(norm.shape[:-2] + (feature_count - 9, norm.shape[-1]), jnp.float32)
    left = jnp.concatenate([wide, pieces, ones, blank], axis=-2).astype(jnp.bfloat16)
    right = jnp.concatenate([-2.0 * wide, ones, pieces, blank], axis=-2).astype(jnp.bfloat16)
    return left, right


def sources_kernel(half_ref, basis_ref, scales_ref, out_ref):
    clusters, rank, _ = basis_ref.shape
    per_row = out_ref.shape[2] // rank
    for cluster in range(clusters):
        projected = dot_nt(half_ref[cluster], basis_ref[cluster])
        scaled = projected * scales_ref[cluster : cluster + 1, :]
        first = (cluster % per_row) * rank
        out_ref[cluster // per_row, :, first : first + rank] = scaled.astype(jnp.bfloat16)


def local_kernel(
    half_ref, left_ref, right_ref, basis_ref, scales_ref, skel_left_ref, skel_right_ref,
    counts_ref, sources_ref, out_ref, gathered_ref
):
    clusters, vecs, size = half_ref.shape
    rank = basis_ref.shape[1]
    parts = sources_ref.shape[0]
    halves = gathered_ref.shape[0]
    per_half = clusters // halves

    def self_step(cluster, carry):
        tile = tile_of(left_ref[cluster], right_ref[cluster])
        out_ref[cluster] = dot_nt(half_ref[cluster], tile)
        return carry

    lax.fori_loop(0, clusters, self_step, 0)
    gathered_ref[...] = jnp.zeros_like(gathered_ref)

    def far_step(part, carry):
        part_features = skel_right_ref[part]
        part_sources = sources_ref[part]
        for side in range(halves):
            values = kernel_values(
                squared_distances(skel_left_ref[side], part_features)
            )
            weights = counts_ref[part, pl.ds(side * per_half, per_half), :]
            values = values.astype(jnp.bfloat16).astype(jnp.float32)
            values = values.reshape(per_half, rank, size) * weights[:, None, :]
            values = values.reshape(per_half * rank, size).astype(jnp.bfloat16)
            gathered_ref[side] += dot_nt(part_sources, values)
        return carry

    lax.fori_loop(0, parts, far_step, 0)
    for cluster in range(clusters):
        side, first = cluster // per_half, (cluster % per_half) * rank
        block = gathered_ref[side][:, first : first + rank]
        lifted = (block * scales_ref[cluster : cluster + 1, :]).astype(jnp.bfloat16)
        out_ref[cluster] += jnp.dot(
            lifted, basis_ref[cluster], preferred_element_type=jnp.float32
        )


def near_kernel(
    live_ref, source_ref, own_ref, mirror_ref, vectors_ref, right_ref, left_ref, local_ref,
    block_ref, prior_ref, beta_ref, stacked_ref, products_ref, total_ref
):
    clusters, vecs, size = local_ref.shape
    total_ref[:clusters] = local_ref[...]

    def entry(place):
        source = source_ref[place]
        own = own_ref[place]
        tile = tile_of(left_ref[own], right_ref[source])
        term = dot_nt(vectors_ref[source], tile)
        rounded = term.astype(jnp.bfloat16).astype(jnp.float32)
        return own, jnp.where(mirror_ref[place] > 0, rounded, term)

    def step(turn, carry):
        first_own, first_term = entry(2 * turn)
        second_own, second_term = entry(2 * turn + 1)
        total_ref[first_own] += first_term
        total_ref[second_own] += second_term
        return carry

    lax.fori_loop(0, lax.div(live_ref[0] + 1, 2), step, 0)
    beta = beta_ref[...]
    sums = jnp.zeros((2 * vecs, 3 * vecs), jnp.float32)
    for cluster in range(clusters):
        block = block_ref[cluster]
        applied = total_ref[cluster]
        shifted = applied - dot_exact(beta, prior_ref[cluster])
        stacked_ref[cluster, :vecs] = shifted
        stacked_ref[cluster, vecs:] = block
        sums += dot_exact(
            jnp.concatenate([block, shifted], axis=0),
            jnp.concatenate([applied, shifted, block], axis=0),
            NT,
        )
    products = jnp.concatenate(
        [sums[:vecs, : 2 * vecs], sums[vecs:, vecs : 2 * vecs], sums[:vecs, 2 * vecs :]], axis=1
    )
    for part in range(products_ref.shape[0]):
        products_ref[part] = products


def finish_kernel(point_count, products_ref, stacked_ref, next_ref, alpha_ref, beta_ref):
    clusters, vecs, size = next_ref.shape
    sums = products_ref[0]
    for part in range(1, products_ref.shape[0]):
        sums = sums + products_ref[part]
    sums = sums * (1.0 / point_count)
    alpha = sums[:, :vecs]
    crossed = sums[:, vecs : 2 * vecs]
    shifted = sums[:, 2 * vecs : 3 * vecs]
    block = sums[:, 3 * vecs :]
    alpha_ref[...] = alpha
    turned = alpha.T
    half_crossed = dot_exact(turned, crossed)
    gram = shifted - half_crossed - half_crossed.T
    gram = gram + dot_exact(turned, dot_exact(block, alpha))
    rows = lax.broadcasted_iota(jnp.int32, (vecs, vecs), 0)
    columns = lax.broadcasted_iota(jnp.int32, (vecs, vecs), 1)
    unit = (rows == columns).astype(jnp.float32)
    work = jnp.concatenate([gram, unit], axis=1)
    row_ids = lax.broadcasted_iota(jnp.int32, (vecs, 1), 0)
    for step in range(vecs - 1):
        pivot_row = work[step : step + 1, :]
        ratio = work[:, step : step + 1] * (1.0 / pivot_row[:, step : step + 1])
        work = work - jnp.where(row_ids > step, ratio, 0.0) * pivot_row
    pivots = jnp.sum(work[:, :vecs] * unit, axis=1, keepdims=True)
    work = work * (1.0 / jnp.sqrt(pivots))
    beta_ref[...] = jnp.where(columns >= rows, work[:, :vecs], 0.0)
    inverse = work[:, vecs:]
    joint = jnp.concatenate([inverse, -dot_exact(inverse, turned)], axis=1)
    for cluster in range(clusters):
        next_ref[cluster] = dot_exact(joint, stacked_ref[cluster])


def call(kernel, out_shape, operands, scratch=(), smem=0, flops=0):
    places = [pltpu.SMEM] * smem + [pltpu.VMEM] * (len(operands) - smem)
    return pl.pallas_call(
        kernel,
        out_shape=out_shape,
        in_specs=[pl.BlockSpec(memory_space=place) for place in places],
        out_specs=jax.tree.map(lambda _: pl.BlockSpec(memory_space=pltpu.VMEM), out_shape),
        scratch_shapes=list(scratch),
        compiler_params=pltpu.CompilerParams(vmem_limit_bytes=vmem_limit),
        cost_estimate=pl.CostEstimate(flops=flops, bytes_accessed=1 << 20, transcendentals=flops // 64),
    )(*operands)


def local(
    block_vectors, prior_vectors, prior_beta, points, basis, scales, skeleton, near_pairs, far_ids
):
    clusters, vecs, size = block_vectors.shape
    rank = basis.shape[1]
    parts = lax.axis_size("clus")
    me = lax.axis_index("clus")
    slots = near_pairs.shape[2]
    total_points = parts * clusters * size
    per_part = 2 * slots
    per_row = size // rank
    halves = clusters // per_row
    wide = functools.partial(jax.ShapeDtypeStruct, dtype=jnp.float32)
    narrow = functools.partial(jax.ShapeDtypeStruct, dtype=jnp.bfloat16)

    half_vectors = block_vectors.astype(jnp.bfloat16)
    all_vectors = lax.all_gather(
        half_vectors.reshape(clusters * vecs, size), "clus", axis=0, tiled=True
    ).reshape(parts * clusters, vecs, size)

    sources = call(
        sources_kernel, narrow((halves, vecs, size)), (half_vectors, basis, scales)
    )
    id_count = parts * per_part
    id_rows = -(-id_count // size)
    ids = jnp.pad(
        near_pairs.reshape(-1).astype(jnp.bfloat16), (0, id_rows * size - id_count)
    ).reshape(id_rows, size)
    skeleton_rows = skeleton.transpose(1, 0, 2).reshape(3 * halves, size)
    pieces = [
        sources.reshape(halves * vecs, size),
        points.reshape(clusters * 3, size),
        skeleton_rows,
        ids,
    ]
    starts = [0]
    for piece in pieces:
        starts.append(starts[-1] + piece.shape[0])
    padding = -starts[-1] % 8
    side = jnp.concatenate(pieces + [jnp.zeros((padding, size), jnp.bfloat16)], axis=0)
    sides = lax.all_gather(side, "clus", axis=0, tiled=False)
    all_sources, all_points, all_skeletons, all_ids = (
        sides[:, starts[k] : starts[k + 1]] for k in range(4)
    )
    all_sources = all_sources.reshape(parts * halves, vecs, size)
    all_points = all_points.reshape(parts * clusters, 3, size)
    all_skeletons = all_skeletons.reshape(parts, 3, halves, size).swapaxes(1, 2)
    all_skeletons = all_skeletons.reshape(parts * halves, 3, size)

    _, far_right = features_of(all_skeletons)
    own_skeleton = skeleton_rows.reshape(3, halves, size).swapaxes(0, 1)
    far_left = features_of(own_skeleton)[0].swapaxes(1, 2)
    own_left, own_right = features_of(points)
    own_left = own_left.swapaxes(1, 2)
    _, all_right = features_of(all_points)

    listed = far_ids[:, :, None] == jnp.arange(parts * clusters, dtype=jnp.int32)
    counts = jnp.sum(listed, axis=1).astype(jnp.float32)
    counts = jnp.repeat(counts, rank, axis=1)
    counts = counts.reshape(clusters, parts * halves, size).swapaxes(0, 1)
    local_part = call(
        local_kernel,
        wide((clusters, vecs, size)),
        (
            half_vectors, own_left, own_right, basis, scales, far_left, far_right,
            counts, all_sources,
        ),
        scratch=[pltpu.VMEM((halves, vecs, size), jnp.float32)],
        flops=1 << 32,
    )

    pairs = all_ids.reshape(parts, -1)[:, :id_count].astype(jnp.int32)
    pairs = pairs.reshape(parts, parts, slots, 2)
    peers = jnp.arange(parts, dtype=jnp.int32)[:, None] * clusters
    asked = near_pairs[0]
    told = lax.dynamic_index_in_dim(pairs, me, axis=1, keepdims=False)
    live = jnp.concatenate([asked[..., 0] >= 0, told[..., 0] >= 0], axis=0).reshape(-1)
    origin = jnp.concatenate([peers + asked[..., 1], peers + told[..., 0]], axis=0).reshape(-1)
    target = jnp.concatenate([asked[..., 0], told[..., 1]], axis=0).reshape(-1)
    mirror = jnp.concatenate([jnp.zeros_like(asked[..., 0]), jnp.ones_like(told[..., 0])], axis=0)
    place = jnp.where(live, jnp.cumsum(live.astype(jnp.int32)) - 1, id_count + 1)
    packed = jnp.stack([origin, target, mirror.reshape(-1)])
    chosen = place[None, :] == jnp.arange(id_count + 1, dtype=jnp.int32)[:, None]
    table = jnp.sum(jnp.where(chosen[None], packed[:, None, :], 0), axis=2)
    spare = jnp.logical_not(jnp.any(chosen, axis=1))
    live_count = jnp.sum(live.astype(jnp.int32)).reshape(1)
    stacked, products = call(
        near_kernel,
        (wide((clusters, 2 * vecs, size)), wide((parts, vecs, 4 * vecs))),
        (
            live_count, table[0], jnp.where(spare, clusters, table[1]), table[2],
            all_vectors, all_right,
            jnp.concatenate([own_left, own_left[:1]], axis=0), local_part,
            block_vectors, prior_vectors, prior_beta,
        ),
        scratch=[pltpu.VMEM((clusters + 1, vecs, size), jnp.float32)],
        smem=4,
        flops=1 << 31,
    )
    summed = lax.all_to_all(products, "clus", split_axis=0, concat_axis=0, tiled=True)
    return call(
        functools.partial(finish_kernel, total_points),
        (wide((clusters, vecs, size)), wide((vecs, vecs)), wide((vecs, vecs))),
        (summed, stacked),
    )


def solution(mesh):
    placed = (
        P(("group", "clus"), None, None),
        P(("group", "clus"), None, None),
        P("group", None),
        P(("group", "clus"), None, None),
        P(("group", "clus"), None, None),
        P(("group", "clus"), None),
        P(("group", "clus"), None, None),
        P(("group", "clus"), None, None, None),
        P(("group", "clus"), None),
    )
    return jax.shard_map(
        local,
        mesh=mesh,
        in_specs=placed,
        out_specs=(P(("group", "clus"), None, None), P("group", None), P("group", None)),
        check_vma=False,
    )
```

time: 331 us -> 179 us (0.54)
  blocking collectives: 162 us -> 41.9 us
  matrix products: 54.2 us -> 0 us
  Pallas kernels: 0 us -> 53.6 us
  waiting for transfers between devices: 26.1 us -> 0.02 us
  starting transfers between devices: 20.3 us -> 0.04 us
  between operations: 0.97 us -> 14.5 us
  other arithmetic: 26.6 us -> 14.8 us
  local copies, waits for them, and re-layouts: 39.2 us -> 51 us
    psum x2 -> x0, blocking collectives: 119 us -> none  [the longest x1 61.5 us: local(): lax.psum(inner_products(block_vectors, applied), 'clus') / total_points]
    dot_general x12 -> x0, matrix products: 54 us -> none  [the longest x1 15.9 us: local(): jnp.einsum('crv,crb->cvb', lifted, basis, preferred_element_type=jnp.floa...]
    pallas_call x0 -> x4, Pallas kernels: none -> 53.6 us  [call(): pl.pallas_call(kernel, out_shape=out_shape, in_specs=[pl.BlockSpec(memory...]
    all_to_all x4 -> x0, waiting for transfers between devices: 26.1 us -> none  [the longest x1 17.4 us: local(): lax.all_to_all(mirrors.reshape(served.shape + (vec_count, cluster_size)),...]
    gather x11 -> x0, local copies, waits for them, and re-layouts: 20.5 us -> none  [the longest x3 13 us: local(): jnp.take(all_sources, far_flat, axis=0)]
    all_to_all x4 -> x0, starting transfers between devices: 20.3 us -> none  [the longest x1 7.39 us: local(): lax.all_to_all(pair_partners, 'clus', split_axis=0, concat_axis=0, tiled=...]
    concatenate x0 -> x9, local copies, waits for them, and re-layouts: none -> 20.2 us  [the longest x3 11.4 us: features_of(): jnp.concatenate([-2.0 * wide, ones, pieces, blank], axis=-2)]
    all_gather x2 -> x1, blocking collectives: 42.7 us -> 27.7 us  [local(): sides = lax.all_gather(side, 'clus', axis=0, tiled=False)]
  transfers between devices with their start and end apart: 4 -> 1, of which waited for: 3 -> 0; matrix products, arithmetic and copies ran while one was open for 19% -> 36% of each run, Pallas kernels for 0% -> 14%
where the time goes in v1:
time: 179 us; the launch traced here: 176 us
  Pallas kernels  53.6 us (30%)
  local copies, waits for them, and re-layouts  51 us (28%)
  blocking collectives  41.9 us (23%)
  other arithmetic  14.8 us (8%)
  between operations  14.5 us (8%)
    pallas_call x4, Pallas kernels, call(): pl.pallas_call(kernel, out_shape=out_shape, in_specs=[pl.BlockSpec(memory...  53.6 us
    all_gather x1, blocking collectives, local(): sides = lax.all_gather(side, 'clus', axis=0, tiled=False)  27.7 us
    all_to_all x1, blocking collectives, local(): lax.all_to_all(products, 'clus', split_axis=0, concat_axis=0, tiled=True)  14.2 us
    concatenate x3, local copies, waits for them, and re-layouts, features_of(): jnp.concatenate([-2.0 * wide, ones, pieces, blank], axis=-2)  11.4 us
    concatenate x2, local copies, waits for them, and re-layouts, features_of(): jnp.concatenate([wide, pieces, ones, blank], axis=-2).astype(jnp.bfloat16)  7.72 us
    another operation x6, other arithmetic  5.88 us
    another operation x2, local copies, waits for them, and re-layouts, local(): counts = counts.reshape(clusters, parts * halves, size).swapaxes(0, 1)  4.89 us
    another operation x5, local copies, waits for them, and re-layouts  4.42 us
  transfers between devices with their start and end apart: 1, of which 0 were waited for; matrix products, arithmetic and copies ran while one was open for 36% of the time, Pallas kernels for 14%

profile of v1, /device:TPU:0, one launch (start us, length us, event | category | flops | bytes accessed | tf_op | source)
XLA Modules:
  0.0 175.8 jit_solution(11345818635901092554)
XLA Ops:
  7.2 1.8 %convert_element_type.67.half_ref = bf16[16,32,256]{2,1,0:T(8,128)(2,1)} convert(f32[16,32,256]{2,1,0:T(8,128)} %block_ref.1) | non-fusion elementwise | flops 131072 | bytes 786432 | tf_op jit(solution)/shard_map/convert_element_type | solution.py:214
  11.6 1.9 %shard_map.112 = bf16[2,32,256]{2,1,0:T(8,128)(2,1)} custom-call(bf16[16,32,256]{2,1,0:T(8,128)(2,1)} %convert_element_type.67.half_ref, bf16[16,32,256]{2,1,0:T(8,128)(2,1)} %basis_ref.3, f32[16,32]{1,0:T(8,128)} %scales_ref.3), custom_call_target="tpu_custom_call" | custom-call | bytes 1048576 | tf_op jit(solution)/shard_map/pallas_call | solution.py:188
  14.3 27.7 %all-gather = bf16[1920,256]{1,0:T(8,128)(2,1)S(1)} all-gather(bf16[120,256]{1,0:T(8,128)(2,1)S(1)} %concatenate.38), channel_id=2, replica_groups=mesh['group'=2,'clus'=16] {'clus'}, dimensions={0}, use_global_device_ids=true | all-gather | bytes 1044480 | tf_op jit(solution)/shard_map/all_gather | solution.py:239
  42.0 1.5 copy.163
  43.7 0.9 slice.63
  49.6 2.0 %copy.160 = f32[16,1,256]{1,2,0:T(8,128)} copy(f32[16,1,256]{2,0,1:T(8,128)S(1)} %bitcast_reduce-precision_fusion.1) | data formatting | bytes 32768 | tf_op jit(solution)/shard_map/reduce_precision | solution.py:47
  51.6 2.0 %copy.161 = f32[16,1,256]{1,2,0:T(8,128)} copy(f32[16,1,256]{2,0,1:T(8,128)S(1)} %bitcast.65) | data formatting | bytes 32768 | tf_op jit(solution)/shard_map/reduce_sum | solution.py:46
  53.5 3.7 %fusion.1 = (bf16[16,1,256]{1,2,0:T(8,128)(2,1)S(1)}, bf16[16,1,256]{1,2,0:T(8,128)(2,1)S(1)}, bf16[16,1,256]{1,2,0:T(8,128)(2,1)S(1)}) fusion(f32[16,1,256]{1,2,0:T(8,128)} %copy.161, f32[16,1,256]{1,2,0:T(8,128)} %copy.160), kind=kLoop, calls=%fused_computation.3 | loop fusion | flops 28672 | bytes 57344 | tf_op jit(solution)/shard_map/convert.28
  57.6 1.0 copy.167
  58.6 1.0 copy.168
  61.0 0.8 copy.172
  61.8 1.5 copy.171
  63.3 1.4 copy.173
  64.8 0.9 convert_reduce_fusion
  65.7 1.9 %broadcast_in_dim.83 = f32[16,256,32]{2,1,0:T(8,128)} broadcast(f32[16,256]{1,0:T(8,128)S(1)} %convert_element_type.80), dimensions={0,1} | broadcast | bytes 540672 | tf_op jit(solution)/shard_map/broadcast_in_dim | solution.py:257
  67.6 2.8 %reshape_reshape.4 = f32[16,32,256]{2,1,0:T(8,128)} reshape(f32[16,256,32]{2,1,0:T(8,128)} %broadcast_in_dim.83) | data formatting | bytes 1048576 | tf_op jit(solution)/shard_map/reshape;reshape | solution.py:258
  70.4 2.1 %copy.197 = f32[16,32,256]{2,0,1:T(8,128)} copy(f32[16,32,256]{2,1,0:T(8,128)} %reshape_reshape.4) | data formatting | bytes 1048576 | tf_op jit(solution)/shard_map/reshape;reshape | solution.py:258
  72.5 1.2 broadcast_in_dim.77
  73.7 1.2 broadcast_in_dim.78
  74.9 6.8 %concatenate.43 = bf16[16,16,256]{1,2,0:T(8,128)(2,1)} concatenate(bf16[16,3,256]{1,2,0:T(8,128)(2,1)} %copy.163, bf16[16,1,256]{1,2,0:T(8,128)(2,1)S(1)} %get-tuple-element.11, bf16[16,1,256]{1,2,0:T(8,128)(2,1)S(1)} %get-tuple-element.10, bf16[16,1,256]{1,2,0:T(8,128)(2,1)S(1)} %get-tuple-element.9, bf16[16,3,256]{1,2,0:T(8,128)(2,1)} %broadcast_in_dim.77, ...), dimensions={1} | concatenate | bytes 262144 | tf_op jit(solution)/shard_map/concatenate | solution.py:53
  81.7 1.5 slice.61
  83.1 1.1 convert_multiply_fusion
  85.6 1.0 concatenate.46
  86.7 1.6 concatenate.47.skel_right_ref
  88.3 1.4 concatenate.45.right_ref
  89.7 1.3 fusion.4
  91.4 8.4 %concatenate.42.right_ref = bf16[256,16,256]{2,1,0:T(8,128)(2,1)} concatenate(bf16[256,3,256]{2,1,0:T(4,128)(2,1)S(1)} %mul.63, bf16[256,3,256]{2,1,0:T(4,128)(2,1)S(1)} %broadcast_in_dim.75, bf16[256,1,256]{2,1,0:T(2,128)(2,1)} %get-tuple-element.18, bf16[256,1,256]{2,1,0:T(2,128)(2,1)} %get-tuple-element.17, bf16[256,1,256]{2,1,0:T(2,128)(2,1)S(1)} %get-tuple-element.16, ...), dimensions={1} | concatenate | bytes 4194304 | tf_op jit(solution)/shard_map/concatenate | solution.py:54
  100.8 1.3 pad_maximum_fusion.left_ref
  103.1 22.6 %shard_map.113.local_ref = f32[16,32,256]{2,1,0:T(8,128)} custom-call(bf16[16,32,256]{2,1,0:T(8,128)(2,1)} %convert_element_type.67.half_ref, bf16[16,256,16]{2,1,0:T(8,128)(2,1)} %bitcast.51, bf16[16,16,256]{2,1,0:T(8,128)(2,1)} %concatenate.45.right_ref, bf16[16,32,256]{2,1,0:T(8,128)(2,1)} %basis_ref.3, f32[16,32]{1,0:T(8,128)} %scales_ref.3, ...), custom_call_target="tpu_custom_call" | custom-call | flops 4294967296 | bytes 1048576 | tf_op jit(solution)/shard_map/pallas_call | solution.py:188
  125.8 22.9 %shard_map.114 = (f32[16,64,256]{2,1,0:T(8,128)}, f32[16,32,128]{2,1,0:T(8,128)}) custom-call(s32[1]{0:T(128)} %bitcast.6.live_ref, s32[97]{0:T(128)} %get-tuple-element.33.source_ref, s32[97]{0:T(128)} %bitcast_select_fusion.own_ref, s32[97]{0:T(128)} %get-tuple-element.32.mirror_ref, bf16[256,32,256]{2,1,0:T(8,128)(2,1)} %bitcast.74, ...), custom_call_target="tpu_custom_call" | custom-call | flops 2147483648 | bytes 1048576 | tf_op jit(solution)/shard_map/pallas_call | solution.py:188
  148.6 14.2 %all_to_all.5.products_ref = f32[16,32,128]{2,1,0:T(8,128)} all-to-all(f32[16,32,128]{2,1,0:T(8,128)} %get-tuple-element.5), channel_id=1, replica_groups=mesh['group'=2,'clus'=16] {'clus'}, dimensions={0} | all-to-all | bytes 524288 | tf_op jit(solution)/shard_map/all_to_all | solution.py:298
  162.9 6.1 %shard_map.115 = (f32[16,32,256]{2,1,0:T(8,128)}, f32[32,32]{1,0:T(8,128)}, f32[32,32]{1,0:T(8,128)}) custom-call(f32[16,32,128]{2,1,0:T(8,128)} %all_to_all.5.products_ref, f32[16,64,256]{2,1,0:T(8,128)} %get-tuple-element.6.stacked_ref), custom_call_target="tpu_custom_call" | custom-call | bytes 1048576 | tf_op jit(solution)/shard_map/pallas_call | solution.py:188
  (113 shorter events, 13.9 us)
Async XLA Ops:
  7.2 36.4 %copy-start.12 = (bf16[16,3,32]{2,0,1:T(8,128)(2,1)S(1)}, bf16[16,3,32]{2,0,1:T(8,128)(2,1)}, u32[]{:S(2)}) copy-start(bf16[16,3,32]{2,0,1:T(8,128)(2,1)} %param.15) | copy-start | bytes 9220
  7.2 34.9 %copy-start.6 = (bf16[16,3,256]{2,0,1:T(8,128)(2,1)S(1)}, bf16[16,3,256]{2,0,1:T(8,128)(2,1)}, u32[]{:S(2)}) copy-start(bf16[16,3,256]{2,0,1:T(8,128)(2,1)} %param.12) | copy-start | bytes 73732
  7.2 118.6 %all-gather.3.cloned.1.call-start = ((), (), s32[]{:S(2)}) async-start(), calls=%async_computation.1 | async-start | bytes 4456448 | tf_op jit(solution)/shard_map/all_gather | solution.py:215
  11.6 33.1 %copy-start.14 = (s32[1,16,3,2]{1,3,2,0:T(2,128)S(1)}, s32[1,16,3,2]{1,3,2,0:T(2,128)}, u32[]{:S(2)}) copy-start(s32[1,16,3,2]{1,3,2,0:T(2,128)} %param.16) | copy-start | bytes 1156
  42.0 9.6 %copy-start.1 = (bf16[1920,256]{1,0:T(8,128)(2,1)}, bf16[1920,256]{1,0:T(8,128)(2,1)S(1)}, u32[]{:S(2)}) copy-start(bf16[1920,256]{1,0:T(8,128)(2,1)S(1)} %all-gather) | copy-start | bytes 2949124
  44.8 1.7 copy-start.15
  60.4 0.6 copy-start.13
  84.2 1.2 copy-start.2
  84.6 1.0 copy-start.3
  84.6 2.0 %copy-start.9 = (f32[32,1,256]{2,1,0:T(1,128)S(1)}, f32[32,1,256]{2,1,0:T(1,128)}, u32[]{:S(2)}) copy-start(f32[32,1,256]{2,1,0:T(1,128)} %reduce_sum.80) | copy-start | bytes 98308
  84.6 2.1 %copy-start.4 = (bf16[16,2,3,256]{3,2,1,0:T(4,128)(2,1)S(1)}, bf16[16,2,3,256]{3,2,1,0:T(4,128)(2,1)}, u32[]{:S(2)}) copy-start(bf16[16,2,3,256]{3,2,1,0:T(4,128)(2,1)} %copy.175) | copy-start | bytes 147460
  85.3 3.0 %copy-start.8 = (bf16[16,3,256]{2,1,0:T(4,128)(2,1)S(1)}, bf16[16,3,256]{2,1,0:T(4,128)(2,1)}, u32[]{:S(2)}) copy-start(bf16[16,3,256]{2,1,0:T(4,128)(2,1)} %copy.164) | copy-start | bytes 73732
  85.3 3.0 %copy-start.10 = (bf16[16,1,256]{2,1,0:T(2,128)(2,1)S(1)}, bf16[16,1,256]{2,1,0:T(2,128)(2,1)}, u32[]{:S(2)}) copy-start(bf16[16,1,256]{2,1,0:T(2,128)(2,1)} %copy.167) | copy-start | bytes 24580
  85.3 3.0 %copy-start.11 = (bf16[16,1,256]{2,1,0:T(2,128)(2,1)S(1)}, bf16[16,1,256]{2,1,0:T(2,128)(2,1)}, u32[]{:S(2)}) copy-start(bf16[16,1,256]{2,1,0:T(2,128)(2,1)} %copy.168) | copy-start | bytes 24580
  91.3 8.5 %copy-start.17 = (s32[1,96]{1,0:T(1,128)S(1)}, s32[1,96]{1,0:T(1,128)}, u32[]{:S(2)}) copy-start(s32[1,96]{1,0:T(1,128)} %stack_reshape.6) | copy-start | bytes 1156
  91.3 8.5 %copy-start.18 = (s32[1,96]{1,0:T(1,128)S(1)}, s32[1,96]{1,0:T(1,128)}, u32[]{:S(2)}) copy-start(s32[1,96]{1,0:T(1,128)} %stack_reshape.7) | copy-start | bytes 1156
  91.3 8.5 %copy-start.19 = (s32[1,96]{1,0:T(1,128)S(1)}, s32[1,96]{1,0:T(1,128)}, u32[]{:S(2)}) copy-start(s32[1,96]{1,0:T(1,128)} %constant.17.clone.1) | copy-start | bytes 1156
  91.3 8.5 %copy-start.16 = (pred[32,3]{0,1:T(4,128)(4,1)S(1)}, pred[32,3]{0,1:T(4,128)(4,1)}, u32[]{:S(2)}) copy-start(pred[32,3]{0,1:T(4,128)(4,1)} %copy-done.15) | copy-start | bytes 292
  91.3 9.1 %copy-start.7 = (s32[96,1]{1,0:T(8,128)S(1)}, s32[96,1]{1,0:T(8,128)}, u32[]{:S(2)}) copy-start(s32[96,1]{1,0:T(8,128)} %reduce-window.8) | copy-start | bytes 1156
  91.3 9.2 %copy-start.20 = (pred[96]{0:T(512)(128)(4,1)S(1)}, pred[96]{0:T(512)(128)(4,1)}, u32[]{:S(2)}) copy-start(pred[96]{0:T(512)(128)(4,1)} %reshape.283) | copy-start | bytes 292
  91.3 9.4 %copy-start = (bf16[16,16,256]{1,2,0:T(8,128)(2,1)S(1)}, bf16[16,16,256]{1,2,0:T(8,128)(2,1)}, u32[]{:S(2)}) copy-start(bf16[16,16,256]{1,2,0:T(8,128)(2,1)} %concatenate.43) | copy-start | bytes 393220
  91.4 9.4 %copy-start.5 = (bf16[1,256,16]{2,1,0:T(8,128)(2,1)S(1)}, bf16[1,256,16]{2,1,0:T(8,128)(2,1)}, u32[]{:S(2)}) copy-start(bf16[1,256,16]{2,1,0:T(8,128)(2,1)} %slice.61) | copy-start | bytes 24580
Sparse Core Ops, SparseCore 0:
  10.2 56.5 all-gather.2

commit v2 on v1

v2 whole, which is shorter than its diff:
```python
import functools
import math

import jax
import jax.numpy as jnp
from jax import lax
from jax.experimental import pallas as pl
from jax.experimental.pallas import tpu as pltpu
from jax.sharding import PartitionSpec as P

root_three = 1.7320508075688772
length_scale = 0.15
steepness = root_three / length_scale
feature_count = 16
unroll = 8
NT = (((1,), (1,)), ((), ()))


def kernel_values(squared):
    squared = jnp.maximum(squared, 1e-12)
    distance = squared * lax.rsqrt(squared)
    decay = jnp.exp2(distance * (-steepness * math.log2(math.e)))
    return (1.0 + distance * steepness) * decay


def dot_nt(left, right):
    return lax.dot_general(left, right, NT, preferred_element_type=jnp.float32)


def dot_exact(left, right, dims=(((1,), (0,)), ((), ()))):
    return lax.dot_general(
        left, right, dims, precision=lax.Precision.HIGHEST, preferred_element_type=jnp.float32
    )


def split(values):
    high = values.astype(jnp.bfloat16)
    return high, (values - high.astype(jnp.float32)).astype(jnp.bfloat16)


def dot_split(left, right):
    left_high, left_low = split(left)
    right_high, right_low = split(right)
    return dot_nt(
        jnp.concatenate([left_high, left_high, left_low], axis=1),
        jnp.concatenate([right_high, right_low, right_high], axis=1),
    )


def values_of(left_features, right_features):
    return kernel_values(jnp.dot(left_features, right_features, preferred_element_type=jnp.float32))


def tile_of(left_features, right_features):
    return values_of(left_features, right_features).astype(jnp.bfloat16)


def norm_pieces(axes):
    norm = axes[0] * axes[0] + axes[1] * axes[1] + axes[2] * axes[2]
    high = norm.astype(jnp.bfloat16).astype(jnp.float32)
    rest = norm - high
    middle = rest.astype(jnp.bfloat16).astype(jnp.float32)
    return [high, middle, rest - middle]


def stack_rows(rows):
    rows = rows + [jnp.zeros_like(rows[0])] * (feature_count - len(rows))
    return jnp.transpose(jnp.stack(rows, axis=0), (1, 0, 2))


def left_rows(axes):
    one = jnp.ones_like(axes[0])
    return stack_rows(list(axes) + norm_pieces(axes) + [one, one, one])


def right_rows(axes):
    one = jnp.ones_like(axes[0])
    return stack_rows([-2.0 * axis for axis in axes] + [one, one, one] + norm_pieces(axes))


def layout_of(clusters, vecs, rank, size):
    halves = clusters * rank // size
    rows = {"sources": clusters * vecs}
    rows["points"] = rows["sources"] + halves * vecs
    rows["skeleton"] = rows["points"] + 3 * clusters
    rows["ids"] = -(-(rows["skeleton"] + 3 * halves) // 8) * 8
    rows["end"] = -(-(rows["ids"] + 8) // 16) * 16
    return rows


def prepare_kernel(
    rows, block_ref, basis_ref, scales_ref, points_ref, skeleton_ref, ids_ref, message_ref
):
    clusters, rank, size = basis_ref.shape
    vecs = block_ref.shape[1]
    per_row = size // rank
    halves = clusters // per_row
    for half in range(halves):
        pieces = []
        for place in range(per_row):
            cluster = half * per_row + place
            vectors = block_ref[cluster].astype(jnp.bfloat16)
            message_ref[cluster * vecs : (cluster + 1) * vecs, :] = vectors
            projected = dot_nt(vectors, basis_ref[cluster])
            pieces.append(projected * scales_ref[cluster : cluster + 1, :])
        start = rows["sources"] + half * vecs
        message_ref[start : start + vecs, :] = jnp.concatenate(pieces, axis=1).astype(jnp.bfloat16)
    for axis in range(3):
        start = rows["points"] + axis * clusters
        message_ref[start : start + clusters, :] = points_ref[axis]
    lines = []
    for axis in range(3):
        skeleton = skeleton_ref[axis].astype(jnp.float32)
        for half in range(halves):
            first = half * per_row
            lines.append(
                jnp.concatenate(
                    [skeleton[first + k : first + k + 1, :] for k in range(per_row)], axis=1
                )
            )
    lines.append(jnp.zeros((rows["ids"] - rows["skeleton"] - len(lines), size), jnp.float32))
    ids = jnp.concatenate([ids_ref[0, slot] for slot in range(ids_ref.shape[1])], axis=0)
    ids = ids.astype(jnp.float32)
    lines.append(
        jnp.concatenate([ids, jnp.zeros((ids.shape[0], size - ids.shape[1]), jnp.float32)], axis=1)
    )
    lines.append(jnp.zeros((rows["end"] - rows["ids"] - ids.shape[0], size), jnp.float32))
    message_ref[rows["skeleton"] :, :] = jnp.concatenate(lines, axis=0).astype(jnp.bfloat16)


def axes_of(values, start, count):
    return [values[start + k * count : start + (k + 1) * count] for k in range(3)]


def local_kernel(
    rows, message_ref, far_ref, block_ref, prior_ref, beta_ref,
    total_ref, early_ref, left_ref, far_left_ref, counts_ref
):
    clusters, vecs, size = block_ref.shape
    blocks = counts_ref.shape[0]
    halves = far_left_ref.shape[0]
    per_row = clusters // halves
    tail = message_ref[rows["points"] :, :].astype(jnp.float32)
    axes = axes_of(tail, 0, clusters)
    left = left_rows(axes)
    right = right_rows(axes).astype(jnp.bfloat16)
    for cluster in range(clusters):
        left_ref[cluster] = left[cluster].T.astype(jnp.bfloat16)
    left_ref[clusters] = jnp.zeros_like(left_ref[clusters])
    far_left = left_rows(axes_of(tail, rows["skeleton"] - rows["points"], halves))
    for half in range(halves):
        far_left_ref[half] = far_left[half].T.astype(jnp.bfloat16)

    beta = beta_ref[...]
    sums = jnp.zeros((vecs, 2 * vecs), jnp.float32)
    for cluster in range(clusters):
        tile = tile_of(left_ref[cluster], right[cluster])
        term = dot_nt(message_ref[cluster * vecs : (cluster + 1) * vecs, :], tile)
        shift = dot_exact(beta, prior_ref[cluster])
        total_ref[cluster] = term - shift
        block = block_ref[cluster]
        sums += dot_split(block, jnp.concatenate([block, shift], axis=0))
    total_ref[clusters] = jnp.zeros_like(total_ref[clusters])
    early_ref[...] = sums

    far_ids = far_ref[...]
    lanes = lax.broadcasted_iota(jnp.int32, (clusters, blocks * per_row), 1)
    listed = jnp.zeros(lanes.shape, jnp.float32)
    for place in range(far_ref.shape[1]):
        listed += (far_ids[:, place : place + 1] == lanes).astype(jnp.float32)
    listed = listed.astype(jnp.bfloat16)
    rank = size // per_row
    rows_of = lax.broadcasted_iota(jnp.int32, (per_row, size), 0)
    widen = (lax.div(lax.broadcasted_iota(jnp.int32, (per_row, size), 1), rank) == rows_of)
    widen = widen.astype(jnp.bfloat16)
    for block in range(blocks):
        counts_ref[block] = jnp.dot(
            listed[:, block * per_row : (block + 1) * per_row], widen,
            preferred_element_type=jnp.float32,
        )


def add_kernel(rows, owner_of, pieces, last, asked_ref, *refs):
    total_in, far_in, left_ref, far_left_ref, counts_ref = refs[:5]
    count = sum(pieces)
    messages, refs = refs[5 : 5 + count], refs[5 + count :]
    if last:
        basis_ref, scales_ref, early_ref, block_ref, stacked_ref, products_ref = refs[:6]
        refs = refs[6:]
    else:
        total_out, far_out = refs[:2]
        refs = refs[2:]
    (
        total_ref, far_ref, vectors_ref, sources_ref, right_ref, far_right_ref, ids_ref,
        ids_scalar_ref, source_ref, own_ref, mirror_ref, copied,
    ) = refs
    devices = len(pieces)
    clusters = left_ref.shape[0] - 1
    size = left_ref.shape[1]
    halves, vecs, _ = far_ref.shape
    per_row = clusters // halves
    rank = size // per_row
    slots = asked_ref.shape[1]
    me = lax.axis_index("clus")
    owners = [owner_of(me, device) for device in range(devices)]

    total_ref[...] = total_in[...]
    far_ref[...] = far_in[...]
    start = 0
    for device, number in enumerate(pieces):
        first = 0
        for piece in messages[start : start + number]:
            upto = min(first + piece.shape[0], clusters * vecs)
            for row in range(first, upto, vecs):
                vectors_ref[device * clusters + row // vecs] = piece[row - first : row - first + vecs, :]
            before, first = first, first + piece.shape[0]
        rest = messages[start + number - 1]
        start += number
        offset = rows["sources"] - before
        for half in range(halves):
            sources_ref[device * halves + half] = rest[offset + half * vecs : offset + (half + 1) * vecs, :]
        tail = rest[rows["points"] - before :, :].astype(jnp.float32)
        right = right_rows(axes_of(tail, 0, clusters))
        right_ref[device * clusters : (device + 1) * clusters] = right.astype(jnp.bfloat16)
        right = right_rows(axes_of(tail, rows["skeleton"] - rows["points"], halves))
        far_right_ref[device * halves : (device + 1) * halves] = right.astype(jnp.bfloat16)
        ids = tail[rows["ids"] - rows["points"] : rows["ids"] - rows["points"] + 8]
        ids_ref[device] = ids[:, : ids_ref.shape[2]].astype(jnp.int32)
    copy = pltpu.make_async_copy(ids_ref, ids_scalar_ref, copied)
    copy.start()

    pair = 2 if devices % 2 == 0 else 1

    def far_step(turn, carry):
        terms = []
        for place in range(pair):
            device = turn * pair + place
            owner = owners[0]
            for known in range(1, devices):
                owner = jnp.where(device == known, owners[known], owner)
            for block in range(halves):
                features = far_right_ref[device * halves + block]
                sources = sources_ref[device * halves + block]
                for side in range(halves):
                    tile = values_of(far_left_ref[side], features)
                    weights = counts_ref[owner * halves + block]
                    weights = weights[side * per_row : (side + 1) * per_row]
                    tile = tile.reshape(per_row, rank, size) * weights[:, None, :]
                    tile = tile.reshape(per_row * rank, size).astype(jnp.bfloat16)
                    terms.append((side, dot_nt(sources, tile)))
        for side in range(halves):
            far_ref[side] += functools.reduce(jnp.add, [term for place, term in terms if place == side])
        return carry

    lax.fori_loop(0, devices // pair, far_step, 0)

    copy.wait()
    live = jnp.int32(0)
    for device in range(devices):
        for slot in range(slots):
            asked = asked_ref[0, slot, 0, owners[device]], asked_ref[0, slot, 1, owners[device]]
            told = ids_scalar_ref[device, 2 * slot, me], ids_scalar_ref[device, 2 * slot + 1, me]
            for row, source, own, mirror in (
                (asked[0], asked[1], asked[0], 0), (told[0], told[0], told[1], 1),
            ):
                source_ref[live] = device * clusters + source
                own_ref[live] = own
                mirror_ref[live] = mirror
                live = live + (row >= 0).astype(jnp.int32)
    for extra in range(unroll):
        source_ref[live + extra] = 0
        own_ref[live + extra] = clusters
        mirror_ref[live + extra] = 0

    def entry(place):
        source = source_ref[place]
        own = own_ref[place]
        tile = tile_of(left_ref[own], right_ref[source])
        term = dot_nt(vectors_ref[source], tile)
        rounded = term.astype(jnp.bfloat16).astype(jnp.float32)
        return own, jnp.where(mirror_ref[place] > 0, rounded, term)

    def near_step(turn, carry):
        terms = [entry(unroll * turn + place) for place in range(unroll)]
        for own, term in terms:
            total_ref[own] += term
        return carry

    lax.fori_loop(0, lax.div(live + (unroll - 1), unroll), near_step, 0)
    if not last:
        total_out[...] = total_ref[...]
        far_out[...] = far_ref[...]
        return

    sums = jnp.zeros((2 * vecs, vecs), jnp.float32)
    for cluster in range(clusters):
        side, first = cluster // per_row, (cluster % per_row) * rank
        part = far_ref[side][:, first : first + rank]
        lifted = (part * scales_ref[cluster : cluster + 1, :]).astype(jnp.bfloat16)
        shifted = total_ref[cluster] + jnp.dot(
            lifted, basis_ref[cluster], preferred_element_type=jnp.float32
        )
        stacked = jnp.concatenate([block_ref[cluster], shifted], axis=0)
        stacked_ref[cluster] = stacked
        sums += dot_split(stacked, shifted)
    early = early_ref[...]
    crossed = sums[:vecs]
    products = jnp.concatenate(
        [crossed + early[:, vecs:], crossed, sums[vecs:], early[:, :vecs]], axis=1
    )
    for part in range(products_ref.shape[0]):
        products_ref[part] = products


def finish_kernel(point_count, products_ref, stacked_ref, next_ref, alpha_ref, beta_ref):
    clusters, vecs, size = next_ref.shape
    sums = products_ref[0]
    for part in range(1, products_ref.shape[0]):
        sums = sums + products_ref[part]
    sums = sums * (1.0 / point_count)
    alpha = sums[:, :vecs]
    crossed = sums[:, vecs : 2 * vecs]
    shifted = sums[:, 2 * vecs : 3 * vecs]
    block = sums[:, 3 * vecs :]
    alpha_ref[...] = alpha
    turned = alpha.T
    crossed = dot_exact(turned, crossed - 0.5 * dot_exact(block, alpha))
    gram = shifted - crossed - crossed.T
    rows = lax.broadcasted_iota(jnp.int32, (vecs, vecs), 0)
    columns = lax.broadcasted_iota(jnp.int32, (vecs, vecs), 1)
    unit = (rows == columns).astype(jnp.float32)
    work = jnp.concatenate([gram, unit], axis=1)
    row_ids = lax.broadcasted_iota(jnp.int32, (vecs, 1), 0)
    for step in range(vecs - 1):
        pivot_row = work[step : step + 1, :]
        ratio = work[:, step : step + 1] * (1.0 / pivot_row[:, step : step + 1])
        work = work - jnp.where(row_ids > step, ratio, 0.0) * pivot_row
    pivots = jnp.sum(work[:, :vecs] * unit, axis=1, keepdims=True)
    work = work * (1.0 / jnp.sqrt(pivots))
    beta_ref[...] = jnp.where(columns >= rows, work[:, :vecs], 0.0)
    inverse = work[:, vecs:]
    joint = jnp.concatenate([-dot_exact(inverse, turned), inverse], axis=1)
    for cluster in range(clusters):
        next_ref[cluster] = dot_exact(joint, stacked_ref[cluster])


def call(kernel, out_shape, operands, scratch=(), smem=0, smem_out=0, flops=0, vmem=20 << 20):
    def specs(total, scalars):
        places = [pltpu.SMEM] * scalars + [pltpu.VMEM] * (total - scalars)
        return [pl.BlockSpec(memory_space=place) for place in places]

    return pl.pallas_call(
        kernel,
        out_shape=out_shape,
        in_specs=specs(len(operands), smem),
        out_specs=specs(len(out_shape), smem_out),
        scratch_shapes=list(scratch),
        compiler_params=pltpu.CompilerParams(vmem_limit_bytes=vmem),
        cost_estimate=pl.CostEstimate(
            flops=flops, bytes_accessed=1 << 20, transcendentals=flops // 64
        ),
    )(*operands)


def spread(message, parts):
    def passed(values, step):
        pairs = [(index, index ^ step) for index in range(parts)]
        return lax.ppermute(values, "clus", pairs)

    def group_of(steps, pieces):
        def owner_of(me, place):
            return me ^ steps[place]

        return owner_of, pieces

    if parts != 16:
        everything = lax.all_gather(message, "clus", axis=0, tiled=False)
        count = 8 if parts % 8 == 0 else 1
        yield
        for first in range(0, parts, count):
            yield (
                functools.partial(lambda first, me, place: first + place, first),
                [[everything[first + place]] for place in range(count)],
            )
        return
    core, along, inner, over = 1, 2, 4, 12
    cut = message.shape[0] // 2
    fetched = [passed(message, step) for step in (over, inner, along)]
    sibling = passed(message, core)
    token = yield
    sibling, _ = lax.optimization_barrier((sibling, token))
    token = yield group_of([0, core], [[message], [sibling]])
    fetched, _ = lax.optimization_barrier((fetched, token))
    mirrored, inward, sideways = fetched
    fetched = [
        passed(mirrored, inner), passed(mirrored, along),
        passed(sideways[:cut], inner), passed(inward[cut:], along),
    ]
    token = yield group_of(
        [over, inner, along, over ^ core, inner ^ core, along ^ core],
        [[mirrored], [inward], [sideways]]
        + [[passed(piece, core)] for piece in (mirrored, inward, sideways)],
    )
    fetched, _ = lax.optimization_barrier((fetched, token))
    mirrored_inward, mirrored_sideways, *diagonal = fetched
    fetched = [
        passed(mirrored_sideways[:cut], inner), passed(mirrored_inward[cut:], along),
    ]
    steps = [over ^ inner, over ^ along, inner ^ along]
    pieces = [[mirrored_inward], [mirrored_sideways], diagonal]
    token = yield group_of(
        steps + [step ^ core for step in steps],
        pieces + [[passed(part, core) for part in piece] for piece in pieces],
    )
    fetched, _ = lax.optimization_barrier((fetched, token))
    last = over ^ inner ^ along
    yield group_of([last, last ^ core], [fetched, [passed(part, core) for part in fetched]])


def local(
    block_vectors, prior_vectors, prior_beta, points, basis, scales, skeleton, near_pairs, far_ids
):
    clusters, vecs, size = block_vectors.shape
    rank = basis.shape[1]
    parts = lax.axis_size("clus")
    slots = near_pairs.shape[2]
    total_points = parts * clusters * size
    halves = clusters * rank // size
    rows = layout_of(clusters, vecs, rank, size)
    wide = functools.partial(jax.ShapeDtypeStruct, dtype=jnp.float32)
    narrow = functools.partial(jax.ShapeDtypeStruct, dtype=jnp.bfloat16)

    asked = near_pairs.transpose(0, 2, 3, 1)
    (message,) = call(
        functools.partial(prepare_kernel, rows),
        [narrow((rows["end"], size))],
        (
            block_vectors, basis, scales, points.transpose(1, 0, 2), skeleton.transpose(1, 0, 2),
            asked,
        ),
        vmem=56 << 20,
    )
    groups = spread(message, parts)
    next(groups)
    total, early, left, far_left, counts = call(
        functools.partial(local_kernel, rows),
        [
            wide((clusters + 1, vecs, size)),
            wide((vecs, 2 * vecs)),
            narrow((clusters + 1, size, feature_count)),
            narrow((halves, size, feature_count)),
            wide((parts * halves, clusters, size)),
        ],
        (message, far_ids, block_vectors, prior_vectors, prior_beta),
        flops=1 << 31,
    )
    far = jnp.zeros((halves, vecs, size), jnp.float32)
    lanes = -(-parts // 128) * 128
    token, seen = early, 0
    while seen < parts:
        owner_of, messages = groups.send(token)
        seen += len(messages)
        last = seen == parts
        devices = len(messages)
        entries = 2 * slots * devices + unroll
        pieces = [piece for message_pieces in messages for piece in message_pieces]
        operands = [asked, total, far, left, far_left, counts] + pieces
        out_shape = [wide((clusters + 1, vecs, size)), wide((halves, vecs, size))]
        if last:
            operands += [basis, scales, early, block_vectors]
            out_shape = [wide((clusters, 2 * vecs, size)), wide((parts, vecs, 4 * vecs))]
        total, far = call(
            functools.partial(
                add_kernel, rows, owner_of, [len(message_pieces) for message_pieces in messages], last
            ),
            out_shape,
            operands,
            scratch=[
                pltpu.VMEM((clusters + 1, vecs, size), jnp.float32),
                pltpu.VMEM((halves, vecs, size), jnp.float32),
                pltpu.VMEM((devices * clusters, vecs, size), jnp.bfloat16),
                pltpu.VMEM((devices * halves, vecs, size), jnp.bfloat16),
                pltpu.VMEM((devices * clusters, feature_count, size), jnp.bfloat16),
                pltpu.VMEM((devices * halves, feature_count, size), jnp.bfloat16),
                pltpu.VMEM((devices, 8, lanes), jnp.int32),
                pltpu.SMEM((devices, 8, lanes), jnp.int32),
                pltpu.SMEM((entries,), jnp.int32),
                pltpu.SMEM((entries,), jnp.int32),
                pltpu.SMEM((entries,), jnp.int32),
                pltpu.SemaphoreType.DMA,
            ],
            smem=1,
            flops=devices << 28,
        )
        token = far
    stacked, products = total, far
    summed = lax.all_to_all(products, "clus", split_axis=0, concat_axis=0, tiled=True)
    return tuple(
        call(
            functools.partial(finish_kernel, total_points),
            [wide((clusters, vecs, size)), wide((vecs, vecs)), wide((vecs, vecs))],
            (summed, stacked),
        )
    )


def solution(mesh):
    placed = (
        P(("group", "clus"), None, None),
        P(("group", "clus"), None, None),
        P("group", None),
        P(("group", "clus"), None, None),
        P(("group", "clus"), None, None),
        P(("group", "clus"), None),
        P(("group", "clus"), None, None),
        P(("group", "clus"), None, None, None),
        P(("group", "clus"), None),
    )
    return jax.shard_map(
        local,
        mesh=mesh,
        in_specs=placed,
        out_specs=(P(("group", "clus"), None, None), P("group", None), P("group", None)),
        check_vma=False,
    )
```

time: 179 us -> 79.4 us (0.44); the launches traced: 176 us -> 79.2 us
  local copies, waits for them, and re-layouts: 51 us -> 1.08 us
  blocking collectives: 41.9 us -> 12.6 us
  starting transfers between devices: 0.04 us -> 14.9 us
  other arithmetic: 14.8 us -> 0 us
  Pallas kernels: 53.6 us -> 39.4 us
  between operations: 14.5 us -> 0.87 us
  waiting for transfers between devices: 0.02 us -> 10.3 us
    all_gather x1 -> x0, blocking collectives: 27.7 us -> none  [local(): sides = lax.all_gather(side, 'clus', axis=0, tiled=False)]
    concatenate x9 -> x0, local copies, waits for them, and re-layouts: 20.2 us -> none  [the longest x3 11.4 us: features_of(): jnp.concatenate([-2.0 * wide, ones, pieces, blank], axis=-2)]
    ppermute x0 -> x19, starting transfers between devices: none -> 14.9 us  [passed(): return lax.ppermute(values, 'clus', pairs)]
    pallas_call x4 -> x7, Pallas kernels: 53.6 us -> 39.4 us  [call(): pl.pallas_call(kernel, out_shape=out_shape, in_specs=specs(len(operands),...]
    another operation x9 -> x0, local copies, waits for them, and re-layouts: 10.6 us -> none  [the longest x2 4.89 us: local(): counts = counts.reshape(clusters, parts * halves, size).swapaxes(0, 1)]
    ppermute x0 -> x19, waiting for transfers between devices: none -> 10.3 us  [passed(): return lax.ppermute(values, 'clus', pairs)]
    another operation x7 -> x0, other arithmetic: 5.89 us -> none
    broadcast_in_dim x12 -> x1, local copies, waits for them, and re-layouts: 4.6 us -> 0.01 us  [local(): far = jnp.zeros((halves, vecs, size), jnp.float32)]
  transfers between devices with their start and end apart: 1 -> 19, of which waited for: 0 -> 5; matrix products, arithmetic and copies ran while one was open for 36% -> 0% of each run, Pallas kernels for 14% -> 32%
where the time goes in v2:
time: 79.4 us; the launch traced here: 79.2 us
  Pallas kernels  39.4 us (50%)
  starting transfers between devices  14.9 us (19%)
  blocking collectives  12.6 us (16%)
  waiting for transfers between devices  10.3 us (13%)
  local copies, waits for them, and re-layouts  1.08 us (1%)
  between operations  0.87 us (1%)
    pallas_call x7, Pallas kernels, call(): pl.pallas_call(kernel, out_shape=out_shape, in_specs=specs(len(operands),...  39.4 us
    ppermute x19, starting transfers between devices, passed(): return lax.ppermute(values, 'clus', pairs)  14.9 us
    all_to_all x1, blocking collectives, local(): lax.all_to_all(products, 'clus', split_axis=0, concat_axis=0, tiled=True)  12.6 us
    ppermute x19, waiting for transfers between devices, passed(): return lax.ppermute(values, 'clus', pairs)  10.3 us
  transfers between devices with their start and end apart: 19, of which 5 were waited for; matrix products, arithmetic and copies ran while one was open for 0% of the time, Pallas kernels for 32%

profile of v2, /device:TPU:0, one launch (start us, length us, event | category | flops | bytes accessed | tf_op | source)
XLA Modules:
  0.0 79.2 jit_solution(15022982594513037332)
XLA Ops:
  0.7 2.2 %shard_map.112.message_ref.refs_5_ = bf16[640,256]{1,0:T(8,128)(2,1)} custom-call(f32[16,32,256]{2,1,0:T(8,128)} %refs_12_.1, bf16[16,32,256]{2,1,0:T(8,128)(2,1)} %refs_9_.1, f32[16,32]{1,0:T(8,128)} %refs_10_.1, bf16[3,16,256]{2,1,0:T(8,128)(2,1)} %bitcast.8, bf16[3,16,32]{2,1,0:T(8,128)(2,1)} %bitcast.9, s32[1,3,2,16]{3,2,1,0:T(2,128)} %bitcast.3), custom_call_target="tpu_custom_call" | custom-call | bytes 1048576 | tf_op jit(solution)/shard_map/pallas_call | solution.py:352
  2.9 0.5 collective-permute-start
  3.4 4.6 %collective-permute-start.1 = (bf16[640,256]{1,0:T(8,128)(2,1)}, bf16[640,256]{1,0:T(8,128)(2,1)S(1)}, u32[]{:S(2)}, u32[]{:S(2)}) collective-permute-start(bf16[640,256]{1,0:T(8,128)(2,1)} %shard_map.112.message_ref.refs_5_), channel_id=1, source_target_pairs={{0,12},{1,13},{2,14},{3,15},{4,8},{5,9},{6,10},{7,11},{8,4},{9,5},... | collective-permute-start | bytes 983048 | tf_op jit(solution)/shard_map/ppermute | solution.py:368
  8.0 1.5 %collective-permute-start.3 = (bf16[640,256]{1,0:T(8,128)(2,1)}, bf16[640,256]{1,0:T(8,128)(2,1)S(1)}, u32[]{:S(2)}, u32[]{:S(2)}) collective-permute-start(bf16[640,256]{1,0:T(8,128)(2,1)} %shard_map.112.message_ref.refs_5_), channel_id=1, source_target_pairs={{0,2},{1,3},{2,0},{3,1},{4,6},{5,7},{6,4},{7,5},{8,10},{9,11},{10,... | collective-permute-start | bytes 983048 | tf_op jit(solution)/shard_map/ppermute | solution.py:368
  9.5 1.0 %copy-done.1 = bf16[640,256]{1,0:T(8,128)(2,1)S(1)} copy-done((bf16[640,256]{1,0:T(8,128)(2,1)S(1)}, bf16[640,256]{1,0:T(8,128)(2,1)}, u32[]{:S(2)}) %copy-start.1) | copy-done | bytes 327704
  10.5 2.9 %shard_map.113 = (f32[17,32,256]{2,1,0:T(8,128)S(1)}, f32[32,64]{1,0:T(8,128)S(1)}, bf16[17,256,16]{2,1,0:T(8,128)(2,1)S(1)}, bf16[2,256,16]{2,1,0:T(8,128)(2,1)S(1)}, f32[32,16,256]{2,1,0:T(8,128)S(1)}) custom-call(bf16[640,256]{1,0:T(8,128)(2,1)S(1)} %copy-done.1, s32[16,64]{1,0:T(8,128)S(1)} %copy-done.8, f32[16,32,256]{2,1,0:T(8,128)S(1)} %copy-done, ...), custom_call_target="tpu_custom_call" | custom-call | flops 2147483648 | bytes 1048576 | tf_op jit(solution)/shard_map/pallas_call | solution.py:352
  13.4 3.9 %shard_map.114 = (f32[17,32,256]{2,1,0:T(8,128)S(1)}, f32[2,32,256]{2,1,0:T(8,128)S(1)}) custom-call(s32[1,3,2,16]{3,2,1,0:T(2,128)S(1)} %bitcast.4, f32[17,32,256]{2,1,0:T(8,128)S(1)} %get-tuple-element.26.refs_0_, f32[2,32,256]{2,1,0:T(8,128)S(1)} %broadcast_in_dim.3.refs_1_, bf16[17,256,16]{2,1,0:T(8,128)(2,1)S(1)} %get-tuple-element.27.refs_2_, ...), custom_call_target="tpu_custom_call" | custom-call | flops 536870912 | bytes 1048576 | tf_op jit(solution)/shard_map/pallas_call | solution.py:352
  17.3 6.4 %collective-permute-done.2.refs_6_ = bf16[640,256]{1,0:T(8,128)(2,1)S(1)} collective-permute-done((bf16[640,256]{1,0:T(8,128)(2,1)}, bf16[640,256]{1,0:T(8,128)(2,1)S(1)}, u32[]{:S(2)}, u32[]{:S(2)}) %collective-permute-start.2) | collective-permute-done | bytes 327712 | tf_op jit(solution)/shard_map/ppermute | solution.py:368
  23.7 0.0 collective-permute-start.4
  23.7 0.5 collective-permute-start.5
  24.2 0.0 collective-permute-start.6
  24.2 1.6 %collective-permute-start.7 = (bf16[640,256]{1,0:T(8,128)(2,1)S(1)}, bf16[640,256]{1,0:T(8,128)(2,1)S(1)}, u32[]{:S(2)}, u32[]{:S(2)}) collective-permute-start(bf16[640,256]{1,0:T(8,128)(2,1)S(1)} %collective-permute-done.1.refs_5_), channel_id=1, source_target_pairs={{0,4},{1,5},{2,6},{3,7},{4,0},{5,1},{6,2},{7,3},{8,12},{9,13},{10,... | collective-permute-start | bytes 983048 | tf_op jit(solution)/shard_map/ppermute | solution.py:368
  25.9 1.5 %collective-permute-start.8 = (bf16[640,256]{1,0:T(8,128)(2,1)S(1)}, bf16[640,256]{1,0:T(8,128)(2,1)S(1)}, u32[]{:S(2)}, u32[]{:S(2)}) collective-permute-start(bf16[640,256]{1,0:T(8,128)(2,1)S(1)} %collective-permute-done.1.refs_5_), channel_id=1, source_target_pairs={{0,2},{1,3},{2,0},{3,1},{4,6},{5,7},{6,4},{7,5},{8,10},{9,11},{10,... | collective-permute-start | bytes 983048 | tf_op jit(solution)/shard_map/ppermute | solution.py:368
  27.5 0.6 collective-permute-start.10
  28.0 0.5 collective-permute-start.9
  28.5 8.8 %shard_map.115 = (f32[17,32,256]{2,1,0:T(8,128)S(1)}, f32[2,32,256]{2,1,0:T(8,128)S(1)}) custom-call(s32[1,3,2,16]{3,2,1,0:T(2,128)S(1)} %bitcast.5, f32[17,32,256]{2,1,0:T(8,128)S(1)} %get-tuple-element.32.refs_0_, f32[2,32,256]{2,1,0:T(8,128)S(1)} %get-tuple-element.33.refs_1_, bf16[17,256,16]{2,1,0:T(8,128)(2,1)S(1)} %get-tuple-element.27.refs_2_, ...), custom_call_target="tpu_custom_call" | custom-call | flops 1610612736 | bytes 1048576 | tf_op jit(solution)/shard_map/pallas_call | solution.py:352
  37.4 1.9 %collective-permute-done.10.refs_8_ = bf16[320,256]{1,0:T(8,128)(2,1)S(1)} collective-permute-done((bf16[320,256]{1,0:T(8,128)(2,1)S(1)}, bf16[320,256]{1,0:T(8,128)(2,1)S(1)}, u32[]{:S(2)}, u32[]{:S(2)}) %collective-permute-start.10) | collective-permute-done | bytes 163872 | tf_op jit(solution)/shard_map/ppermute | solution.py:368
  39.3 0.1 collective-permute-start.11
  39.3 0.5 collective-permute-start.12
  39.8 0.1 collective-permute-start.13
  39.9 0.4 collective-permute-start.14
  40.4 0.4 collective-permute-start.15
  40.8 0.9 %collective-permute-done.13.refs_11_ = bf16[320,256]{1,0:T(8,128)(2,1)S(1)} collective-permute-done((bf16[320,256]{1,0:T(8,128)(2,1)S(1)}, bf16[320,256]{1,0:T(8,128)(2,1)S(1)}, u32[]{:S(2)}, u32[]{:S(2)}) %collective-permute-start.13) | collective-permute-done | bytes 163872 | tf_op jit(solution)/shard_map/ppermute | solution.py:368
  41.7 1.5 %collective-permute-start.16 = (bf16[320,256]{1,0:T(8,128)(2,1)S(1)}, bf16[320,256]{1,0:T(8,128)(2,1)S(1)}, u32[]{:S(2)}, u32[]{:S(2)}) collective-permute-start(bf16[320,256]{1,0:T(8,128)(2,1)S(1)} %slice.15), channel_id=1, source_target_pairs={{0,2},{1,3},{2,0},{3,1},{4,6},{5,7},{6,4},{7,5},{8,10},{9,11},{10,... | collective-permute-start | bytes 491528 | tf_op jit(solution)/shard_map/ppermute | solution.py:368
  43.2 9.9 %shard_map.116 = (f32[17,32,256]{2,1,0:T(8,128)S(1)}, f32[2,32,256]{2,1,0:T(8,128)S(1)}) custom-call(s32[1,3,2,16]{3,2,1,0:T(2,128)S(1)} %bitcast.6, f32[17,32,256]{2,1,0:T(8,128)S(1)} %get-tuple-element.37.refs_0_, f32[2,32,256]{2,1,0:T(8,128)S(1)} %get-tuple-element.38.refs_1_, bf16[17,256,16]{2,1,0:T(8,128)(2,1)S(1)} %get-tuple-element.27.refs_2_, ...), custom_call_target="tpu_custom_call" | custom-call | flops 1610612736 | bytes 1048576 | tf_op jit(solution)/shard_map/pallas_call | solution.py:352
  53.1 0.1 collective-permute-start.17
  53.2 0.5 collective-permute-start.18
  53.7 0.9 %collective-permute-done.17.refs_7_ = bf16[320,256]{1,0:T(8,128)(2,1)S(1)} collective-permute-done((bf16[320,256]{1,0:T(8,128)(2,1)S(1)}, bf16[320,256]{1,0:T(8,128)(2,1)S(1)}, u32[]{:S(2)}, u32[]{:S(2)}) %collective-permute-start.17) | collective-permute-done | bytes 163872 | tf_op jit(solution)/shard_map/ppermute | solution.py:368
  54.6 0.2 collective-permute-done.18.refs_8_
  54.8 6.8 %shard_map.117 = (f32[16,64,256]{2,1,0:T(8,128)S(1)}, f32[16,32,128]{2,1,0:T(8,128)S(1)}) custom-call(s32[1,3,2,16]{3,2,1,0:T(2,128)S(1)} %bitcast.7, f32[17,32,256]{2,1,0:T(8,128)S(1)} %get-tuple-element.43.refs_0_, f32[2,32,256]{2,1,0:T(8,128)S(1)} %get-tuple-element.44.refs_1_, bf16[17,256,16]{2,1,0:T(8,128)(2,1)S(1)} %get-tuple-element.27.refs_2_, ...), custom_call_target="tpu_custom_call" | custom-call | flops 536870912 | bytes 1048576 | tf_op jit(solution)/shard_map/pallas_call | solution.py:352
  61.6 12.6 %all_to_all.5.products_ref = f32[16,32,128]{2,1,0:T(8,128)S(1)} all-to-all(f32[16,32,128]{2,1,0:T(8,128)S(1)} %get-tuple-element.47), channel_id=1, replica_groups=mesh['group'=2,'clus'=16] {'clus'}, dimensions={0} | all-to-all | bytes 524288 | tf_op jit(solution)/shard_map/all_to_all | solution.py:497
  74.3 5.0 %shard_map.118 = (f32[16,32,256]{2,1,0:T(8,128)}, f32[32,32]{1,0:T(8,128)}, f32[32,32]{1,0:T(8,128)}) custom-call(f32[16,32,128]{2,1,0:T(8,128)S(1)} %all_to_all.5.products_ref, f32[16,64,256]{2,1,0:T(8,128)S(1)} %get-tuple-element.48.stacked_ref), custom_call_target="tpu_custom_call" | custom-call | bytes 1048576 | tf_op jit(solution)/shard_map/pallas_call | solution.py:352
  (37 shorter events, 0.1 us)
Async XLA Ops:
  0.6 8.9 %copy-start = (f32[16,32,256]{2,1,0:T(8,128)S(1)}, f32[16,32,256]{2,1,0:T(8,128)}, u32[]{:S(2)}) copy-start(f32[16,32,256]{2,1,0:T(8,128)} %refs_12_.1) | copy-start | bytes 1572868
  0.6 8.9 %copy-start.6 = (f32[16,32,256]{2,1,0:T(8,128)S(1)}, f32[16,32,256]{2,1,0:T(8,128)}, u32[]{:S(2)}) copy-start(f32[16,32,256]{2,1,0:T(8,128)} %prior_ref.1) | copy-start | bytes 1572868
  0.7 8.8 %copy-start.7 = (f32[32,32]{1,0:T(8,128)S(1)}, f32[32,32]{1,0:T(8,128)}, u32[]{:S(2)}) copy-start(f32[32,32]{1,0:T(8,128)} %beta_ref.1) | copy-start | bytes 12292
  0.7 8.8 %copy-start.8 = (s32[16,64]{1,0:T(8,128)S(1)}, s32[16,64]{1,0:T(8,128)}, u32[]{:S(2)}) copy-start(s32[16,64]{1,0:T(8,128)} %far_ref.1) | copy-start | bytes 12292
  0.7 12.7 %copy-start.5 = (s32[1,16,3,2]{1,3,2,0:T(2,128)S(1)}, s32[1,16,3,2]{1,3,2,0:T(2,128)}, u32[]{:S(2)}) copy-start(s32[1,16,3,2]{1,3,2,0:T(2,128)} %param.16) | copy-start | bytes 1156
  2.9 10.4 %collective-permute-start = (bf16[640,256]{1,0:T(8,128)(2,1)}, bf16[640,256]{1,0:T(8,128)(2,1)S(1)}, u32[]{:S(2)}, u32[]{:S(2)}) collective-permute-start(bf16[640,256]{1,0:T(8,128)(2,1)} %shard_map.112.message_ref.refs_5_), channel_id=1, source_target_pairs={{0,1},{1,0},{2,3},{3,2},{4,5},{5,4},{6,7},{7,6},{8,9},{9,8},{10,11... | collective-permute-start | bytes 983048 | tf_op jit(solution)/shard_map/ppermute | solution.py:368
  3.4 13.9 %collective-permute-start.1 = (bf16[640,256]{1,0:T(8,128)(2,1)}, bf16[640,256]{1,0:T(8,128)(2,1)S(1)}, u32[]{:S(2)}, u32[]{:S(2)}) collective-permute-start(bf16[640,256]{1,0:T(8,128)(2,1)} %shard_map.112.message_ref.refs_5_), channel_id=1, source_target_pairs={{0,12},{1,13},{2,14},{3,15},{4,8},{5,9},{6,10},{7,11},{8,4},{9,5},... | collective-permute-start | bytes 983048 | tf_op jit(solution)/shard_map/ppermute | solution.py:368
  8.0 15.7 %collective-permute-start.2 = (bf16[640,256]{1,0:T(8,128)(2,1)}, bf16[640,256]{1,0:T(8,128)(2,1)S(1)}, u32[]{:S(2)}, u32[]{:S(2)}) collective-permute-start(bf16[640,256]{1,0:T(8,128)(2,1)} %shard_map.112.message_ref.refs_5_), channel_id=1, source_target_pairs={{0,4},{1,5},{2,6},{3,7},{4,0},{5,1},{6,2},{7,3},{8,12},{9,13},{10,... | collective-permute-start | bytes 983048 | tf_op jit(solution)/shard_map/ppermute | solution.py:368
  8.0 15.7 %collective-permute-start.3 = (bf16[640,256]{1,0:T(8,128)(2,1)}, bf16[640,256]{1,0:T(8,128)(2,1)S(1)}, u32[]{:S(2)}, u32[]{:S(2)}) collective-permute-start(bf16[640,256]{1,0:T(8,128)(2,1)} %shard_map.112.message_ref.refs_5_), channel_id=1, source_target_pairs={{0,2},{1,3},{2,0},{3,1},{4,6},{5,7},{6,4},{7,5},{8,10},{9,11},{10,... | collective-permute-start | bytes 983048 | tf_op jit(solution)/shard_map/ppermute | solution.py:368
  9.5 1.0 %copy-start.1 = (bf16[640,256]{1,0:T(8,128)(2,1)S(1)}, bf16[640,256]{1,0:T(8,128)(2,1)}, u32[]{:S(2)}) copy-start(bf16[640,256]{1,0:T(8,128)(2,1)} %shard_map.112.message_ref.refs_5_) | copy-start | bytes 983044
  10.5 2.9 %copy-start.2 = (bf16[640,256]{1,0:T(8,128)(2,1)S(1)}, bf16[640,256]{1,0:T(8,128)(2,1)}, u32[]{:S(2)}) copy-start(bf16[640,256]{1,0:T(8,128)(2,1)} %shard_map.112.message_ref.refs_5_) | copy-start | bytes 983044
  23.7 3.8 %collective-permute-start.4 = (bf16[640,256]{1,0:T(8,128)(2,1)S(1)}, bf16[640,256]{1,0:T(8,128)(2,1)S(1)}, u32[]{:S(2)}, u32[]{:S(2)}) collective-permute-start(bf16[640,256]{1,0:T(8,128)(2,1)S(1)} %collective-permute-done.1.refs_5_), channel_id=1, source_target_pairs={{0,1},{1,0},{2,3},{3,2},{4,5},{5,4},{6,7},{7,6},{8,9},{9,8},{10,11... | collective-permute-start | bytes 983048 | tf_op jit(solution)/shard_map/ppermute | solution.py:368
  23.7 4.3 %collective-permute-start.5 = (bf16[640,256]{1,0:T(8,128)(2,1)S(1)}, bf16[640,256]{1,0:T(8,128)(2,1)S(1)}, u32[]{:S(2)}, u32[]{:S(2)}) collective-permute-start(bf16[640,256]{1,0:T(8,128)(2,1)S(1)} %collective-permute-done.2.refs_6_), channel_id=1, source_target_pairs={{0,1},{1,0},{2,3},{3,2},{4,5},{5,4},{6,7},{7,6},{8,9},{9,8},{10,11... | collective-permute-start | bytes 983048 | tf_op jit(solution)/shard_map/ppermute | solution.py:368
  24.2 4.3 %collective-permute-start.6 = (bf16[640,256]{1,0:T(8,128)(2,1)S(1)}, bf16[640,256]{1,0:T(8,128)(2,1)S(1)}, u32[]{:S(2)}, u32[]{:S(2)}) collective-permute-start(bf16[640,256]{1,0:T(8,128)(2,1)S(1)} %collective-permute-done.3.refs_7_), channel_id=1, source_target_pairs={{0,1},{1,0},{2,3},{3,2},{4,5},{5,4},{6,7},{7,6},{8,9},{9,8},{10,11... | collective-permute-start | bytes 983048 | tf_op jit(solution)/shard_map/ppermute | solution.py:368
  24.2 15.0 %collective-permute-start.7 = (bf16[640,256]{1,0:T(8,128)(2,1)S(1)}, bf16[640,256]{1,0:T(8,128)(2,1)S(1)}, u32[]{:S(2)}, u32[]{:S(2)}) collective-permute-start(bf16[640,256]{1,0:T(8,128)(2,1)S(1)} %collective-permute-done.1.refs_5_), channel_id=1, source_target_pairs={{0,4},{1,5},{2,6},{3,7},{4,0},{5,1},{6,2},{7,3},{8,12},{9,13},{10,... | collective-permute-start | bytes 983048 | tf_op jit(solution)/shard_map/ppermute | solution.py:368
  25.9 13.4 %collective-permute-start.8 = (bf16[640,256]{1,0:T(8,128)(2,1)S(1)}, bf16[640,256]{1,0:T(8,128)(2,1)S(1)}, u32[]{:S(2)}, u32[]{:S(2)}) collective-permute-start(bf16[640,256]{1,0:T(8,128)(2,1)S(1)} %collective-permute-done.1.refs_5_), channel_id=1, source_target_pairs={{0,2},{1,3},{2,0},{3,1},{4,6},{5,7},{6,4},{7,5},{8,10},{9,11},{10,... | collective-permute-start | bytes 983048 | tf_op jit(solution)/shard_map/ppermute | solution.py:368
  27.5 11.8 %collective-permute-start.10 = (bf16[320,256]{1,0:T(8,128)(2,1)S(1)}, bf16[320,256]{1,0:T(8,128)(2,1)S(1)}, u32[]{:S(2)}, u32[]{:S(2)}) collective-permute-start(bf16[320,256]{1,0:T(8,128)(2,1)S(1)} %slice.13), channel_id=1, source_target_pairs={{0,2},{1,3},{2,0},{3,1},{4,6},{5,7},{6,4},{7,5},{8,10},{9,11},{10,... | collective-permute-start | bytes 491528 | tf_op jit(solution)/shard_map/ppermute | solution.py:368
  28.0 11.2 %collective-permute-start.9 = (bf16[320,256]{1,0:T(8,128)(2,1)S(1)}, bf16[320,256]{1,0:T(8,128)(2,1)S(1)}, u32[]{:S(2)}, u32[]{:S(2)}) collective-permute-start(bf16[320,256]{1,0:T(8,128)(2,1)S(1)} %slice.12), channel_id=1, source_target_pairs={{0,4},{1,5},{2,6},{3,7},{4,0},{5,1},{6,2},{7,3},{8,12},{9,13},{10,... | collective-permute-start | bytes 491528 | tf_op jit(solution)/shard_map/ppermute | solution.py:368
  39.3 3.9 %collective-permute-start.11 = (bf16[640,256]{1,0:T(8,128)(2,1)S(1)}, bf16[640,256]{1,0:T(8,128)(2,1)S(1)}, u32[]{:S(2)}, u32[]{:S(2)}) collective-permute-start(bf16[640,256]{1,0:T(8,128)(2,1)S(1)} %collective-permute-done.7.refs_5_), channel_id=1, source_target_pairs={{0,1},{1,0},{2,3},{3,2},{4,5},{5,4},{6,7},{7,6},{8,9},{9,8},{10,11... | collective-permute-start | bytes 983048 | tf_op jit(solution)/shard_map/ppermute | solution.py:368
  39.3 3.8 %collective-permute-start.12 = (bf16[640,256]{1,0:T(8,128)(2,1)S(1)}, bf16[640,256]{1,0:T(8,128)(2,1)S(1)}, u32[]{:S(2)}, u32[]{:S(2)}) collective-permute-start(bf16[640,256]{1,0:T(8,128)(2,1)S(1)} %collective-permute-done.8.refs_6_), channel_id=1, source_target_pairs={{0,1},{1,0},{2,3},{3,2},{4,5},{5,4},{6,7},{7,6},{8,9},{9,8},{10,11... | collective-permute-start | bytes 983048 | tf_op jit(solution)/shard_map/ppermute | solution.py:368
  39.8 1.8 %collective-permute-start.13 = (bf16[320,256]{1,0:T(8,128)(2,1)S(1)}, bf16[320,256]{1,0:T(8,128)(2,1)S(1)}, u32[]{:S(2)}, u32[]{:S(2)}) collective-permute-start(bf16[320,256]{1,0:T(8,128)(2,1)S(1)} %collective-permute-done.9.refs_7_), channel_id=1, source_target_pairs={{0,1},{1,0},{2,3},{3,2},{4,5},{5,4},{6,7},{7,6},{8,9},{9,8},{10,11... | collective-permute-start | bytes 491528 | tf_op jit(solution)/shard_map/ppermute | solution.py:368
  39.9 3.3 %collective-permute-start.14 = (bf16[320,256]{1,0:T(8,128)(2,1)S(1)}, bf16[320,256]{1,0:T(8,128)(2,1)S(1)}, u32[]{:S(2)}, u32[]{:S(2)}) collective-permute-start(bf16[320,256]{1,0:T(8,128)(2,1)S(1)} %collective-permute-done.10.refs_8_), channel_id=1, source_target_pairs={{0,1},{1,0},{2,3},{3,2},{4,5},{5,4},{6,7},{7,6},{8,9},{9,8},{10,11... | collective-permute-start | bytes 491528 | tf_op jit(solution)/shard_map/ppermute | solution.py:368
  40.4 12.7 %collective-permute-start.15 = (bf16[320,256]{1,0:T(8,128)(2,1)S(1)}, bf16[320,256]{1,0:T(8,128)(2,1)S(1)}, u32[]{:S(2)}, u32[]{:S(2)}) collective-permute-start(bf16[320,256]{1,0:T(8,128)(2,1)S(1)} %slice.14), channel_id=1, source_target_pairs={{0,4},{1,5},{2,6},{3,7},{4,0},{5,1},{6,2},{7,3},{8,12},{9,13},{10,... | collective-permute-start | bytes 491528 | tf_op jit(solution)/shard_map/ppermute | solution.py:368
  41.7 11.4 %collective-permute-start.16 = (bf16[320,256]{1,0:T(8,128)(2,1)S(1)}, bf16[320,256]{1,0:T(8,128)(2,1)S(1)}, u32[]{:S(2)}, u32[]{:S(2)}) collective-permute-start(bf16[320,256]{1,0:T(8,128)(2,1)S(1)} %slice.15), channel_id=1, source_target_pairs={{0,2},{1,3},{2,0},{3,1},{4,6},{5,7},{6,4},{7,5},{8,10},{9,11},{10,... | collective-permute-start | bytes 491528 | tf_op jit(solution)/shard_map/ppermute | solution.py:368
  43.2 11.6 %copy-start.3 = (bf16[16,32,256]{2,1,0:T(8,128)(2,1)S(1)}, bf16[16,32,256]{2,1,0:T(8,128)(2,1)}, u32[]{:S(2)}) copy-start(bf16[16,32,256]{2,1,0:T(8,128)(2,1)} %refs_9_.1) | copy-start | bytes 786436
  43.2 11.6 %copy-start.4 = (f32[16,32]{1,0:T(8,128)S(1)}, f32[16,32]{1,0:T(8,128)}, u32[]{:S(2)}) copy-start(f32[16,32]{1,0:T(8,128)} %refs_10_.1) | copy-start | bytes 6148
  53.1 1.5 %collective-permute-start.17 = (bf16[320,256]{1,0:T(8,128)(2,1)S(1)}, bf16[320,256]{1,0:T(8,128)(2,1)S(1)}, u32[]{:S(2)}, u32[]{:S(2)}) collective-permute-start(bf16[320,256]{1,0:T(8,128)(2,1)S(1)} %collective-permute-done.15.refs_5_), channel_id=1, source_target_pairs={{0,1},{1,0},{2,3},{3,2},{4,5},{5,4},{6,7},{7,6},{8,9},{9,8},{10,11... | collective-permute-start | bytes 491528 | tf_op jit(solution)/shard_map/ppermute | solution.py:368
  53.2 1.6 %collective-permute-start.18 = (bf16[320,256]{1,0:T(8,128)(2,1)S(1)}, bf16[320,256]{1,0:T(8,128)(2,1)S(1)}, u32[]{:S(2)}, u32[]{:S(2)}) collective-permute-start(bf16[320,256]{1,0:T(8,128)(2,1)S(1)} %collective-permute-done.16.refs_6_), channel_id=1, source_target_pairs={{0,1},{1,0},{2,3},{3,2},{4,5},{5,4},{6,7},{7,6},{8,9},{9,8},{10,11... | collective-permute-start | bytes 491528 | tf_op jit(solution)/shard_map/ppermute | solution.py:368

commit v3 on v2

--- a/solution.py
+++ b/solution.py
@@ -10,17 +10,17 @@
 
 root_three = 1.7320508075688772
 length_scale = 0.15
-steepness = root_three / length_scale
+scale = root_three / length_scale * math.log2(math.e)
 feature_count = 16
-unroll = 8
+unroll = 16
 NT = (((1,), (1,)), ((), ()))
 
 
 def kernel_values(squared):
-    squared = jnp.maximum(squared, 1e-12)
+    squared = jnp.maximum(squared, 1e-9)
     distance = squared * lax.rsqrt(squared)
-    decay = jnp.exp2(distance * (-steepness * math.log2(math.e)))
-    return (1.0 + distance * steepness) * decay
+    decay = jnp.exp2(math.log2(math.log(2.0)) - distance)
+    return (distance + 1.0 / math.log(2.0)) * decay
 
 
 def dot_nt(left, right):
@@ -55,12 +55,16 @@
     return values_of(left_features, right_features).astype(jnp.bfloat16)
 
 
+def pieces_of(values):
+    high = values.astype(jnp.bfloat16).astype(jnp.float32)
+    rest = values - high
+    middle = rest.astype(jnp.bfloat16).astype(jnp.float32)
+    return [high, middle, rest - middle]
+
+
 def norm_pieces(axes):
     norm = axes[0] * axes[0] + axes[1] * axes[1] + axes[2] * axes[2]
-    high = norm.astype(jnp.bfloat16).astype(jnp.float32)
-    rest = norm - high
-    middle = rest.astype(jnp.bfloat16).astype(jnp.float32)
-    return [high, middle, rest - middle]
+    return pieces_of(norm * (scale * scale))
 
 
 def stack_rows(rows):
@@ -70,12 +74,13 @@
 
 def left_rows(axes):
     one = jnp.ones_like(axes[0])
-    return stack_rows(list(axes) + norm_pieces(axes) + [one, one, one])
+    return stack_rows([axis for axis in axes for _ in range(3)] + norm_pieces(axes) + [one] * 3)
 
 
 def right_rows(axes):
     one = jnp.ones_like(axes[0])
-    return stack_rows([-2.0 * axis for axis in axes] + [one, one, one] + norm_pieces(axes))
+    crossed = [piece for axis in axes for piece in pieces_of(axis * (-2.0 * scale * scale))]
+    return stack_rows(crossed + [one] * 3 + norm_pieces(axes))
 
 
 def layout_of(clusters, vecs, rank, size):
@@ -229,7 +234,7 @@
     copy = pltpu.make_async_copy(ids_ref, ids_scalar_ref, copied)
     copy.start()
 
-    pair = 2 if devices % 2 == 0 else 1
+    pair = devices // 2 if devices % 2 == 0 else 1
 
     def far_step(turn, carry):
         terms = []
@@ -248,8 +253,8 @@
                     tile = tile.reshape(per_row, rank, size) * weights[:, None, :]
                     tile = tile.reshape(per_row * rank, size).astype(jnp.bfloat16)
                     terms.append((side, dot_nt(sources, tile)))
-        for side in range(halves):
-            far_ref[side] += functools.reduce(jnp.add, [term for place, term in terms if place == side])
+        for side, term in terms:
+            far_ref[side] += term
         return carry
 
     lax.fori_loop(0, devices // pair, far_step, 0)
@@ -280,29 +285,54 @@
         rounded = term.astype(jnp.bfloat16).astype(jnp.float32)
         return own, jnp.where(mirror_ref[place] > 0, rounded, term)
 
-    def near_step(turn, carry):
-        terms = [entry(unroll * turn + place) for place in range(unroll)]
+    def near_step(first, together):
+        terms = [entry(first + place) for place in range(together)]
         for own, term in terms:
             total_ref[own] += term
+
+    half, few = unroll // 2, unroll // 4
+    turns = lax.div(live + (few - 1), unroll)
+
+    def full_step(turn, carry):
+        near_step(unroll * turn, unroll)
         return carry
 
-    lax.fori_loop(0, lax.div(live + (unroll - 1), unroll), near_step, 0)
+    lax.fori_loop(0, turns, full_step, 0)
+    done = unroll * turns
+    more = live - done > few
+
+    @pl.when(more)
+    def _():
+        near_step(done, half)
+
+    done = done + jnp.where(more, half, 0)
+
+    @pl.when(live > done)
+    def _():
+        near_step(done, few)
+
     if not last:
         total_out[...] = total_ref[...]
         far_out[...] = far_ref[...]
         return
 
     sums = jnp.zeros((2 * vecs, vecs), jnp.float32)
-    for cluster in range(clusters):
-        side, first = cluster // per_row, (cluster % per_row) * rank
-        part = far_ref[side][:, first : first + rank]
-        lifted = (part * scales_ref[cluster : cluster + 1, :]).astype(jnp.bfloat16)
-        shifted = total_ref[cluster] + jnp.dot(
-            lifted, basis_ref[cluster], preferred_element_type=jnp.float32
-        )
-        stacked = jnp.concatenate([block_ref[cluster], shifted], axis=0)
-        stacked_ref[cluster] = stacked
-        sums += dot_split(stacked, shifted)
+    place_ids = lax.broadcasted_iota(jnp.int32, (per_row, vecs, size), 0)
+    lane_ids = lax.broadcasted_iota(jnp.int32, (per_row, vecs, size), 2)
+    own_lanes = lax.div(lane_ids, rank) == place_ids
+    for side in range(halves):
+        scales = scales_ref[side * per_row : (side + 1) * per_row, :]
+        scales = jnp.concatenate([scales[place : place + 1] for place in range(per_row)], axis=1)
+        lifted = jnp.where(own_lanes, (far_ref[side] * scales)[None], 0.0)
+        lifted = lifted.reshape(per_row * vecs, size).astype(jnp.bfloat16)
+        basis = basis_ref[side * per_row : (side + 1) * per_row].reshape(per_row * rank, size)
+        terms = jnp.dot(lifted, basis, preferred_element_type=jnp.float32)
+        for place in range(per_row):
+            cluster = side * per_row + place
+            shifted = total_ref[cluster] + terms[place * vecs : (place + 1) * vecs]
+            stacked = jnp.concatenate([block_ref[cluster], shifted], axis=0)
+            stacked_ref[cluster] = stacked
+            sums += dot_split(stacked, shifted)
     early = early_ref[...]
     crossed = sums[:vecs]
     products = jnp.concatenate(
@@ -331,10 +361,23 @@
     unit = (rows == columns).astype(jnp.float32)
     work = jnp.concatenate([gram, unit], axis=1)
     row_ids = lax.broadcasted_iota(jnp.int32, (vecs, 1), 0)
-    for step in range(vecs - 1):
-        pivot_row = work[step : step + 1, :]
-        ratio = work[:, step : step + 1] * (1.0 / pivot_row[:, step : step + 1])
-        work = work - jnp.where(row_ids > step, ratio, 0.0) * pivot_row
+    full = (vecs, 2 * vecs)
+    row_full = lax.broadcasted_iota(jnp.int32, full, 0)
+    for step in range(0, vecs - 2, 2):
+        left = jnp.broadcast_to(work[:, step : step + 1], full)
+        right = jnp.broadcast_to(work[:, step + 1 : step + 2], full)
+        first, second = work[step : step + 1, :], work[step + 1 : step + 2, :]
+        corner, side = left[step : step + 1, :], left[step + 1 : step + 2, :]
+        other = right[step + 1 : step + 2, :]
+        scale = 1.0 / (corner * other - side * side)
+        first, second = (other * first - side * second) * scale, (corner * second - side * first) * scale
+        below = row_full > step + 1
+        work = work - jnp.where(below, left * first + right * second, 0.0)
+    pivots = jnp.sum(work[:, :vecs] * unit, axis=1, keepdims=True)
+    beside = (columns == rows + 1).astype(jnp.float32)
+    ratios = jnp.sum(work[:, :vecs] * beside, axis=1, keepdims=True) / pivots
+    taken = jnp.where(row_ids % 2 == 0, ratios, 0.0) * work
+    work = work - jnp.concatenate([jnp.zeros((1, 2 * vecs), jnp.float32), taken[:-1]], axis=0)
     pivots = jnp.sum(work[:, :vecs] * unit, axis=1, keepdims=True)
     work = work * (1.0 / jnp.sqrt(pivots))
     beta_ref[...] = jnp.where(columns >= rows, work[:, :vecs], 0.0)

time: 79.4 us -> 72.5 us (0.913)
  Pallas kernels: 39.4 us -> 30 us
  waiting for transfers between devices: 10.3 us -> 12.8 us
    pallas_call x7, Pallas kernels: 39.4 us -> 30 us  [call(): pl.pallas_call(kernel, out_shape=out_shape, in_specs=specs(len(operands),...]
    ppermute x19, waiting for transfers between devices: 10.3 us -> 12.8 us  [passed(): return lax.ppermute(values, 'clus', pairs)]
  transfers between devices with their start and end apart: 19 -> 19, of which waited for: 5 -> 5; matrix products, arithmetic and copies ran while one was open for 0% -> 0% of each run, Pallas kernels for 32% -> 27%
where the time goes in v3:
time: 72.5 us; the launch traced here: 72.3 us
  Pallas kernels  30 us (41%)
  starting transfers between devices  14.9 us (21%)
  waiting for transfers between devices  12.8 us (18%)
  blocking collectives  12.6 us (17%)
  local copies, waits for them, and re-layouts  1.08 us (1%)
  between operations  0.86 us (1%)
    pallas_call x7, Pallas kernels, call(): pl.pallas_call(kernel, out_shape=out_shape, in_specs=specs(len(operands),...  30 us
    ppermute x19, starting transfers between devices, passed(): return lax.ppermute(values, 'clus', pairs)  14.9 us
    ppermute x19, waiting for transfers between devices, passed(): return lax.ppermute(values, 'clus', pairs)  12.8 us
    all_to_all x1, blocking collectives, local(): lax.all_to_all(products, 'clus', split_axis=0, concat_axis=0, tiled=True)  12.6 us
  transfers between devices with their start and end apart: 19, of which 5 were waited for; matrix products, arithmetic and copies ran while one was open for 0% of the time, Pallas kernels for 27%

profile of v3, /device:TPU:0, one launch (start us, length us, event | category | flops | bytes accessed | tf_op | source)
XLA Modules:
  0.0 72.3 jit_solution(4029641999501951752)
XLA Ops:
  0.7 2.2 %shard_map.112.message_ref.refs_5_ = bf16[640,256]{1,0:T(8,128)(2,1)} custom-call(f32[16,32,256]{2,1,0:T(8,128)} %refs_12_.1, bf16[16,32,256]{2,1,0:T(8,128)(2,1)} %refs_9_.1, f32[16,32]{1,0:T(8,128)} %refs_10_.1, bf16[3,16,256]{2,1,0:T(8,128)(2,1)} %bitcast.8, bf16[3,16,32]{2,1,0:T(8,128)(2,1)} %bitcast.9, s32[1,3,2,16]{3,2,1,0:T(2,128)} %bitcast.3), custom_call_target="tpu_custom_call" | custom-call | bytes 1048576 | tf_op jit(solution)/shard_map/pallas_call | solution.py:395
  2.9 0.5 collective-permute-start
  3.4 4.6 %collective-permute-start.1 = (bf16[640,256]{1,0:T(8,128)(2,1)}, bf16[640,256]{1,0:T(8,128)(2,1)S(1)}, u32[]{:S(2)}, u32[]{:S(2)}) collective-permute-start(bf16[640,256]{1,0:T(8,128)(2,1)} %shard_map.112.message_ref.refs_5_), channel_id=1, source_target_pairs={{0,12},{1,13},{2,14},{3,15},{4,8},{5,9},{6,10},{7,11},{8,4},{9,5},... | collective-permute-start | bytes 983048 | tf_op jit(solution)/shard_map/ppermute | solution.py:411
  8.0 1.5 %collective-permute-start.3 = (bf16[640,256]{1,0:T(8,128)(2,1)}, bf16[640,256]{1,0:T(8,128)(2,1)S(1)}, u32[]{:S(2)}, u32[]{:S(2)}) collective-permute-start(bf16[640,256]{1,0:T(8,128)(2,1)} %shard_map.112.message_ref.refs_5_), channel_id=1, source_target_pairs={{0,2},{1,3},{2,0},{3,1},{4,6},{5,7},{6,4},{7,5},{8,10},{9,11},{10,... | collective-permute-start | bytes 983048 | tf_op jit(solution)/shard_map/ppermute | solution.py:411
  9.5 1.0 %copy-done.1 = bf16[640,256]{1,0:T(8,128)(2,1)S(1)} copy-done((bf16[640,256]{1,0:T(8,128)(2,1)S(1)}, bf16[640,256]{1,0:T(8,128)(2,1)}, u32[]{:S(2)}) %copy-start.1) | copy-done | bytes 327704
  10.5 2.8 %shard_map.113 = (f32[17,32,256]{2,1,0:T(8,128)S(1)}, f32[32,64]{1,0:T(8,128)S(1)}, bf16[17,256,16]{2,1,0:T(8,128)(2,1)S(1)}, bf16[2,256,16]{2,1,0:T(8,128)(2,1)S(1)}, f32[32,16,256]{2,1,0:T(8,128)S(1)}) custom-call(bf16[640,256]{1,0:T(8,128)(2,1)S(1)} %copy-done.1, s32[16,64]{1,0:T(8,128)S(1)} %copy-done.8, f32[16,32,256]{2,1,0:T(8,128)S(1)} %copy-done, ...), custom_call_target="tpu_custom_call" | custom-call | flops 2147483648 | bytes 1048576 | tf_op jit(solution)/shard_map/pallas_call | solution.py:395
  13.3 3.5 %shard_map.114 = (f32[17,32,256]{2,1,0:T(8,128)S(1)}, f32[2,32,256]{2,1,0:T(8,128)S(1)}) custom-call(s32[1,3,2,16]{3,2,1,0:T(2,128)S(1)} %bitcast.4, f32[17,32,256]{2,1,0:T(8,128)S(1)} %get-tuple-element.26.refs_0_, f32[2,32,256]{2,1,0:T(8,128)S(1)} %broadcast_in_dim.3.refs_1_, bf16[17,256,16]{2,1,0:T(8,128)(2,1)S(1)} %get-tuple-element.27.refs_2_, ...), custom_call_target="tpu_custom_call" | custom-call | flops 536870912 | bytes 1048576 | tf_op jit(solution)/shard_map/pallas_call | solution.py:395
  16.8 0.0 collective-permute-done.1.refs_5_
  16.8 6.9 %collective-permute-done.2.refs_6_ = bf16[640,256]{1,0:T(8,128)(2,1)S(1)} collective-permute-done((bf16[640,256]{1,0:T(8,128)(2,1)}, bf16[640,256]{1,0:T(8,128)(2,1)S(1)}, u32[]{:S(2)}, u32[]{:S(2)}) %collective-permute-start.2) | collective-permute-done | bytes 327712 | tf_op jit(solution)/shard_map/ppermute | solution.py:411
  23.7 0.0 collective-permute-start.4
  23.7 0.5 collective-permute-start.5
  24.2 1.6 %collective-permute-start.7 = (bf16[640,256]{1,0:T(8,128)(2,1)S(1)}, bf16[640,256]{1,0:T(8,128)(2,1)S(1)}, u32[]{:S(2)}, u32[]{:S(2)}) collective-permute-start(bf16[640,256]{1,0:T(8,128)(2,1)S(1)} %collective-permute-done.1.refs_5_), channel_id=1, source_target_pairs={{0,4},{1,5},{2,6},{3,7},{4,0},{5,1},{6,2},{7,3},{8,12},{9,13},{10,... | collective-permute-start | bytes 983048 | tf_op jit(solution)/shard_map/ppermute | solution.py:411
  25.9 1.5 %collective-permute-start.8 = (bf16[640,256]{1,0:T(8,128)(2,1)S(1)}, bf16[640,256]{1,0:T(8,128)(2,1)S(1)}, u32[]{:S(2)}, u32[]{:S(2)}) collective-permute-start(bf16[640,256]{1,0:T(8,128)(2,1)S(1)} %collective-permute-done.1.refs_5_), channel_id=1, source_target_pairs={{0,2},{1,3},{2,0},{3,1},{4,6},{5,7},{6,4},{7,5},{8,10},{9,11},{10,... | collective-permute-start | bytes 983048 | tf_op jit(solution)/shard_map/ppermute | solution.py:411
  27.5 0.6 collective-permute-start.10
  28.0 0.5 collective-permute-start.9
  28.5 6.8 %shard_map.115 = (f32[17,32,256]{2,1,0:T(8,128)S(1)}, f32[2,32,256]{2,1,0:T(8,128)S(1)}) custom-call(s32[1,3,2,16]{3,2,1,0:T(2,128)S(1)} %bitcast.5, f32[17,32,256]{2,1,0:T(8,128)S(1)} %get-tuple-element.32.refs_0_, f32[2,32,256]{2,1,0:T(8,128)S(1)} %get-tuple-element.33.refs_1_, bf16[17,256,16]{2,1,0:T(8,128)(2,1)S(1)} %get-tuple-element.27.refs_2_, ...), custom_call_target="tpu_custom_call" | custom-call | flops 1610612736 | bytes 1048576 | tf_op jit(solution)/shard_map/pallas_call | solution.py:395
  35.4 3.9 %collective-permute-done.10.refs_8_ = bf16[320,256]{1,0:T(8,128)(2,1)S(1)} collective-permute-done((bf16[320,256]{1,0:T(8,128)(2,1)S(1)}, bf16[320,256]{1,0:T(8,128)(2,1)S(1)}, u32[]{:S(2)}, u32[]{:S(2)}) %collective-permute-start.10) | collective-permute-done | bytes 163872 | tf_op jit(solution)/shard_map/ppermute | solution.py:411
  39.3 0.1 collective-permute-start.11
  39.3 0.5 collective-permute-start.12
  39.8 0.1 collective-permute-start.13
  39.9 0.4 collective-permute-start.14
  40.4 0.4 collective-permute-start.15
  40.8 0.9 %collective-permute-done.13.refs_11_ = bf16[320,256]{1,0:T(8,128)(2,1)S(1)} collective-permute-done((bf16[320,256]{1,0:T(8,128)(2,1)S(1)}, bf16[320,256]{1,0:T(8,128)(2,1)S(1)}, u32[]{:S(2)}, u32[]{:S(2)}) %collective-permute-start.13) | collective-permute-done | bytes 163872 | tf_op jit(solution)/shard_map/ppermute | solution.py:411
  41.7 1.5 %collective-permute-start.16 = (bf16[320,256]{1,0:T(8,128)(2,1)S(1)}, bf16[320,256]{1,0:T(8,128)(2,1)S(1)}, u32[]{:S(2)}, u32[]{:S(2)}) collective-permute-start(bf16[320,256]{1,0:T(8,128)(2,1)S(1)} %slice.15), channel_id=1, source_target_pairs={{0,2},{1,3},{2,0},{3,1},{4,6},{5,7},{6,4},{7,5},{8,10},{9,11},{10,... | collective-permute-start | bytes 491528 | tf_op jit(solution)/shard_map/ppermute | solution.py:411
  43.2 6.7 %shard_map.116 = (f32[17,32,256]{2,1,0:T(8,128)S(1)}, f32[2,32,256]{2,1,0:T(8,128)S(1)}) custom-call(s32[1,3,2,16]{3,2,1,0:T(2,128)S(1)} %bitcast.6, f32[17,32,256]{2,1,0:T(8,128)S(1)} %get-tuple-element.37.refs_0_, f32[2,32,256]{2,1,0:T(8,128)S(1)} %get-tuple-element.38.refs_1_, bf16[17,256,16]{2,1,0:T(8,128)(2,1)S(1)} %get-tuple-element.27.refs_2_, ...), custom_call_target="tpu_custom_call" | custom-call | flops 1610612736 | bytes 1048576 | tf_op jit(solution)/shard_map/pallas_call | solution.py:395
  49.9 0.1 collective-permute-start.17
  50.0 0.5 collective-permute-start.18
  50.5 0.9 %collective-permute-done.17.refs_7_ = bf16[320,256]{1,0:T(8,128)(2,1)S(1)} collective-permute-done((bf16[320,256]{1,0:T(8,128)(2,1)S(1)}, bf16[320,256]{1,0:T(8,128)(2,1)S(1)}, u32[]{:S(2)}, u32[]{:S(2)}) %collective-permute-start.17) | collective-permute-done | bytes 163872 | tf_op jit(solution)/shard_map/ppermute | solution.py:411
  51.4 0.2 collective-permute-done.18.refs_8_
  51.6 4.1 %shard_map.117 = (f32[16,64,256]{2,1,0:T(8,128)S(1)}, f32[16,32,128]{2,1,0:T(8,128)S(1)}) custom-call(s32[1,3,2,16]{3,2,1,0:T(2,128)S(1)} %bitcast.7, f32[17,32,256]{2,1,0:T(8,128)S(1)} %get-tuple-element.43.refs_0_, f32[2,32,256]{2,1,0:T(8,128)S(1)} %get-tuple-element.44.refs_1_, bf16[17,256,16]{2,1,0:T(8,128)(2,1)S(1)} %get-tuple-element.27.refs_2_, ...), custom_call_target="tpu_custom_call" | custom-call | flops 536870912 | bytes 1048576 | tf_op jit(solution)/shard_map/pallas_call | solution.py:395
  55.8 12.6 %all_to_all.5.products_ref = f32[16,32,128]{2,1,0:T(8,128)S(1)} all-to-all(f32[16,32,128]{2,1,0:T(8,128)S(1)} %get-tuple-element.47), channel_id=1, replica_groups=mesh['group'=2,'clus'=16] {'clus'}, dimensions={0} | all-to-all | bytes 524288 | tf_op jit(solution)/shard_map/all_to_all | solution.py:540
  68.4 3.9 %shard_map.118 = (f32[16,32,256]{2,1,0:T(8,128)}, f32[32,32]{1,0:T(8,128)}, f32[32,32]{1,0:T(8,128)}) custom-call(f32[16,32,128]{2,1,0:T(8,128)S(1)} %all_to_all.5.products_ref, f32[16,64,256]{2,1,0:T(8,128)S(1)} %get-tuple-element.48.stacked_ref), custom_call_target="tpu_custom_call" | custom-call | bytes 1048576 | tf_op jit(solution)/shard_map/pallas_call | solution.py:395
  (37 shorter events, 0.2 us)
Async XLA Ops:
  0.6 8.9 %copy-start = (f32[16,32,256]{2,1,0:T(8,128)S(1)}, f32[16,32,256]{2,1,0:T(8,128)}, u32[]{:S(2)}) copy-start(f32[16,32,256]{2,1,0:T(8,128)} %refs_12_.1) | copy-start | bytes 1572868
  0.6 8.9 %copy-start.6 = (f32[16,32,256]{2,1,0:T(8,128)S(1)}, f32[16,32,256]{2,1,0:T(8,128)}, u32[]{:S(2)}) copy-start(f32[16,32,256]{2,1,0:T(8,128)} %prior_ref.1) | copy-start | bytes 1572868
  0.7 8.8 %copy-start.7 = (f32[32,32]{1,0:T(8,128)S(1)}, f32[32,32]{1,0:T(8,128)}, u32[]{:S(2)}) copy-start(f32[32,32]{1,0:T(8,128)} %beta_ref.1) | copy-start | bytes 12292
  0.7 8.8 %copy-start.8 = (s32[16,64]{1,0:T(8,128)S(1)}, s32[16,64]{1,0:T(8,128)}, u32[]{:S(2)}) copy-start(s32[16,64]{1,0:T(8,128)} %far_ref.1) | copy-start | bytes 12292
  0.7 12.6 %copy-start.5 = (s32[1,16,3,2]{1,3,2,0:T(2,128)S(1)}, s32[1,16,3,2]{1,3,2,0:T(2,128)}, u32[]{:S(2)}) copy-start(s32[1,16,3,2]{1,3,2,0:T(2,128)} %param.16) | copy-start | bytes 1156
  2.9 10.4 %collective-permute-start = (bf16[640,256]{1,0:T(8,128)(2,1)}, bf16[640,256]{1,0:T(8,128)(2,1)S(1)}, u32[]{:S(2)}, u32[]{:S(2)}) collective-permute-start(bf16[640,256]{1,0:T(8,128)(2,1)} %shard_map.112.message_ref.refs_5_), channel_id=1, source_target_pairs={{0,1},{1,0},{2,3},{3,2},{4,5},{5,4},{6,7},{7,6},{8,9},{9,8},{10,11... | collective-permute-start | bytes 983048 | tf_op jit(solution)/shard_map/ppermute | solution.py:411
  3.4 13.5 %collective-permute-start.1 = (bf16[640,256]{1,0:T(8,128)(2,1)}, bf16[640,256]{1,0:T(8,128)(2,1)S(1)}, u32[]{:S(2)}, u32[]{:S(2)}) collective-permute-start(bf16[640,256]{1,0:T(8,128)(2,1)} %shard_map.112.message_ref.refs_5_), channel_id=1, source_target_pairs={{0,12},{1,13},{2,14},{3,15},{4,8},{5,9},{6,10},{7,11},{8,4},{9,5},... | collective-permute-start | bytes 983048 | tf_op jit(solution)/shard_map/ppermute | solution.py:411
  8.0 15.7 %collective-permute-start.2 = (bf16[640,256]{1,0:T(8,128)(2,1)}, bf16[640,256]{1,0:T(8,128)(2,1)S(1)}, u32[]{:S(2)}, u32[]{:S(2)}) collective-permute-start(bf16[640,256]{1,0:T(8,128)(2,1)} %shard_map.112.message_ref.refs_5_), channel_id=1, source_target_pairs={{0,4},{1,5},{2,6},{3,7},{4,0},{5,1},{6,2},{7,3},{8,12},{9,13},{10,... | collective-permute-start | bytes 983048 | tf_op jit(solution)/shard_map/ppermute | solution.py:411
  8.0 15.7 %collective-permute-start.3 = (bf16[640,256]{1,0:T(8,128)(2,1)}, bf16[640,256]{1,0:T(8,128)(2,1)S(1)}, u32[]{:S(2)}, u32[]{:S(2)}) collective-permute-start(bf16[640,256]{1,0:T(8,128)(2,1)} %shard_map.112.message_ref.refs_5_), channel_id=1, source_target_pairs={{0,2},{1,3},{2,0},{3,1},{4,6},{5,7},{6,4},{7,5},{8,10},{9,11},{10,... | collective-permute-start | bytes 983048 | tf_op jit(solution)/shard_map/ppermute | solution.py:411
  9.5 1.0 %copy-start.1 = (bf16[640,256]{1,0:T(8,128)(2,1)S(1)}, bf16[640,256]{1,0:T(8,128)(2,1)}, u32[]{:S(2)}) copy-start(bf16[640,256]{1,0:T(8,128)(2,1)} %shard_map.112.message_ref.refs_5_) | copy-start | bytes 983044
  10.5 2.8 %copy-start.2 = (bf16[640,256]{1,0:T(8,128)(2,1)S(1)}, bf16[640,256]{1,0:T(8,128)(2,1)}, u32[]{:S(2)}) copy-start(bf16[640,256]{1,0:T(8,128)(2,1)} %shard_map.112.message_ref.refs_5_) | copy-start | bytes 983044
  23.7 3.8 %collective-permute-start.4 = (bf16[640,256]{1,0:T(8,128)(2,1)S(1)}, bf16[640,256]{1,0:T(8,128)(2,1)S(1)}, u32[]{:S(2)}, u32[]{:S(2)}) collective-permute-start(bf16[640,256]{1,0:T(8,128)(2,1)S(1)} %collective-permute-done.1.refs_5_), channel_id=1, source_target_pairs={{0,1},{1,0},{2,3},{3,2},{4,5},{5,4},{6,7},{7,6},{8,9},{9,8},{10,11... | collective-permute-start | bytes 983048 | tf_op jit(solution)/shard_map/ppermute | solution.py:411
  23.7 4.3 %collective-permute-start.5 = (bf16[640,256]{1,0:T(8,128)(2,1)S(1)}, bf16[640,256]{1,0:T(8,128)(2,1)S(1)}, u32[]{:S(2)}, u32[]{:S(2)}) collective-permute-start(bf16[640,256]{1,0:T(8,128)(2,1)S(1)} %collective-permute-done.2.refs_6_), channel_id=1, source_target_pairs={{0,1},{1,0},{2,3},{3,2},{4,5},{5,4},{6,7},{7,6},{8,9},{9,8},{10,11... | collective-permute-start | bytes 983048 | tf_op jit(solution)/shard_map/ppermute | solution.py:411
  24.2 4.3 %collective-permute-start.6 = (bf16[640,256]{1,0:T(8,128)(2,1)S(1)}, bf16[640,256]{1,0:T(8,128)(2,1)S(1)}, u32[]{:S(2)}, u32[]{:S(2)}) collective-permute-start(bf16[640,256]{1,0:T(8,128)(2,1)S(1)} %collective-permute-done.3.refs_7_), channel_id=1, source_target_pairs={{0,1},{1,0},{2,3},{3,2},{4,5},{5,4},{6,7},{7,6},{8,9},{9,8},{10,11... | collective-permute-start | bytes 983048 | tf_op jit(solution)/shard_map/ppermute | solution.py:411
  24.2 15.0 %collective-permute-start.7 = (bf16[640,256]{1,0:T(8,128)(2,1)S(1)}, bf16[640,256]{1,0:T(8,128)(2,1)S(1)}, u32[]{:S(2)}, u32[]{:S(2)}) collective-permute-start(bf16[640,256]{1,0:T(8,128)(2,1)S(1)} %collective-permute-done.1.refs_5_), channel_id=1, source_target_pairs={{0,4},{1,5},{2,6},{3,7},{4,0},{5,1},{6,2},{7,3},{8,12},{9,13},{10,... | collective-permute-start | bytes 983048 | tf_op jit(solution)/shard_map/ppermute | solution.py:411
  25.9 13.4 %collective-permute-start.8 = (bf16[640,256]{1,0:T(8,128)(2,1)S(1)}, bf16[640,256]{1,0:T(8,128)(2,1)S(1)}, u32[]{:S(2)}, u32[]{:S(2)}) collective-permute-start(bf16[640,256]{1,0:T(8,128)(2,1)S(1)} %collective-permute-done.1.refs_5_), channel_id=1, source_target_pairs={{0,2},{1,3},{2,0},{3,1},{4,6},{5,7},{6,4},{7,5},{8,10},{9,11},{10,... | collective-permute-start | bytes 983048 | tf_op jit(solution)/shard_map/ppermute | solution.py:411
  27.5 11.8 %collective-permute-start.10 = (bf16[320,256]{1,0:T(8,128)(2,1)S(1)}, bf16[320,256]{1,0:T(8,128)(2,1)S(1)}, u32[]{:S(2)}, u32[]{:S(2)}) collective-permute-start(bf16[320,256]{1,0:T(8,128)(2,1)S(1)} %slice.13), channel_id=1, source_target_pairs={{0,2},{1,3},{2,0},{3,1},{4,6},{5,7},{6,4},{7,5},{8,10},{9,11},{10,... | collective-permute-start | bytes 491528 | tf_op jit(solution)/shard_map/ppermute | solution.py:411
  28.0 11.2 %collective-permute-start.9 = (bf16[320,256]{1,0:T(8,128)(2,1)S(1)}, bf16[320,256]{1,0:T(8,128)(2,1)S(1)}, u32[]{:S(2)}, u32[]{:S(2)}) collective-permute-start(bf16[320,256]{1,0:T(8,128)(2,1)S(1)} %slice.12), channel_id=1, source_target_pairs={{0,4},{1,5},{2,6},{3,7},{4,0},{5,1},{6,2},{7,3},{8,12},{9,13},{10,... | collective-permute-start | bytes 491528 | tf_op jit(solution)/shard_map/ppermute | solution.py:411
  39.3 3.9 %collective-permute-start.11 = (bf16[640,256]{1,0:T(8,128)(2,1)S(1)}, bf16[640,256]{1,0:T(8,128)(2,1)S(1)}, u32[]{:S(2)}, u32[]{:S(2)}) collective-permute-start(bf16[640,256]{1,0:T(8,128)(2,1)S(1)} %collective-permute-done.7.refs_5_), channel_id=1, source_target_pairs={{0,1},{1,0},{2,3},{3,2},{4,5},{5,4},{6,7},{7,6},{8,9},{9,8},{10,11... | collective-permute-start | bytes 983048 | tf_op jit(solution)/shard_map/ppermute | solution.py:411
  39.3 3.8 %collective-permute-start.12 = (bf16[640,256]{1,0:T(8,128)(2,1)S(1)}, bf16[640,256]{1,0:T(8,128)(2,1)S(1)}, u32[]{:S(2)}, u32[]{:S(2)}) collective-permute-start(bf16[640,256]{1,0:T(8,128)(2,1)S(1)} %collective-permute-done.8.refs_6_), channel_id=1, source_target_pairs={{0,1},{1,0},{2,3},{3,2},{4,5},{5,4},{6,7},{7,6},{8,9},{9,8},{10,11... | collective-permute-start | bytes 983048 | tf_op jit(solution)/shard_map/ppermute | solution.py:411
  39.8 1.8 %collective-permute-start.13 = (bf16[320,256]{1,0:T(8,128)(2,1)S(1)}, bf16[320,256]{1,0:T(8,128)(2,1)S(1)}, u32[]{:S(2)}, u32[]{:S(2)}) collective-permute-start(bf16[320,256]{1,0:T(8,128)(2,1)S(1)} %collective-permute-done.9.refs_7_), channel_id=1, source_target_pairs={{0,1},{1,0},{2,3},{3,2},{4,5},{5,4},{6,7},{7,6},{8,9},{9,8},{10,11... | collective-permute-start | bytes 491528 | tf_op jit(solution)/shard_map/ppermute | solution.py:411
  39.9 3.3 %collective-permute-start.14 = (bf16[320,256]{1,0:T(8,128)(2,1)S(1)}, bf16[320,256]{1,0:T(8,128)(2,1)S(1)}, u32[]{:S(2)}, u32[]{:S(2)}) collective-permute-start(bf16[320,256]{1,0:T(8,128)(2,1)S(1)} %collective-permute-done.10.refs_8_), channel_id=1, source_target_pairs={{0,1},{1,0},{2,3},{3,2},{4,5},{5,4},{6,7},{7,6},{8,9},{9,8},{10,11... | collective-permute-start | bytes 491528 | tf_op jit(solution)/shard_map/ppermute | solution.py:411
  40.4 9.5 %collective-permute-start.15 = (bf16[320,256]{1,0:T(8,128)(2,1)S(1)}, bf16[320,256]{1,0:T(8,128)(2,1)S(1)}, u32[]{:S(2)}, u32[]{:S(2)}) collective-permute-start(bf16[320,256]{1,0:T(8,128)(2,1)S(1)} %slice.14), channel_id=1, source_target_pairs={{0,4},{1,5},{2,6},{3,7},{4,0},{5,1},{6,2},{7,3},{8,12},{9,13},{10,... | collective-permute-start | bytes 491528 | tf_op jit(solution)/shard_map/ppermute | solution.py:411
  41.7 8.3 %collective-permute-start.16 = (bf16[320,256]{1,0:T(8,128)(2,1)S(1)}, bf16[320,256]{1,0:T(8,128)(2,1)S(1)}, u32[]{:S(2)}, u32[]{:S(2)}) collective-permute-start(bf16[320,256]{1,0:T(8,128)(2,1)S(1)} %slice.15), channel_id=1, source_target_pairs={{0,2},{1,3},{2,0},{3,1},{4,6},{5,7},{6,4},{7,5},{8,10},{9,11},{10,... | collective-permute-start | bytes 491528 | tf_op jit(solution)/shard_map/ppermute | solution.py:411
  43.2 8.5 %copy-start.3 = (bf16[16,32,256]{2,1,0:T(8,128)(2,1)S(1)}, bf16[16,32,256]{2,1,0:T(8,128)(2,1)}, u32[]{:S(2)}) copy-start(bf16[16,32,256]{2,1,0:T(8,128)(2,1)} %refs_9_.1) | copy-start | bytes 786436
  43.2 8.4 %copy-start.4 = (f32[16,32]{1,0:T(8,128)S(1)}, f32[16,32]{1,0:T(8,128)}, u32[]{:S(2)}) copy-start(f32[16,32]{1,0:T(8,128)} %refs_10_.1) | copy-start | bytes 6148
  49.9 1.5 %collective-permute-start.17 = (bf16[320,256]{1,0:T(8,128)(2,1)S(1)}, bf16[320,256]{1,0:T(8,128)(2,1)S(1)}, u32[]{:S(2)}, u32[]{:S(2)}) collective-permute-start(bf16[320,256]{1,0:T(8,128)(2,1)S(1)} %collective-permute-done.15.refs_5_), channel_id=1, source_target_pairs={{0,1},{1,0},{2,3},{3,2},{4,5},{5,4},{6,7},{7,6},{8,9},{9,8},{10,11... | collective-permute-start | bytes 491528 | tf_op jit(solution)/shard_map/ppermute | solution.py:411
  50.0 1.6 %collective-permute-start.18 = (bf16[320,256]{1,0:T(8,128)(2,1)S(1)}, bf16[320,256]{1,0:T(8,128)(2,1)S(1)}, u32[]{:S(2)}, u32[]{:S(2)}) collective-permute-start(bf16[320,256]{1,0:T(8,128)(2,1)S(1)} %collective-permute-done.16.refs_6_), channel_id=1, source_target_pairs={{0,1},{1,0},{2,3},{3,2},{4,5},{5,4},{6,7},{7,6},{8,9},{9,8},{10,11... | collective-permute-start | bytes 491528 | tf_op jit(solution)/shard_map/ppermute | solution.py:411

commit v4 on v3

--- a/solution.py
+++ b/solution.py
@@ -94,7 +94,7 @@
 
 
 def prepare_kernel(
-    rows, block_ref, basis_ref, scales_ref, points_ref, skeleton_ref, ids_ref, message_ref
+    rows, block_ref, basis_ref, scales_ref, points_ref, skeleton_ref, ids_ref, message_ref, *half_refs
 ):
     clusters, rank, size = basis_ref.shape
     vecs = block_ref.shape[1]
@@ -131,81 +131,89 @@
     )
     lines.append(jnp.zeros((rows["end"] - rows["ids"] - ids.shape[0], size), jnp.float32))
     message_ref[rows["skeleton"] :, :] = jnp.concatenate(lines, axis=0).astype(jnp.bfloat16)
+    for place, half_ref in enumerate(half_refs):
+        count = half_ref.shape[0]
+        half_ref[...] = message_ref[place * count : (place + 1) * count, :]
 
 
 def axes_of(values, start, count):
     return [values[start + k * count : start + (k + 1) * count] for k in range(3)]
 
 
-def local_kernel(
-    rows, message_ref, far_ref, block_ref, prior_ref, beta_ref,
-    total_ref, early_ref, left_ref, far_left_ref, counts_ref
-):
+def local_kernel(rows, targets, *refs):
+    messages, far_refs, refs = refs[:targets], refs[targets : 2 * targets], refs[2 * targets :]
+    (
+        block_ref, prior_ref, beta_ref,
+        total_ref, far_ref, early_ref, left_ref, far_left_ref, counts_ref, ids_ref,
+    ) = refs
     clusters, vecs, size = block_ref.shape
-    blocks = counts_ref.shape[0]
-    halves = far_left_ref.shape[0]
+    blocks = counts_ref.shape[0] // targets
+    halves = far_left_ref.shape[0] // targets
     per_row = clusters // halves
-    tail = message_ref[rows["points"] :, :].astype(jnp.float32)
-    axes = axes_of(tail, 0, clusters)
-    left = left_rows(axes)
-    right = right_rows(axes).astype(jnp.bfloat16)
-    for cluster in range(clusters):
-        left_ref[cluster] = left[cluster].T.astype(jnp.bfloat16)
-    left_ref[clusters] = jnp.zeros_like(left_ref[clusters])
-    far_left = left_rows(axes_of(tail, rows["skeleton"] - rows["points"], halves))
-    for half in range(halves):
-        far_left_ref[half] = far_left[half].T.astype(jnp.bfloat16)
+    rank = size // per_row
+    lanes = lax.broadcasted_iota(jnp.int32, (clusters, blocks * per_row), 1)
+    row_ids = lax.broadcasted_iota(jnp.int32, (per_row, size), 0)
+    widen = lax.div(lax.broadcasted_iota(jnp.int32, (per_row, size), 1), rank) == row_ids
+    widen = widen.astype(jnp.bfloat16)
+    for target in range(targets):
+        tail = messages[target][rows["points"] :, :].astype(jnp.float32)
+        axes = axes_of(tail, 0, clusters)
+        left = left_rows(axes)
+        for cluster in range(clusters):
+            left_ref[target * clusters + cluster] = left[cluster].T.astype(jnp.bfloat16)
+        if target == 0:
+            right = right_rows(axes).astype(jnp.bfloat16)
+        far_left = left_rows(axes_of(tail, rows["skeleton"] - rows["points"], halves))
+        for half in range(halves):
+            far_left_ref[target * halves + half] = far_left[half].T.astype(jnp.bfloat16)
+        ids = tail[rows["ids"] - rows["points"] : rows["ids"] - rows["points"] + 8]
+        ids_ref[target] = ids[:, : ids_ref.shape[2]].astype(jnp.int32)
+
+        far_ids = far_refs[target][...]
+        listed = jnp.zeros(lanes.shape, jnp.float32)
+        for place in range(far_ids.shape[1]):
+            listed += (far_ids[:, place : place + 1] == lanes).astype(jnp.float32)
+        listed = listed.astype(jnp.bfloat16)
+        for block in range(blocks):
+            counts_ref[target * blocks + block] = jnp.dot(
+                listed[:, block * per_row : (block + 1) * per_row], widen,
+                preferred_element_type=jnp.float32,
+            )
 
     beta = beta_ref[...]
     sums = jnp.zeros((vecs, 2 * vecs), jnp.float32)
     for cluster in range(clusters):
         tile = tile_of(left_ref[cluster], right[cluster])
-        term = dot_nt(message_ref[cluster * vecs : (cluster + 1) * vecs, :], tile)
+        term = dot_nt(messages[0][cluster * vecs : (cluster + 1) * vecs, :], tile)
         shift = dot_exact(beta, prior_ref[cluster])
         total_ref[cluster] = term - shift
         block = block_ref[cluster]
         sums += dot_split(block, jnp.concatenate([block, shift], axis=0))
-    total_ref[clusters] = jnp.zeros_like(total_ref[clusters])
     early_ref[...] = sums
-
-    far_ids = far_ref[...]
-    lanes = lax.broadcasted_iota(jnp.int32, (clusters, blocks * per_row), 1)
-    listed = jnp.zeros(lanes.shape, jnp.float32)
-    for place in range(far_ref.shape[1]):
-        listed += (far_ids[:, place : place + 1] == lanes).astype(jnp.float32)
-    listed = listed.astype(jnp.bfloat16)
-    rank = size // per_row
-    rows_of = lax.broadcasted_iota(jnp.int32, (per_row, size), 0)
-    widen = (lax.div(lax.broadcasted_iota(jnp.int32, (per_row, size), 1), rank) == rows_of)
-    widen = widen.astype(jnp.bfloat16)
-    for block in range(blocks):
-        counts_ref[block] = jnp.dot(
-            listed[:, block * per_row : (block + 1) * per_row], widen,
-            preferred_element_type=jnp.float32,
-        )
-
-
-def add_kernel(rows, owner_of, pieces, last, asked_ref, *refs):
-    total_in, far_in, left_ref, far_left_ref, counts_ref = refs[:5]
+    total_ref[clusters:] = jnp.zeros((total_ref.shape[0] - clusters, vecs, size), jnp.float32)
+    far_ref[...] = jnp.zeros_like(far_ref)
+
+
+def add_kernel(rows, owner_of, target_of, pieces, last, *refs):
+    total_in, far_in, left_ref, far_left_ref, counts_ref, own_ids_ref = refs[:6]
     count = sum(pieces)
-    messages, refs = refs[5 : 5 + count], refs[5 + count :]
-    if last:
-        basis_ref, scales_ref, early_ref, block_ref, stacked_ref, products_ref = refs[:6]
-        refs = refs[6:]
-    else:
-        total_out, far_out = refs[:2]
-        refs = refs[2:]
+    messages, refs = refs[6 : 6 + count], refs[6 + count :]
+    outputs, refs = refs[: 3 if last else 2], refs[3 if last else 2 :]
     (
         total_ref, far_ref, vectors_ref, sources_ref, right_ref, far_right_ref, ids_ref,
         ids_scalar_ref, source_ref, own_ref, mirror_ref, copied,
     ) = refs
     devices = len(pieces)
-    clusters = left_ref.shape[0] - 1
+    targets = own_ids_ref.shape[0]
+    clusters = left_ref.shape[0] // targets
     size = left_ref.shape[1]
-    halves, vecs, _ = far_ref.shape
+    sides = far_ref.shape[0]
+    halves = sides // targets
+    vecs = far_ref.shape[1]
     per_row = clusters // halves
     rank = size // per_row
-    slots = asked_ref.shape[1]
+    slots = rows["slots"]
+    blocks = counts_ref.shape[0] // targets
     me = lax.axis_index("clus")
     owners = [owner_of(me, device) for device in range(devices)]
 
@@ -231,10 +239,12 @@
         far_right_ref[device * halves : (device + 1) * halves] = right.astype(jnp.bfloat16)
         ids = tail[rows["ids"] - rows["points"] : rows["ids"] - rows["points"] + 8]
         ids_ref[device] = ids[:, : ids_ref.shape[2]].astype(jnp.int32)
+    for target in range(targets):
+        ids_ref[devices + target] = own_ids_ref[target]
     copy = pltpu.make_async_copy(ids_ref, ids_scalar_ref, copied)
     copy.start()
 
-    pair = devices // 2 if devices % 2 == 0 else 1
+    pair = 2 if devices % 2 == 0 else 1
 
     def far_step(turn, carry):
         terms = []
@@ -246,10 +256,11 @@
             for block in range(halves):
                 features = far_right_ref[device * halves + block]
                 sources = sources_ref[device * halves + block]
-                for side in range(halves):
+                for side in range(sides):
                     tile = values_of(far_left_ref[side], features)
-                    weights = counts_ref[owner * halves + block]
-                    weights = weights[side * per_row : (side + 1) * per_row]
+                    weights = counts_ref[(side // halves) * blocks + owner * halves + block]
+                    first = (side % halves) * per_row
+                    weights = weights[first : first + per_row]
                     tile = tile.reshape(per_row, rank, size) * weights[:, None, :]
                     tile = tile.reshape(per_row * rank, size).astype(jnp.bfloat16)
                     terms.append((side, dot_nt(sources, tile)))
@@ -262,25 +273,29 @@
     copy.wait()
     live = jnp.int32(0)
     for device in range(devices):
-        for slot in range(slots):
-            asked = asked_ref[0, slot, 0, owners[device]], asked_ref[0, slot, 1, owners[device]]
-            told = ids_scalar_ref[device, 2 * slot, me], ids_scalar_ref[device, 2 * slot + 1, me]
-            for row, source, own, mirror in (
-                (asked[0], asked[1], asked[0], 0), (told[0], told[0], told[1], 1),
-            ):
-                source_ref[live] = device * clusters + source
-                own_ref[live] = own
-                mirror_ref[live] = mirror
-                live = live + (row >= 0).astype(jnp.int32)
+        for target in range(targets):
+            asker = target_of(me, target)
+            base = target * clusters
+            for slot in range(slots):
+                row, partner = 2 * slot, 2 * slot + 1
+                asked = [ids_scalar_ref[devices + target, k, owners[device]] for k in (row, partner)]
+                told = [ids_scalar_ref[device, k, asker] for k in (row, partner)]
+                for alive, source, own, mirror in (
+                    (asked[0], asked[1], asked[0], 0), (told[0], told[0], told[1], 1),
+                ):
+                    source_ref[live] = device * clusters + source
+                    own_ref[live] = base + own
+                    mirror_ref[live] = mirror
+                    live = live + (alive >= 0).astype(jnp.int32)
     for extra in range(unroll):
         source_ref[live + extra] = 0
-        own_ref[live + extra] = clusters
+        own_ref[live + extra] = targets * clusters
         mirror_ref[live + extra] = 0
 
     def entry(place):
         source = source_ref[place]
         own = own_ref[place]
-        tile = tile_of(left_ref[own], right_ref[source])
+        tile = tile_of(left_ref[jnp.minimum(own, targets * clusters - 1)], right_ref[source])
         term = dot_nt(vectors_ref[source], tile)
         rounded = term.astype(jnp.bfloat16).astype(jnp.float32)
         return own, jnp.where(mirror_ref[place] > 0, rounded, term)
@@ -312,10 +327,23 @@
         near_step(done, few)
 
     if not last:
-        total_out[...] = total_ref[...]
-        far_out[...] = far_ref[...]
+        outputs[0][...] = total_ref[...]
+        outputs[1][...] = far_ref[...]
         return
-
+    outputs[0][...] = total_ref[:clusters]
+    outputs[1][...] = far_ref[:halves]
+    outputs[2][:clusters] = total_ref[(targets - 1) * clusters : targets * clusters]
+    outputs[2][clusters:] = far_ref[(targets - 1) * halves :]
+
+
+def combine_kernel(
+    given, total_ref, far_ref, given_ref, basis_ref, scales_ref, early_ref, block_ref,
+    stacked_ref, products_ref
+):
+    clusters, vecs, size = total_ref.shape
+    halves = far_ref.shape[0]
+    per_row = clusters // halves
+    rank = size // per_row
     sums = jnp.zeros((2 * vecs, vecs), jnp.float32)
     place_ids = lax.broadcasted_iota(jnp.int32, (per_row, vecs, size), 0)
     lane_ids = lax.broadcasted_iota(jnp.int32, (per_row, vecs, size), 2)
@@ -323,13 +351,18 @@
     for side in range(halves):
         scales = scales_ref[side * per_row : (side + 1) * per_row, :]
         scales = jnp.concatenate([scales[place : place + 1] for place in range(per_row)], axis=1)
-        lifted = jnp.where(own_lanes, (far_ref[side] * scales)[None], 0.0)
+        gathered = far_ref[side]
+        if given:
+            gathered = gathered + given_ref[clusters + side]
+        lifted = jnp.where(own_lanes, (gathered * scales)[None], 0.0)
         lifted = lifted.reshape(per_row * vecs, size).astype(jnp.bfloat16)
         basis = basis_ref[side * per_row : (side + 1) * per_row].reshape(per_row * rank, size)
         terms = jnp.dot(lifted, basis, preferred_element_type=jnp.float32)
         for place in range(per_row):
             cluster = side * per_row + place
             shifted = total_ref[cluster] + terms[place * vecs : (place + 1) * vecs]
+            if given:
+                shifted = shifted + given_ref[cluster]
             stacked = jnp.concatenate([block_ref[cluster], shifted], axis=0)
             stacked_ref[cluster] = stacked
             sums += dot_split(stacked, shifted)
@@ -405,11 +438,12 @@
     )(*operands)
 
 
-def spread(message, parts):
-    def passed(values, step):
-        pairs = [(index, index ^ step) for index in range(parts)]
-        return lax.ppermute(values, "clus", pairs)
-
+def passed(values, parts, step):
+    pairs = [(index, index ^ step) for index in range(parts)]
+    return lax.ppermute(values, "clus", pairs)
+
+
+def spread(message, halved, parts):
     def group_of(steps, pieces):
         def owner_of(me, place):
             return me ^ steps[place]
@@ -426,38 +460,35 @@
                 [[everything[first + place]] for place in range(count)],
             )
         return
-    core, along, inner, over = 1, 2, 4, 12
-    cut = message.shape[0] // 2
-    fetched = [passed(message, step) for step in (over, inner, along)]
-    sibling = passed(message, core)
+    along, inner, over = 2, 4, 12
+
+    def held(values, token):
+        return lax.optimization_barrier((values, token))[0]
+
+    def fetched(values, step):
+        return passed(values, parts, step)
+
+    head, tail = (fetched(half, over) for half in halved)
+    inward, sideways = fetched(message, inner), fetched(message, along)
     token = yield
-    sibling, _ = lax.optimization_barrier((sibling, token))
-    token = yield group_of([0, core], [[message], [sibling]])
-    fetched, _ = lax.optimization_barrier((fetched, token))
-    mirrored, inward, sideways = fetched
-    fetched = [
-        passed(mirrored, inner), passed(mirrored, along),
-        passed(sideways[:cut], inner), passed(inward[cut:], along),
-    ]
+    head, sideways = held((head, sideways), token)
+    inner_head, side_head = fetched(head, inner), fetched(head, along)
+    token = yield group_of([0], [[message]])
+    tail, inward, side_head = held((tail, inward, side_head), token)
+    side_tail, inner_tail = fetched(tail, along), fetched(tail, inner)
+    last_head = fetched(side_head, inner)
+    diagonal = fetched(inward, along)
+    token = yield group_of([over, inner, along], [[head, tail], [inward], [sideways]])
+    side_tail, diagonal, inner_head, inner_tail, last_head = held(
+        (side_tail, diagonal, inner_head, inner_tail, last_head), token
+    )
+    last_tail = fetched(side_tail, inner)
     token = yield group_of(
-        [over, inner, along, over ^ core, inner ^ core, along ^ core],
-        [[mirrored], [inward], [sideways]]
-        + [[passed(piece, core)] for piece in (mirrored, inward, sideways)],
-    )
-    fetched, _ = lax.optimization_barrier((fetched, token))
-    mirrored_inward, mirrored_sideways, *diagonal = fetched
-    fetched = [
-        passed(mirrored_sideways[:cut], inner), passed(mirrored_inward[cut:], along),
-    ]
-    steps = [over ^ inner, over ^ along, inner ^ along]
-    pieces = [[mirrored_inward], [mirrored_sideways], diagonal]
-    token = yield group_of(
-        steps + [step ^ core for step in steps],
-        pieces + [[passed(part, core) for part in piece] for piece in pieces],
-    )
-    fetched, _ = lax.optimization_barrier((fetched, token))
-    last = over ^ inner ^ along
-    yield group_of([last, last ^ core], [fetched, [passed(part, core) for part in fetched]])
+        [inner ^ along, over ^ inner, over ^ along],
+        [[diagonal], [inner_head, inner_tail], [side_head, side_tail]],
+    )
+    last_tail = held(last_tail, token)
+    yield group_of([over ^ inner ^ along], [[last_head, last_tail]])
 
 
 def local(
@@ -469,74 +500,94 @@
     slots = near_pairs.shape[2]
     total_points = parts * clusters * size
     halves = clusters * rank // size
-    rows = layout_of(clusters, vecs, rank, size)
+    rows = dict(layout_of(clusters, vecs, rank, size), slots=slots)
+    core = 1
+    shared = parts == 16
+    targets = 2 if shared else 1
     wide = functools.partial(jax.ShapeDtypeStruct, dtype=jnp.float32)
     narrow = functools.partial(jax.ShapeDtypeStruct, dtype=jnp.bfloat16)
 
     asked = near_pairs.transpose(0, 2, 3, 1)
-    (message,) = call(
+    message, *halved = call(
         functools.partial(prepare_kernel, rows),
-        [narrow((rows["end"], size))],
+        [narrow((rows["end"], size))] + [narrow((rows["end"] // 2, size))] * (2 if shared else 0),
         (
             block_vectors, basis, scales, points.transpose(1, 0, 2), skeleton.transpose(1, 0, 2),
             asked,
         ),
         vmem=56 << 20,
     )
-    groups = spread(message, parts)
+    groups = spread(message, halved, parts)
     next(groups)
-    total, early, left, far_left, counts = call(
-        functools.partial(local_kernel, rows),
-        [
-            wide((clusters + 1, vecs, size)),
+    own, lists = [message], [far_ids]
+    if shared:
+        own.append(passed(message, parts, core))
+        lists.append(passed(far_ids, parts, core))
+    lanes = -(-parts // 128) * 128
+    blocks = parts * halves
+    state = [wide((targets * clusters + 1, vecs, size)), wide((targets * halves, vecs, size))]
+    total, far, early, left, far_left, counts, ids = call(
+        functools.partial(local_kernel, rows, targets),
+        state
+        + [
             wide((vecs, 2 * vecs)),
-            narrow((clusters + 1, size, feature_count)),
-            narrow((halves, size, feature_count)),
-            wide((parts * halves, clusters, size)),
+            narrow((targets * clusters, size, feature_count)),
+            narrow((targets * halves, size, feature_count)),
+            wide((targets * blocks, clusters, size)),
+            jax.ShapeDtypeStruct((targets, 8, lanes), jnp.int32),
         ],
-        (message, far_ids, block_vectors, prior_vectors, prior_beta),
+        (*own, *lists, block_vectors, prior_vectors, prior_beta),
         flops=1 << 31,
     )
-    far = jnp.zeros((halves, vecs, size), jnp.float32)
-    lanes = -(-parts // 128) * 128
-    token, seen = early, 0
-    while seen < parts:
+
+    def target_of(me, target):
+        return me ^ (core * target)
+
+    token, seen, sources = early, 0, parts // targets
+    while seen < sources:
         owner_of, messages = groups.send(token)
         seen += len(messages)
-        last = seen == parts
+        last = seen == sources
         devices = len(messages)
-        entries = 2 * slots * devices + unroll
+        entries = 2 * slots * devices * targets + unroll
         pieces = [piece for message_pieces in messages for piece in message_pieces]
-        operands = [asked, total, far, left, far_left, counts] + pieces
-        out_shape = [wide((clusters + 1, vecs, size)), wide((halves, vecs, size))]
+        out_shape = state
         if last:
-            operands += [basis, scales, early, block_vectors]
-            out_shape = [wide((clusters, 2 * vecs, size)), wide((parts, vecs, 4 * vecs))]
-        total, far = call(
+            out_shape = [wide((clusters, vecs, size)), wide((halves, vecs, size))]
+            out_shape.append(wide((clusters + halves, vecs, size)))
+        total, far, *given = call(
             functools.partial(
-                add_kernel, rows, owner_of, [len(message_pieces) for message_pieces in messages], last
+                add_kernel, rows, owner_of, target_of,
+                [len(message_pieces) for message_pieces in messages], last,
             ),
             out_shape,
-            operands,
+            [total, far, left, far_left, counts, ids] + pieces,
             scratch=[
-                pltpu.VMEM((clusters + 1, vecs, size), jnp.float32),
-                pltpu.VMEM((halves, vecs, size), jnp.float32),
+                pltpu.VMEM((targets * clusters + 1, vecs, size), jnp.float32),
+                pltpu.VMEM((targets * halves, vecs, size), jnp.float32),
                 pltpu.VMEM((devices * clusters, vecs, size), jnp.bfloat16),
                 pltpu.VMEM((devices * halves, vecs, size), jnp.bfloat16),
                 pltpu.VMEM((devices * clusters, feature_count, size), jnp.bfloat16),
                 pltpu.VMEM((devices * halves, feature_count, size), jnp.bfloat16),
-                pltpu.VMEM((devices, 8, lanes), jnp.int32),
-                pltpu.SMEM((devices, 8, lanes), jnp.int32),
+                pltpu.VMEM((devices + targets, 8, lanes), jnp.int32),
+                pltpu.SMEM((devices + targets, 8, lanes), jnp.int32),
                 pltpu.SMEM((entries,), jnp.int32),
                 pltpu.SMEM((entries,), jnp.int32),
                 pltpu.SMEM((entries,), jnp.int32),
                 pltpu.SemaphoreType.DMA,
             ],
-            smem=1,
             flops=devices << 28,
         )
         token = far
-    stacked, products = total, far
+    given = given[0]
+    if shared:
+        given = passed(given, parts, core)
+    stacked, products = call(
+        functools.partial(combine_kernel, shared),
+        [wide((clusters, 2 * vecs, size)), wide((parts, vecs, 4 * vecs))],
+        (total, far, given, basis, scales, early, block_vectors),
+        flops=1 << 28,
+    )
     summed = lax.all_to_all(products, "clus", split_axis=0, concat_axis=0, tiled=True)
     return tuple(
         call(

time: 72.5 us -> 70 us (0.966)
  Pallas kernels: 30 us -> 24.5 us
  local copies, waits for them, and re-layouts: 1.08 us -> 4.48 us
  blocking collectives: 12.6 us -> 14.5 us
  starting transfers between devices: 14.9 us -> 13.3 us
  waiting for transfers between devices: 12.8 us -> 11.8 us
    pallas_call x7 -> x8, Pallas kernels: 30 us -> 24.5 us  [call(): pl.pallas_call(kernel, out_shape=out_shape, in_specs=specs(len(operands),...]
    unnamed x18, local copies, waits for them, and re-layouts: 1.02 us -> 4.48 us
    all_to_all x1, blocking collectives: 12.6 us -> 14.5 us  [local(): lax.all_to_all(products, 'clus', split_axis=0, concat_axis=0, tiled=True)]
    ppermute x19 -> x14, starting transfers between devices: 14.9 us -> 13.3 us  [passed(): return lax.ppermute(values, 'clus', pairs)]
    ppermute x19 -> x14, waiting for transfers between devices: 12.8 us -> 11.8 us  [passed(): return lax.ppermute(values, 'clus', pairs)]
  transfers between devices with their start and end apart: 19 -> 14, of which waited for: 5 -> 7; matrix products, arithmetic and copies ran while one was open for 0% -> 0% of each run, Pallas kernels for 27% -> 21%
where the time goes in v4:
time: 70 us; the launch traced here: 69.3 us
  Pallas kernels  24.5 us (35%)
  blocking collectives  14.5 us (21%)
  starting transfers between devices  13.3 us (19%)
  waiting for transfers between devices  11.8 us (17%)
  local copies, waits for them, and re-layouts  4.48 us (6%)
  between operations  0.73 us (1%)
    pallas_call x8, Pallas kernels, call(): pl.pallas_call(kernel, out_shape=out_shape, in_specs=specs(len(operands),...  24.5 us
    all_to_all x1, blocking collectives, local(): lax.all_to_all(products, 'clus', split_axis=0, concat_axis=0, tiled=True)  14.5 us
    ppermute x14, starting transfers between devices, passed(): return lax.ppermute(values, 'clus', pairs)  13.3 us
    ppermute x14, waiting for transfers between devices, passed(): return lax.ppermute(values, 'clus', pairs)  11.8 us
    unnamed x18, local copies, waits for them, and re-layouts  4.48 us
  transfers between devices with their start and end apart: 14, of which 7 were waited for; matrix products, arithmetic and copies ran while one was open for 0% of the time, Pallas kernels for 21%

profile of v4, /device:TPU:0, one launch (start us, length us, event | category | flops | bytes accessed | tf_op | source)
XLA Modules:
  0.0 69.3 jit_solution(16513886532435463967)
XLA Ops:
  0.6 2.2 %shard_map.112 = (bf16[640,256]{1,0:T(8,128)(2,1)}, bf16[320,256]{1,0:T(8,128)(2,1)}, bf16[320,256]{1,0:T(8,128)(2,1)}) custom-call(f32[16,32,256]{2,1,0:T(8,128)} %block_ref.3, bf16[16,32,256]{2,1,0:T(8,128)(2,1)} %basis_ref.3, f32[16,32]{1,0:T(8,128)} %scales_ref.3, bf16[3,16,256]{2,1,0:T(8,128)(2,1)} %bitcast.3, bf16[3,16,32]{2,1,0:T(8,128)(2,1)} %bitcast.4, ...), custom_call_target="tpu_custom_call" | custom-call | bytes 1048576 | tf_op jit(solution)/shard_map/pallas_call | solution.py:428
  2.8 0.5 collective-permute-start
  3.3 2.5 %collective-permute-start.3 = (bf16[640,256]{1,0:T(8,128)(2,1)}, bf16[640,256]{1,0:T(8,128)(2,1)S(1)}, u32[]{:S(2)}, u32[]{:S(2)}) collective-permute-start(bf16[640,256]{1,0:T(8,128)(2,1)} %get-tuple-element.35.refs_0_.refs_6_), channel_id=1, source_target_pairs={{0,2},{1,3},{2,0},{3,1},{4,6},{5,7},{6,4},{7,5},{8,10},{9,11},{10,... | collective-permute-start | bytes 983048 | tf_op jit(solution)/shard_map/ppermute | solution.py:443
  5.8 0.2 collective-permute-start.1
  6.0 1.6 %collective-permute-start.5 = (bf16[640,256]{1,0:T(8,128)(2,1)}, bf16[640,256]{1,0:T(8,128)(2,1)S(1)}, u32[]{:S(2)}, u32[]{:S(2)}) collective-permute-start(bf16[640,256]{1,0:T(8,128)(2,1)} %get-tuple-element.35.refs_0_.refs_6_), channel_id=1, source_target_pairs={{0,4},{1,5},{2,6},{3,7},{4,0},{5,1},{6,2},{7,3},{8,12},{9,13},{10,... | collective-permute-start | bytes 983048 | tf_op jit(solution)/shard_map/ppermute | solution.py:443
  7.6 2.5 %collective-permute-start.2 = (bf16[320,256]{1,0:T(8,128)(2,1)}, bf16[320,256]{1,0:T(8,128)(2,1)S(1)}, u32[]{:S(2)}, u32[]{:S(2)}) collective-permute-start(bf16[320,256]{1,0:T(8,128)(2,1)} %get-tuple-element.44), channel_id=1, source_target_pairs={{0,12},{1,13},{2,14},{3,15},{4,8},{5,9},{6,10},{7,11},{8,4},{9,5},... | collective-permute-start | bytes 491528 | tf_op jit(solution)/shard_map/ppermute | solution.py:443
  10.1 1.3 %collective-permute-start.4 = (bf16[320,256]{1,0:T(8,128)(2,1)}, bf16[320,256]{1,0:T(8,128)(2,1)S(1)}, u32[]{:S(2)}, u32[]{:S(2)}) collective-permute-start(bf16[320,256]{1,0:T(8,128)(2,1)} %get-tuple-element.47), channel_id=1, source_target_pairs={{0,12},{1,13},{2,14},{3,15},{4,8},{5,9},{6,10},{7,11},{8,4},{9,5},... | collective-permute-start | bytes 491528 | tf_op jit(solution)/shard_map/ppermute | solution.py:443
  11.4 1.0 %copy-done = f32[16,32,256]{2,1,0:T(8,128)S(1)} copy-done((f32[16,32,256]{2,1,0:T(8,128)S(1)}, f32[16,32,256]{2,1,0:T(8,128)}, u32[]{:S(2)}) %copy-start) | copy-done | bytes 524312
  12.5 1.0 %copy-done.4 = f32[16,32,256]{2,1,0:T(8,128)S(1)} copy-done((f32[16,32,256]{2,1,0:T(8,128)S(1)}, f32[16,32,256]{2,1,0:T(8,128)}, u32[]{:S(2)}) %copy-start.4) | copy-done | bytes 524312
  13.5 1.0 %copy-done.5 = bf16[640,256]{1,0:T(8,128)(2,1)S(1)} copy-done((bf16[640,256]{1,0:T(8,128)(2,1)S(1)}, bf16[640,256]{1,0:T(8,128)(2,1)}, u32[]{:S(2)}) %copy-start.5) | copy-done | bytes 327704
  14.5 0.7 %copy-done.7 = f32[32,32]{1,0:T(8,128)S(1)} copy-done((f32[32,32]{1,0:T(8,128)S(1)}, f32[32,32]{1,0:T(8,128)}, u32[]{:S(2)}) %copy-start.7) | copy-done | bytes 4120
  15.2 0.7 %copy-done.8 = s32[16,64]{1,0:T(8,128)S(1)} copy-done((s32[16,64]{1,0:T(8,128)S(1)}, s32[16,64]{1,0:T(8,128)}, u32[]{:S(2)}) %copy-start.8) | copy-done | bytes 4120
  15.9 3.2 %shard_map.113 = (f32[33,32,256]{2,1,0:T(8,128)S(1)}, f32[4,32,256]{2,1,0:T(8,128)S(1)}, f32[32,64]{1,0:T(8,128)S(1)}, bf16[32,256,16]{2,1,0:T(8,128)(2,1)S(1)},...) custom-call(bf16[640,256]{1,0:T(8,128)(2,1)S(1)} %copy-done.5, ...), custom_call_target="tpu_custom_call" | custom-call | flops 2147483648 | bytes 1048576 | tf_op jit(solution)/shard_map/pallas_call | solution.py:428
  19.1 3.3 %collective-permute-done.2.refs_6_ = bf16[320,256]{1,0:T(8,128)(2,1)S(1)} collective-permute-done((bf16[320,256]{1,0:T(8,128)(2,1)}, bf16[320,256]{1,0:T(8,128)(2,1)S(1)}, u32[]{:S(2)}, u32[]{:S(2)}) %collective-permute-start.2) | collective-permute-done | bytes 163872 | tf_op jit(solution)/shard_map/ppermute | solution.py:443
  22.4 0.5 collective-permute-start.6
  22.9 1.8 %shard_map.114 = (f32[33,32,256]{2,1,0:T(8,128)S(1)}, f32[4,32,256]{2,1,0:T(8,128)S(1)}) custom-call(f32[33,32,256]{2,1,0:T(8,128)S(1)} %get-tuple-element.36.refs_0_, f32[4,32,256]{2,1,0:T(8,128)S(1)} %get-tuple-element.37.refs_1_, bf16[32,256,16]{2,1,0:T(8,128)(2,1)S(1)} %get-tuple-element.38.refs_2_, bf16[4,256,16]{2,1,0:T(8,128)(2,1)S(1)} %get-tuple-element.39.refs_3_, ...), custom_call_target="tpu_custom_call" | custom-call | flops 268435456 | bytes 1048576 | tf_op jit(solution)/shard_map/pallas_call | solution.py:428
  24.7 0.5 collective-permute-done.4.refs_7_
  25.3 2.4 %collective-permute-done.6.refs_9_ = bf16[320,256]{1,0:T(8,128)(2,1)S(1)} collective-permute-done((bf16[320,256]{1,0:T(8,128)(2,1)S(1)}, bf16[320,256]{1,0:T(8,128)(2,1)S(1)}, u32[]{:S(2)}, u32[]{:S(2)}) %collective-permute-start.6) | collective-permute-done | bytes 163872 | tf_op jit(solution)/shard_map/ppermute | solution.py:443
  27.7 0.5 collective-permute-start.8
  28.3 2.0 %collective-permute-start.10 = (bf16[320,256]{1,0:T(8,128)(2,1)S(1)}, bf16[320,256]{1,0:T(8,128)(2,1)S(1)}, u32[]{:S(2)}, u32[]{:S(2)}) collective-permute-start(bf16[320,256]{1,0:T(8,128)(2,1)S(1)} %collective-permute-done.4.refs_7_), channel_id=1, source_target_pairs={{0,4},{1,5},{2,6},{3,7},{4,0},{5,1},{6,2},{7,3},{8,12},{9,13},{10,... | collective-permute-start | bytes 491528 | tf_op jit(solution)/shard_map/ppermute | solution.py:443
  30.3 1.5 %collective-permute-start.7 = (bf16[320,256]{1,0:T(8,128)(2,1)S(1)}, bf16[320,256]{1,0:T(8,128)(2,1)S(1)}, u32[]{:S(2)}, u32[]{:S(2)}) collective-permute-start(bf16[320,256]{1,0:T(8,128)(2,1)S(1)} %collective-permute-done.4.refs_7_), channel_id=1, source_target_pairs={{0,2},{1,3},{2,0},{3,1},{4,6},{5,7},{6,4},{7,5},{8,10},{9,11},{10,... | collective-permute-start | bytes 491528 | tf_op jit(solution)/shard_map/ppermute | solution.py:443
  31.8 4.9 %shard_map.115 = (f32[33,32,256]{2,1,0:T(8,128)S(1)}, f32[4,32,256]{2,1,0:T(8,128)S(1)}) custom-call(f32[33,32,256]{2,1,0:T(8,128)S(1)} %get-tuple-element.42.refs_0_, f32[4,32,256]{2,1,0:T(8,128)S(1)} %get-tuple-element.43.refs_1_, bf16[32,256,16]{2,1,0:T(8,128)(2,1)S(1)} %get-tuple-element.38.refs_2_, bf16[4,256,16]{2,1,0:T(8,128)(2,1)S(1)} %get-tuple-element.39.refs_3_, ...), custom_call_target="tpu_custom_call" | custom-call | flops 805306368 | bytes 1048576 | tf_op jit(solution)/shard_map/pallas_call | solution.py:428
  36.7 0.6 collective-permute-done.10.refs_8_
  37.3 2.3 %collective-permute-done.11.refs_6_ = bf16[320,256]{1,0:T(8,128)(2,1)S(1)} collective-permute-done((bf16[320,256]{1,0:T(8,128)(2,1)S(1)}, bf16[320,256]{1,0:T(8,128)(2,1)S(1)}, u32[]{:S(2)}, u32[]{:S(2)}) %collective-permute-start.11) | collective-permute-done | bytes 163872 | tf_op jit(solution)/shard_map/ppermute | solution.py:443
  39.7 4.7 %shard_map.116 = (f32[33,32,256]{2,1,0:T(8,128)S(1)}, f32[4,32,256]{2,1,0:T(8,128)S(1)}) custom-call(f32[33,32,256]{2,1,0:T(8,128)S(1)} %get-tuple-element.51.refs_0_, f32[4,32,256]{2,1,0:T(8,128)S(1)} %get-tuple-element.52.refs_1_, bf16[32,256,16]{2,1,0:T(8,128)(2,1)S(1)} %get-tuple-element.38.refs_2_, bf16[4,256,16]{2,1,0:T(8,128)(2,1)S(1)} %get-tuple-element.39.refs_3_, ...), custom_call_target="tpu_custom_call" | custom-call | flops 805306368 | bytes 1048576 | tf_op jit(solution)/shard_map/pallas_call | solution.py:428
  44.4 0.6 collective-permute-done.12.refs_7_
  45.0 2.6 %shard_map.117 = (f32[16,32,256]{2,1,0:T(8,128)S(1)}, f32[2,32,256]{2,1,0:T(8,128)S(1)}, f32[18,32,256]{2,1,0:T(8,128)S(1)}) custom-call(f32[33,32,256]{2,1,0:T(8,128)S(1)} %get-tuple-element.58.refs_0_, f32[4,32,256]{2,1,0:T(8,128)S(1)} %get-tuple-element.59.refs_1_, bf16[32,256,16]{2,1,0:T(8,128)(2,1)S(1)} %get-tuple-element.38.refs_2_, ...), custom_call_target="tpu_custom_call" | custom-call | flops 268435456 | bytes 1048576 | tf_op jit(solution)/shard_map/pallas_call | solution.py:428
  47.6 0.1 collective-permute-start.13
  47.7 2.0 %collective-permute-done.13.given_ref = f32[18,32,256]{2,1,0:T(8,128)S(1)} collective-permute-done((f32[18,32,256]{2,1,0:T(8,128)S(1)}, f32[18,32,256]{2,1,0:T(8,128)S(1)}, u32[]{:S(2)}, u32[]{:S(2)}) %collective-permute-start.13) | collective-permute-done | bytes 589856 | tf_op jit(solution)/shard_map/ppermute | solution.py:443
  49.7 1.3 %shard_map.118 = (f32[16,64,256]{2,1,0:T(8,128)S(1)}, f32[16,32,128]{2,1,0:T(8,128)S(1)}) custom-call(f32[16,32,256]{2,1,0:T(8,128)S(1)} %get-tuple-element.62.total_ref, f32[2,32,256]{2,1,0:T(8,128)S(1)} %get-tuple-element.63.far_ref, f32[18,32,256]{2,1,0:T(8,128)S(1)} %collective-permute-done.13.given_ref, bf16[16,32,256]{2,1,0:T(8,128)(2,1)S(1)} %copy-done.2, ...), custom_call_target="tpu_custom_call" | custom-call | flops 268435456 | bytes 1048576 | tf_op jit(solution)/shard_map/pallas_call | solution.py:428
  50.9 14.5 %all_to_all.5.products_ref = f32[16,32,128]{2,1,0:T(8,128)S(1)} all-to-all(f32[16,32,128]{2,1,0:T(8,128)S(1)} %get-tuple-element.65), channel_id=1, replica_groups=mesh['group'=2,'clus'=16] {'clus'}, dimensions={0} | all-to-all | bytes 524288 | tf_op jit(solution)/shard_map/all_to_all | solution.py:591
  65.4 3.9 %shard_map.119 = (f32[16,32,256]{2,1,0:T(8,128)}, f32[32,32]{1,0:T(8,128)}, f32[32,32]{1,0:T(8,128)}) custom-call(f32[16,32,128]{2,1,0:T(8,128)S(1)} %all_to_all.5.products_ref, f32[16,64,256]{2,1,0:T(8,128)S(1)} %get-tuple-element.66.stacked_ref), custom_call_target="tpu_custom_call" | custom-call | bytes 1048576 | tf_op jit(solution)/shard_map/pallas_call | solution.py:428
  (23 shorter events, 0.1 us)
Async XLA Ops:
  2.8 8.6 %collective-permute-start = (bf16[640,256]{1,0:T(8,128)(2,1)}, bf16[640,256]{1,0:T(8,128)(2,1)S(1)}, u32[]{:S(2)}, u32[]{:S(2)}) collective-permute-start(bf16[640,256]{1,0:T(8,128)(2,1)} %get-tuple-element.35.refs_0_.refs_6_), channel_id=1, source_target_pairs={{0,1},{1,0},{2,3},{3,2},{4,5},{5,4},{6,7},{7,6},{8,9},{9,8},{10,11... | collective-permute-start | bytes 983048 | tf_op jit(solution)/shard_map/ppermute | solution.py:443
  3.3 19.1 %collective-permute-start.3 = (bf16[640,256]{1,0:T(8,128)(2,1)}, bf16[640,256]{1,0:T(8,128)(2,1)S(1)}, u32[]{:S(2)}, u32[]{:S(2)}) collective-permute-start(bf16[640,256]{1,0:T(8,128)(2,1)} %get-tuple-element.35.refs_0_.refs_6_), channel_id=1, source_target_pairs={{0,2},{1,3},{2,0},{3,1},{4,6},{5,7},{6,4},{7,5},{8,10},{9,11},{10,... | collective-permute-start | bytes 983048 | tf_op jit(solution)/shard_map/ppermute | solution.py:443
  5.8 4.3 %collective-permute-start.1 = (s32[16,64]{1,0:T(8,128)}, s32[16,64]{1,0:T(8,128)S(1)}, u32[]{:S(2)}, u32[]{:S(2)}) collective-permute-start(s32[16,64]{1,0:T(8,128)} %refs_2_.1), channel_id=1, source_target_pairs={{0,1},{1,0},{2,3},{3,2},{4,5},{5,4},{6,7},{7,6},{8,9},{9,8},{10,11... | collective-permute-start | bytes 12296 | tf_op jit(solution)/shard_map/ppermute | solution.py:443
  6.0 19.3 %collective-permute-start.5 = (bf16[640,256]{1,0:T(8,128)(2,1)}, bf16[640,256]{1,0:T(8,128)(2,1)S(1)}, u32[]{:S(2)}, u32[]{:S(2)}) collective-permute-start(bf16[640,256]{1,0:T(8,128)(2,1)} %get-tuple-element.35.refs_0_.refs_6_), channel_id=1, source_target_pairs={{0,4},{1,5},{2,6},{3,7},{4,0},{5,1},{6,2},{7,3},{8,12},{9,13},{10,... | collective-permute-start | bytes 983048 | tf_op jit(solution)/shard_map/ppermute | solution.py:443
  7.6 14.8 %collective-permute-start.2 = (bf16[320,256]{1,0:T(8,128)(2,1)}, bf16[320,256]{1,0:T(8,128)(2,1)S(1)}, u32[]{:S(2)}, u32[]{:S(2)}) collective-permute-start(bf16[320,256]{1,0:T(8,128)(2,1)} %get-tuple-element.44), channel_id=1, source_target_pairs={{0,12},{1,13},{2,14},{3,15},{4,8},{5,9},{6,10},{7,11},{8,4},{9,5},... | collective-permute-start | bytes 491528 | tf_op jit(solution)/shard_map/ppermute | solution.py:443
  10.1 15.2 %collective-permute-start.4 = (bf16[320,256]{1,0:T(8,128)(2,1)}, bf16[320,256]{1,0:T(8,128)(2,1)S(1)}, u32[]{:S(2)}, u32[]{:S(2)}) collective-permute-start(bf16[320,256]{1,0:T(8,128)(2,1)} %get-tuple-element.47), channel_id=1, source_target_pairs={{0,12},{1,13},{2,14},{3,15},{4,8},{5,9},{6,10},{7,11},{8,4},{9,5},... | collective-permute-start | bytes 491528 | tf_op jit(solution)/shard_map/ppermute | solution.py:443
  11.4 1.0 %copy-start = (f32[16,32,256]{2,1,0:T(8,128)S(1)}, f32[16,32,256]{2,1,0:T(8,128)}, u32[]{:S(2)}) copy-start(f32[16,32,256]{2,1,0:T(8,128)} %block_ref.3) | copy-start | bytes 1572868
  12.5 1.0 %copy-start.4 = (f32[16,32,256]{2,1,0:T(8,128)S(1)}, f32[16,32,256]{2,1,0:T(8,128)}, u32[]{:S(2)}) copy-start(f32[16,32,256]{2,1,0:T(8,128)} %refs_5_.1) | copy-start | bytes 1572868
  13.5 1.0 %copy-start.5 = (bf16[640,256]{1,0:T(8,128)(2,1)S(1)}, bf16[640,256]{1,0:T(8,128)(2,1)}, u32[]{:S(2)}) copy-start(bf16[640,256]{1,0:T(8,128)(2,1)} %get-tuple-element.35.refs_0_.refs_6_) | copy-start | bytes 983044
  14.5 0.7 %copy-start.7 = (f32[32,32]{1,0:T(8,128)S(1)}, f32[32,32]{1,0:T(8,128)}, u32[]{:S(2)}) copy-start(f32[32,32]{1,0:T(8,128)} %refs_6_.1) | copy-start | bytes 12292
  15.2 0.7 %copy-start.8 = (s32[16,64]{1,0:T(8,128)S(1)}, s32[16,64]{1,0:T(8,128)}, u32[]{:S(2)}) copy-start(s32[16,64]{1,0:T(8,128)} %refs_2_.1) | copy-start | bytes 12292
  15.9 7.0 %copy-start.6 = (bf16[640,256]{1,0:T(8,128)(2,1)S(1)}, bf16[640,256]{1,0:T(8,128)(2,1)}, u32[]{:S(2)}) copy-start(bf16[640,256]{1,0:T(8,128)(2,1)} %get-tuple-element.35.refs_0_.refs_6_) | copy-start | bytes 983044
  22.4 5.3 %collective-permute-start.6 = (bf16[320,256]{1,0:T(8,128)(2,1)S(1)}, bf16[320,256]{1,0:T(8,128)(2,1)S(1)}, u32[]{:S(2)}, u32[]{:S(2)}) collective-permute-start(bf16[320,256]{1,0:T(8,128)(2,1)S(1)} %collective-permute-done.2.refs_6_), channel_id=1, source_target_pairs={{0,2},{1,3},{2,0},{3,1},{4,6},{5,7},{6,4},{7,5},{8,10},{9,11},{10,... | collective-permute-start | bytes 491528 | tf_op jit(solution)/shard_map/ppermute | solution.py:443
  27.7 11.9 %collective-permute-start.8 = (bf16[640,256]{1,0:T(8,128)(2,1)S(1)}, bf16[640,256]{1,0:T(8,128)(2,1)S(1)}, u32[]{:S(2)}, u32[]{:S(2)}) collective-permute-start(bf16[640,256]{1,0:T(8,128)(2,1)S(1)} %collective-permute-done.5.refs_8_), channel_id=1, source_target_pairs={{0,2},{1,3},{2,0},{3,1},{4,6},{5,7},{6,4},{7,5},{8,10},{9,11},{10,... | collective-permute-start | bytes 983048 | tf_op jit(solution)/shard_map/ppermute | solution.py:443
  28.3 8.5 %collective-permute-start.9 = (bf16[320,256]{1,0:T(8,128)(2,1)S(1)}, bf16[320,256]{1,0:T(8,128)(2,1)S(1)}, u32[]{:S(2)}, u32[]{:S(2)}) collective-permute-start(bf16[320,256]{1,0:T(8,128)(2,1)S(1)} %collective-permute-done.2.refs_6_), channel_id=1, source_target_pairs={{0,4},{1,5},{2,6},{3,7},{4,0},{5,1},{6,2},{7,3},{8,12},{9,13},{10,... | collective-permute-start | bytes 491528 | tf_op jit(solution)/shard_map/ppermute | solution.py:443
  28.3 9.0 %collective-permute-start.10 = (bf16[320,256]{1,0:T(8,128)(2,1)S(1)}, bf16[320,256]{1,0:T(8,128)(2,1)S(1)}, u32[]{:S(2)}, u32[]{:S(2)}) collective-permute-start(bf16[320,256]{1,0:T(8,128)(2,1)S(1)} %collective-permute-done.4.refs_7_), channel_id=1, source_target_pairs={{0,4},{1,5},{2,6},{3,7},{4,0},{5,1},{6,2},{7,3},{8,12},{9,13},{10,... | collective-permute-start | bytes 491528 | tf_op jit(solution)/shard_map/ppermute | solution.py:443
  30.3 9.3 %collective-permute-start.11 = (bf16[320,256]{1,0:T(8,128)(2,1)S(1)}, bf16[320,256]{1,0:T(8,128)(2,1)S(1)}, u32[]{:S(2)}, u32[]{:S(2)}) collective-permute-start(bf16[320,256]{1,0:T(8,128)(2,1)S(1)} %collective-permute-done.6.refs_9_), channel_id=1, source_target_pairs={{0,4},{1,5},{2,6},{3,7},{4,0},{5,1},{6,2},{7,3},{8,12},{9,13},{10,... | collective-permute-start | bytes 491528 | tf_op jit(solution)/shard_map/ppermute | solution.py:443
  30.3 9.3 %collective-permute-start.7 = (bf16[320,256]{1,0:T(8,128)(2,1)S(1)}, bf16[320,256]{1,0:T(8,128)(2,1)S(1)}, u32[]{:S(2)}, u32[]{:S(2)}) collective-permute-start(bf16[320,256]{1,0:T(8,128)(2,1)S(1)} %collective-permute-done.4.refs_7_), channel_id=1, source_target_pairs={{0,2},{1,3},{2,0},{3,1},{4,6},{5,7},{6,4},{7,5},{8,10},{9,11},{10,... | collective-permute-start | bytes 491528 | tf_op jit(solution)/shard_map/ppermute | solution.py:443
  39.6 5.3 %collective-permute-start.12 = (bf16[320,256]{1,0:T(8,128)(2,1)S(1)}, bf16[320,256]{1,0:T(8,128)(2,1)S(1)}, u32[]{:S(2)}, u32[]{:S(2)}) collective-permute-start(bf16[320,256]{1,0:T(8,128)(2,1)S(1)} %collective-permute-done.7.refs_10_), channel_id=1, source_target_pairs={{0,4},{1,5},{2,6},{3,7},{4,0},{5,1},{6,2},{7,3},{8,12},{9,13},{10,... | collective-permute-start | bytes 491528 | tf_op jit(solution)/shard_map/ppermute | solution.py:443
  45.0 4.7 %copy-start.1 = (f32[16,32,256]{2,1,0:T(8,128)S(1)}, f32[16,32,256]{2,1,0:T(8,128)}, u32[]{:S(2)}) copy-start(f32[16,32,256]{2,1,0:T(8,128)} %block_ref.3) | copy-start | bytes 1572868
  45.0 4.7 %copy-start.2 = (bf16[16,32,256]{2,1,0:T(8,128)(2,1)S(1)}, bf16[16,32,256]{2,1,0:T(8,128)(2,1)}, u32[]{:S(2)}) copy-start(bf16[16,32,256]{2,1,0:T(8,128)(2,1)} %basis_ref.3) | copy-start | bytes 786436
  45.0 4.7 %copy-start.3 = (f32[16,32]{1,0:T(8,128)S(1)}, f32[16,32]{1,0:T(8,128)}, u32[]{:S(2)}) copy-start(f32[16,32]{1,0:T(8,128)} %scales_ref.3) | copy-start | bytes 6148
  47.6 2.1 %collective-permute-start.13 = (f32[18,32,256]{2,1,0:T(8,128)S(1)}, f32[18,32,256]{2,1,0:T(8,128)S(1)}, u32[]{:S(2)}, u32[]{:S(2)}) collective-permute-start(f32[18,32,256]{2,1,0:T(8,128)S(1)} %get-tuple-element.64), channel_id=1, source_target_pairs={{0,1},{1,0},{2,3},{3,2},{4,5},{5,4},{6,7},{7,6},{8,9},{9,8},{10,11... | collective-permute-start | bytes 1769480 | tf_op jit(solution)/shard_map/ppermute | solution.py:443

commit v5 on v4

--- a/solution.py
+++ b/solution.py
@@ -194,11 +194,11 @@
     far_ref[...] = jnp.zeros_like(far_ref)
 
 
-def add_kernel(rows, owner_of, target_of, pieces, last, *refs):
+def add_kernel(rows, owner_of, target_of, pieces, chosen, given, *refs):
     total_in, far_in, left_ref, far_left_ref, counts_ref, own_ids_ref = refs[:6]
     count = sum(pieces)
     messages, refs = refs[6 : 6 + count], refs[6 + count :]
-    outputs, refs = refs[: 3 if last else 2], refs[3 if last else 2 :]
+    outputs, refs = refs[: 1 if given else 2], refs[1 if given else 2 :]
     (
         total_ref, far_ref, vectors_ref, sources_ref, right_ref, far_right_ref, ids_ref,
         ids_scalar_ref, source_ref, own_ref, mirror_ref, copied,
@@ -217,8 +217,11 @@
     me = lax.axis_index("clus")
     owners = [owner_of(me, device) for device in range(devices)]
 
-    total_ref[...] = total_in[...]
+    for target in chosen:
+        base = target * clusters
+        total_ref[base : base + clusters] = total_in[base : base + clusters]
     far_ref[...] = far_in[...]
+    total_ref[targets * clusters] = jnp.zeros((vecs, size), jnp.float32)
     start = 0
     for device, number in enumerate(pieces):
         first = 0
@@ -239,11 +242,12 @@
         far_right_ref[device * halves : (device + 1) * halves] = right.astype(jnp.bfloat16)
         ids = tail[rows["ids"] - rows["points"] : rows["ids"] - rows["points"] + 8]
         ids_ref[device] = ids[:, : ids_ref.shape[2]].astype(jnp.int32)
-    for target in range(targets):
+    for target in chosen:
         ids_ref[devices + target] = own_ids_ref[target]
     copy = pltpu.make_async_copy(ids_ref, ids_scalar_ref, copied)
     copy.start()
 
+    chosen_sides = [target * halves + half for target in chosen for half in range(halves)]
     pair = 2 if devices % 2 == 0 else 1
 
     def far_step(turn, carry):
@@ -256,7 +260,7 @@
             for block in range(halves):
                 features = far_right_ref[device * halves + block]
                 sources = sources_ref[device * halves + block]
-                for side in range(sides):
+                for side in chosen_sides:
                     tile = values_of(far_left_ref[side], features)
                     weights = counts_ref[(side // halves) * blocks + owner * halves + block]
                     first = (side % halves) * per_row
@@ -273,7 +277,7 @@
     copy.wait()
     live = jnp.int32(0)
     for device in range(devices):
-        for target in range(targets):
+        for target in chosen:
             asker = target_of(me, target)
             base = target * clusters
             for slot in range(slots):
@@ -326,14 +330,14 @@
     def _():
         near_step(done, few)
 
-    if not last:
-        outputs[0][...] = total_ref[...]
-        outputs[1][...] = far_ref[...]
+    first, upto = chosen[0], chosen[-1] + 1
+    if given:
+        outputs[0][:clusters] = total_ref[first * clusters : upto * clusters]
+        outputs[0][clusters:] = far_ref[first * halves : upto * halves]
         return
-    outputs[0][...] = total_ref[:clusters]
-    outputs[1][...] = far_ref[:halves]
-    outputs[2][:clusters] = total_ref[(targets - 1) * clusters : targets * clusters]
-    outputs[2][clusters:] = far_ref[(targets - 1) * halves :]
+    rest = outputs[0].shape[0] - (upto - first) * clusters
+    outputs[0][...] = total_ref[first * clusters : upto * clusters + rest]
+    outputs[1][...] = far_ref[first * halves : upto * halves]
 
 
 def combine_kernel(
@@ -420,16 +424,13 @@
         next_ref[cluster] = dot_exact(joint, stacked_ref[cluster])
 
 
-def call(kernel, out_shape, operands, scratch=(), smem=0, smem_out=0, flops=0, vmem=20 << 20):
-    def specs(total, scalars):
-        places = [pltpu.SMEM] * scalars + [pltpu.VMEM] * (total - scalars)
-        return [pl.BlockSpec(memory_space=place) for place in places]
-
+def call(kernel, out_shape, operands, scratch=(), flops=0, vmem=20 << 20):
+    held = pl.BlockSpec(memory_space=pltpu.VMEM)
     return pl.pallas_call(
         kernel,
         out_shape=out_shape,
-        in_specs=specs(len(operands), smem),
-        out_specs=specs(len(out_shape), smem_out),
+        in_specs=[held] * len(operands),
+        out_specs=[held] * len(out_shape),
         scratch_shapes=list(scratch),
         compiler_params=pltpu.CompilerParams(vmem_limit_bytes=vmem),
         cost_estimate=pl.CostEstimate(
@@ -468,27 +469,23 @@
     def fetched(values, step):
         return passed(values, parts, step)
 
-    head, tail = (fetched(half, over) for half in halved)
-    inward, sideways = fetched(message, inner), fetched(message, along)
-    token = yield
-    head, sideways = held((head, sideways), token)
-    inner_head, side_head = fetched(head, inner), fetched(head, along)
+    cut = message.shape[0] // 2
+    sideways, inward, mirrored = (fetched(message, step) for step in (along, inner, over))
+    yield
     token = yield group_of([0], [[message]])
-    tail, inward, side_head = held((tail, inward, side_head), token)
-    side_tail, inner_tail = fetched(tail, along), fetched(tail, inner)
-    last_head = fetched(side_head, inner)
-    diagonal = fetched(inward, along)
-    token = yield group_of([over, inner, along], [[head, tail], [inward], [sideways]])
-    side_tail, diagonal, inner_head, inner_tail, last_head = held(
-        (side_tail, diagonal, inner_head, inner_tail, last_head), token
-    )
-    last_tail = fetched(side_tail, inner)
+    mirrored, inward, sideways = held((mirrored, inward, sideways), token)
+    diagonal = [fetched(sideways[:cut], inner), fetched(inward[cut:], along)]
+    mirrored_inward = fetched(mirrored, inner)
+    mirrored_sideways = fetched(mirrored, along)
+    token = yield group_of([over, inner, along], [[mirrored], [inward], [sideways]])
+    mirrored_inward, mirrored_sideways = held((mirrored_inward, mirrored_sideways), token)
+    last = [fetched(mirrored_sideways[:cut], inner), fetched(mirrored_inward[cut:], along)]
     token = yield group_of(
         [inner ^ along, over ^ inner, over ^ along],
-        [[diagonal], [inner_head, inner_tail], [side_head, side_tail]],
-    )
-    last_tail = held(last_tail, token)
-    yield group_of([over ^ inner ^ along], [[last_head, last_tail]])
+        [diagonal, [mirrored_inward], [mirrored_sideways]],
+    )
+    last = held(last, token)
+    yield group_of([over ^ inner ^ along], [last])
 
 
 def local(
@@ -551,37 +548,42 @@
         devices = len(messages)
         entries = 2 * slots * devices * targets + unroll
         pieces = [piece for message_pieces in messages for piece in message_pieces]
-        out_shape = state
-        if last:
-            out_shape = [wide((clusters, vecs, size)), wide((halves, vecs, size))]
-            out_shape.append(wide((clusters + halves, vecs, size)))
-        total, far, *given = call(
-            functools.partial(
-                add_kernel, rows, owner_of, target_of,
-                [len(message_pieces) for message_pieces in messages], last,
-            ),
-            out_shape,
-            [total, far, left, far_left, counts, ids] + pieces,
-            scratch=[
-                pltpu.VMEM((targets * clusters + 1, vecs, size), jnp.float32),
-                pltpu.VMEM((targets * halves, vecs, size), jnp.float32),
-                pltpu.VMEM((devices * clusters, vecs, size), jnp.bfloat16),
-                pltpu.VMEM((devices * halves, vecs, size), jnp.bfloat16),
-                pltpu.VMEM((devices * clusters, feature_count, size), jnp.bfloat16),
-                pltpu.VMEM((devices * halves, feature_count, size), jnp.bfloat16),
-                pltpu.VMEM((devices + targets, 8, lanes), jnp.int32),
-                pltpu.SMEM((devices + targets, 8, lanes), jnp.int32),
-                pltpu.SMEM((entries,), jnp.int32),
-                pltpu.SMEM((entries,), jnp.int32),
-                pltpu.SMEM((entries,), jnp.int32),
-                pltpu.SemaphoreType.DMA,
-            ],
-            flops=devices << 28,
-        )
-        token = far
-    given = given[0]
+
+
+        def add(total, chosen, out_shape, given=False):
+            return call(
+                functools.partial(
+                    add_kernel, rows, owner_of, target_of,
+                    [len(message_pieces) for message_pieces in messages], chosen, given,
+                ),
+                out_shape,
+                [total, far, left, far_left, counts, ids] + pieces,
+                scratch=[
+                    pltpu.VMEM((targets * clusters + 1, vecs, size), jnp.float32),
+                    pltpu.VMEM((targets * halves, vecs, size), jnp.float32),
+                    pltpu.VMEM((devices * clusters, vecs, size), jnp.bfloat16),
+                    pltpu.VMEM((devices * halves, vecs, size), jnp.bfloat16),
+                    pltpu.VMEM((devices * clusters, feature_count, size), jnp.bfloat16),
+                    pltpu.VMEM((devices * halves, feature_count, size), jnp.bfloat16),
+                    pltpu.VMEM((devices + targets, 8, lanes), jnp.int32),
+                    pltpu.SMEM((devices + targets, 8, lanes), jnp.int32),
+                    pltpu.SMEM((entries,), jnp.int32),
+                    pltpu.SMEM((entries,), jnp.int32),
+                    pltpu.SMEM((entries,), jnp.int32),
+                    pltpu.SemaphoreType.DMA,
+                ],
+                flops=devices << 28,
+            )
+
+        if not last:
+            total, far = add(total, tuple(range(targets)), state)
+            token = far
+    given = far
     if shared:
+        (given,) = add(total, (1,), [wide((clusters + halves, vecs, size))], True)
+        total, given = lax.optimization_barrier((total, given))
         given = passed(given, parts, core)
+    total, far = add(total, (0,), [wide((clusters, vecs, size)), wide((halves, vecs, size))])
     stacked, products = call(
         functools.partial(combine_kernel, shared),
         [wide((clusters, 2 * vecs, size)), wide((parts, vecs, 4 * vecs))],

time: 70 us -> 68 us (0.971)
  Pallas kernels: 24.5 us -> 29.5 us
  waiting for transfers between devices: 11.8 us -> 7.3 us
  blocking collectives: 14.5 us -> 12.9 us
    pallas_call x8 -> x9, Pallas kernels: 24.5 us -> 29.5 us  [call(): pl.pallas_call(kernel, out_shape=out_shape, in_specs=[held] * len(operand...]
    ppermute x14 -> x12, waiting for transfers between devices: 11.8 us -> 7.3 us  [passed(): return lax.ppermute(values, 'clus', pairs)]
    all_to_all x1, blocking collectives: 14.5 us -> 12.9 us  [local(): lax.all_to_all(products, 'clus', split_axis=0, concat_axis=0, tiled=True)]
    ppermute x14 -> x12, starting transfers between devices: 13.3 us -> 12.8 us  [passed(): return lax.ppermute(values, 'clus', pairs)]
  transfers between devices with their start and end apart: 14 -> 12, of which waited for: 7 -> 6; matrix products, arithmetic and copies ran while one was open for 0% -> 0% of each run, Pallas kernels for 21% -> 30%
where the time goes in v5:
time: 68 us; the launch traced here: 67.8 us
  Pallas kernels  29.5 us (43%)
  blocking collectives  12.9 us (19%)
  starting transfers between devices  12.8 us (19%)
  waiting for transfers between devices  7.3 us (11%)
  local copies, waits for them, and re-layouts  4.54 us (7%)
  between operations  0.78 us (1%)
    pallas_call x9, Pallas kernels, call(): pl.pallas_call(kernel, out_shape=out_shape, in_specs=[held] * len(operand...  29.5 us
    all_to_all x1, blocking collectives, local(): lax.all_to_all(products, 'clus', split_axis=0, concat_axis=0, tiled=True)  12.9 us
    ppermute x12, starting transfers between devices, passed(): return lax.ppermute(values, 'clus', pairs)  12.8 us
    ppermute x12, waiting for transfers between devices, passed(): return lax.ppermute(values, 'clus', pairs)  7.3 us
    unnamed x18, local copies, waits for them, and re-layouts  4.49 us
  transfers between devices with their start and end apart: 12, of which 6 were waited for; matrix products, arithmetic and copies ran while one was open for 0% of the time, Pallas kernels for 30%

profile of v5, /device:TPU:0, one launch (start us, length us, event | category | flops | bytes accessed | tf_op | source)
XLA Modules:
  0.0 67.8 jit_solution(13279817280000121868)
XLA Ops:
  0.6 2.2 %shard_map.112 = (bf16[640,256]{1,0:T(8,128)(2,1)}, bf16[320,256]{1,0:T(8,128)(2,1)}, bf16[320,256]{1,0:T(8,128)(2,1)}) custom-call(f32[16,32,256]{2,1,0:T(8,128)} %block_ref.3, bf16[16,32,256]{2,1,0:T(8,128)(2,1)} %basis_ref.3, f32[16,32]{1,0:T(8,128)} %scales_ref.3, bf16[3,16,256]{2,1,0:T(8,128)(2,1)} %bitcast.3, bf16[3,16,32]{2,1,0:T(8,128)(2,1)} %bitcast.4, ...), custom_call_target="tpu_custom_call" | custom-call | bytes 1048576 | tf_op jit(solution)/shard_map/pallas_call | solution.py:429
  2.8 0.5 collective-permute-start
  3.3 4.6 %collective-permute-start.2 = (bf16[640,256]{1,0:T(8,128)(2,1)}, bf16[640,256]{1,0:T(8,128)(2,1)S(1)}, u32[]{:S(2)}, u32[]{:S(2)}) collective-permute-start(bf16[640,256]{1,0:T(8,128)(2,1)} %get-tuple-element.30.refs_0_.refs_6_), channel_id=1, source_target_pairs={{0,12},{1,13},{2,14},{3,15},{4,8},{5,9},{6,10},{7,11},{8,4},{9,5},... | collective-permute-start | bytes 983048 | tf_op jit(solution)/shard_map/ppermute | solution.py:444
  7.9 1.5 %collective-permute-start.4 = (bf16[640,256]{1,0:T(8,128)(2,1)}, bf16[640,256]{1,0:T(8,128)(2,1)S(1)}, u32[]{:S(2)}, u32[]{:S(2)}) collective-permute-start(bf16[640,256]{1,0:T(8,128)(2,1)} %get-tuple-element.30.refs_0_.refs_6_), channel_id=1, source_target_pairs={{0,2},{1,3},{2,0},{3,1},{4,6},{5,7},{6,4},{7,5},{8,10},{9,11},{10,... | collective-permute-start | bytes 983048 | tf_op jit(solution)/shard_map/ppermute | solution.py:444
  9.4 1.4 %collective-permute-done.1.refs_3_ = s32[16,64]{1,0:T(8,128)S(1)} collective-permute-done((s32[16,64]{1,0:T(8,128)}, s32[16,64]{1,0:T(8,128)S(1)}, u32[]{:S(2)}, u32[]{:S(2)}) %collective-permute-start.1) | collective-permute-done | bytes 4128 | tf_op jit(solution)/shard_map/ppermute | solution.py:444
  10.8 1.0 %copy-done = f32[16,32,256]{2,1,0:T(8,128)S(1)} copy-done((f32[16,32,256]{2,1,0:T(8,128)S(1)}, f32[16,32,256]{2,1,0:T(8,128)}, u32[]{:S(2)}) %copy-start) | copy-done | bytes 524312
  11.8 1.0 %copy-done.4 = f32[16,32,256]{2,1,0:T(8,128)S(1)} copy-done((f32[16,32,256]{2,1,0:T(8,128)S(1)}, f32[16,32,256]{2,1,0:T(8,128)}, u32[]{:S(2)}) %copy-start.4) | copy-done | bytes 524312
  12.9 1.0 %copy-done.5 = bf16[640,256]{1,0:T(8,128)(2,1)S(1)} copy-done((bf16[640,256]{1,0:T(8,128)(2,1)S(1)}, bf16[640,256]{1,0:T(8,128)(2,1)}, u32[]{:S(2)}) %copy-start.5) | copy-done | bytes 327704
  13.9 0.7 %copy-done.7 = f32[32,32]{1,0:T(8,128)S(1)} copy-done((f32[32,32]{1,0:T(8,128)S(1)}, f32[32,32]{1,0:T(8,128)}, u32[]{:S(2)}) %copy-start.7) | copy-done | bytes 4120
  14.6 0.7 %copy-done.8 = s32[16,64]{1,0:T(8,128)S(1)} copy-done((s32[16,64]{1,0:T(8,128)S(1)}, s32[16,64]{1,0:T(8,128)}, u32[]{:S(2)}) %copy-start.8) | copy-done | bytes 4120
  15.3 3.2 %shard_map.113 = (f32[33,32,256]{2,1,0:T(8,128)S(1)}, f32[4,32,256]{2,1,0:T(8,128)S(1)}, f32[32,64]{1,0:T(8,128)S(1)}, bf16[32,256,16]{2,1,0:T(8,128)(2,1)S(1)},...) custom-call(bf16[640,256]{1,0:T(8,128)(2,1)S(1)} %copy-done.5, ...), custom_call_target="tpu_custom_call" | custom-call | flops 2147483648 | bytes 1048576 | tf_op jit(solution)/shard_map/pallas_call | solution.py:429
  18.4 3.2 %shard_map.114 = (f32[33,32,256]{2,1,0:T(8,128)S(1)}, f32[4,32,256]{2,1,0:T(8,128)S(1)}) custom-call(f32[33,32,256]{2,1,0:T(8,128)S(1)} %get-tuple-element.31.refs_0_, f32[4,32,256]{2,1,0:T(8,128)S(1)} %get-tuple-element.32.refs_1_, bf16[32,256,16]{2,1,0:T(8,128)(2,1)S(1)} %get-tuple-element.33.refs_2_, bf16[4,256,16]{2,1,0:T(8,128)(2,1)S(1)} %get-tuple-element.34.refs_3_, ...), custom_call_target="tpu_custom_call" | custom-call | flops 268435456 | bytes 1048576 | tf_op jit(solution)/shard_map/pallas_call | solution.py:429
  21.6 2.0 %collective-permute-done.3.refs_7_ = bf16[640,256]{1,0:T(8,128)(2,1)S(1)} collective-permute-done((bf16[640,256]{1,0:T(8,128)(2,1)}, bf16[640,256]{1,0:T(8,128)(2,1)S(1)}, u32[]{:S(2)}, u32[]{:S(2)}) %collective-permute-start.3) | collective-permute-done | bytes 327712 | tf_op jit(solution)/shard_map/ppermute | solution.py:444
  23.6 1.7 %collective-permute-start.7 = (bf16[640,256]{1,0:T(8,128)(2,1)S(1)}, bf16[640,256]{1,0:T(8,128)(2,1)S(1)}, u32[]{:S(2)}, u32[]{:S(2)}) collective-permute-start(bf16[640,256]{1,0:T(8,128)(2,1)S(1)} %collective-permute-done.2.refs_6_), channel_id=1, source_target_pairs={{0,4},{1,5},{2,6},{3,7},{4,0},{5,1},{6,2},{7,3},{8,12},{9,13},{10,... | collective-permute-start | bytes 983048 | tf_op jit(solution)/shard_map/ppermute | solution.py:444
  25.3 1.5 %collective-permute-start.8 = (bf16[640,256]{1,0:T(8,128)(2,1)S(1)}, bf16[640,256]{1,0:T(8,128)(2,1)S(1)}, u32[]{:S(2)}, u32[]{:S(2)}) collective-permute-start(bf16[640,256]{1,0:T(8,128)(2,1)S(1)} %collective-permute-done.2.refs_6_), channel_id=1, source_target_pairs={{0,2},{1,3},{2,0},{3,1},{4,6},{5,7},{6,4},{7,5},{8,10},{9,11},{10,... | collective-permute-start | bytes 983048 | tf_op jit(solution)/shard_map/ppermute | solution.py:444
  26.8 0.4 collective-permute-start.5
  27.2 0.6 collective-permute-start.6
  27.8 5.8 %shard_map.115 = (f32[33,32,256]{2,1,0:T(8,128)S(1)}, f32[4,32,256]{2,1,0:T(8,128)S(1)}) custom-call(f32[33,32,256]{2,1,0:T(8,128)S(1)} %get-tuple-element.37.refs_0_, f32[4,32,256]{2,1,0:T(8,128)S(1)} %get-tuple-element.38.refs_1_, bf16[32,256,16]{2,1,0:T(8,128)(2,1)S(1)} %get-tuple-element.33.refs_2_, bf16[4,256,16]{2,1,0:T(8,128)(2,1)S(1)} %get-tuple-element.34.refs_3_, ...), custom_call_target="tpu_custom_call" | custom-call | flops 805306368 | bytes 1048576 | tf_op jit(solution)/shard_map/pallas_call | solution.py:429
  33.6 0.6 collective-permute-done.7.refs_8_
  34.2 1.8 %collective-permute-done.8.refs_9_ = bf16[640,256]{1,0:T(8,128)(2,1)S(1)} collective-permute-done((bf16[640,256]{1,0:T(8,128)(2,1)S(1)}, bf16[640,256]{1,0:T(8,128)(2,1)S(1)}, u32[]{:S(2)}, u32[]{:S(2)}) %collective-permute-start.8) | collective-permute-done | bytes 327712 | tf_op jit(solution)/shard_map/ppermute | solution.py:444
  36.0 1.6 %collective-permute-start.10 = (bf16[320,256]{1,0:T(8,128)(2,1)S(1)}, bf16[320,256]{1,0:T(8,128)(2,1)S(1)}, u32[]{:S(2)}, u32[]{:S(2)}) collective-permute-start(bf16[320,256]{1,0:T(8,128)(2,1)S(1)} %slice.15), channel_id=1, source_target_pairs={{0,2},{1,3},{2,0},{3,1},{4,6},{5,7},{6,4},{7,5},{8,10},{9,11},{10,... | collective-permute-start | bytes 491528 | tf_op jit(solution)/shard_map/ppermute | solution.py:444
  37.6 0.4 collective-permute-start.9
  37.9 1.5 %collective-permute-done.6.refs_7_ = bf16[320,256]{1,0:T(8,128)(2,1)S(1)} collective-permute-done((bf16[320,256]{1,0:T(8,128)(2,1)S(1)}, bf16[320,256]{1,0:T(8,128)(2,1)S(1)}, u32[]{:S(2)}, u32[]{:S(2)}) %collective-permute-start.6) | collective-permute-done | bytes 163872 | tf_op jit(solution)/shard_map/ppermute | solution.py:444
  39.5 6.2 %shard_map.116 = (f32[33,32,256]{2,1,0:T(8,128)S(1)}, f32[4,32,256]{2,1,0:T(8,128)S(1)}) custom-call(f32[33,32,256]{2,1,0:T(8,128)S(1)} %get-tuple-element.42.refs_0_, f32[4,32,256]{2,1,0:T(8,128)S(1)} %get-tuple-element.43.refs_1_, bf16[32,256,16]{2,1,0:T(8,128)(2,1)S(1)} %get-tuple-element.33.refs_2_, bf16[4,256,16]{2,1,0:T(8,128)(2,1)S(1)} %get-tuple-element.34.refs_3_, ...), custom_call_target="tpu_custom_call" | custom-call | flops 805306368 | bytes 1048576 | tf_op jit(solution)/shard_map/pallas_call | solution.py:429
  45.7 1.9 %shard_map.117 = f32[18,32,256]{2,1,0:T(8,128)S(1)} custom-call(f32[33,32,256]{2,1,0:T(8,128)S(1)} %get-tuple-element.50.refs_0_, f32[4,32,256]{2,1,0:T(8,128)S(1)} %get-tuple-element.47.refs_1_, bf16[32,256,16]{2,1,0:T(8,128)(2,1)S(1)} %get-tuple-element.33.refs_2_, bf16[4,256,16]{2,1,0:T(8,128)(2,1)S(1)} %get-tuple-element.34.refs_3_, ...), custom_call_target="tpu_custom_call" | custom-call | flops 268435456 | bytes 1048576 | tf_op jit(solution)/shard_map/pallas_call | solution.py:429
  47.7 0.0 copy-start.1
  47.7 0.1 collective-permute-start.11
  47.8 1.9 %shard_map.118 = (f32[16,32,256]{2,1,0:T(8,128)S(1)}, f32[2,32,256]{2,1,0:T(8,128)S(1)}) custom-call(f32[33,32,256]{2,1,0:T(8,128)S(1)} %get-tuple-element.50.refs_0_, f32[4,32,256]{2,1,0:T(8,128)S(1)} %get-tuple-element.47.refs_1_, bf16[32,256,16]{2,1,0:T(8,128)(2,1)S(1)} %get-tuple-element.33.refs_2_, bf16[4,256,16]{2,1,0:T(8,128)(2,1)S(1)} %get-tuple-element.34.refs_3_, ...), custom_call_target="tpu_custom_call" | custom-call | flops 268435456 | bytes 1048576 | tf_op jit(solution)/shard_map/pallas_call | solution.py:429
  49.7 0.1 collective-permute-done.11.given_ref
  49.8 1.3 %shard_map.119 = (f32[16,64,256]{2,1,0:T(8,128)S(1)}, f32[16,32,128]{2,1,0:T(8,128)S(1)}) custom-call(f32[16,32,256]{2,1,0:T(8,128)S(1)} %get-tuple-element.51.total_ref, f32[2,32,256]{2,1,0:T(8,128)S(1)} %get-tuple-element.52.far_ref, f32[18,32,256]{2,1,0:T(8,128)S(1)} %collective-permute-done.11.given_ref, bf16[16,32,256]{2,1,0:T(8,128)(2,1)S(1)} %copy-done.2, ...), custom_call_target="tpu_custom_call" | custom-call | flops 268435456 | bytes 1048576 | tf_op jit(solution)/shard_map/pallas_call | solution.py:429
  51.0 12.9 %all_to_all.5.products_ref = f32[16,32,128]{2,1,0:T(8,128)S(1)} all-to-all(f32[16,32,128]{2,1,0:T(8,128)S(1)} %get-tuple-element.55), channel_id=1, replica_groups=mesh['group'=2,'clus'=16] {'clus'}, dimensions={0} | all-to-all | bytes 524288 | tf_op jit(solution)/shard_map/all_to_all | solution.py:593
  64.0 3.9 %shard_map.120 = (f32[16,32,256]{2,1,0:T(8,128)}, f32[32,32]{1,0:T(8,128)}, f32[32,32]{1,0:T(8,128)}) custom-call(f32[16,32,128]{2,1,0:T(8,128)S(1)} %all_to_all.5.products_ref, f32[16,64,256]{2,1,0:T(8,128)S(1)} %get-tuple-element.56.stacked_ref), custom_call_target="tpu_custom_call" | custom-call | bytes 1048576 | tf_op jit(solution)/shard_map/pallas_call | solution.py:429
  (24 shorter events, 0.1 us)
Async XLA Ops:
  2.8 8.0 %collective-permute-start = (bf16[640,256]{1,0:T(8,128)(2,1)}, bf16[640,256]{1,0:T(8,128)(2,1)S(1)}, u32[]{:S(2)}, u32[]{:S(2)}) collective-permute-start(bf16[640,256]{1,0:T(8,128)(2,1)} %get-tuple-element.30.refs_0_.refs_6_), channel_id=1, source_target_pairs={{0,1},{1,0},{2,3},{3,2},{4,5},{5,4},{6,7},{7,6},{8,9},{9,8},{10,11... | collective-permute-start | bytes 983048 | tf_op jit(solution)/shard_map/ppermute | solution.py:444
  3.3 18.3 %collective-permute-start.2 = (bf16[640,256]{1,0:T(8,128)(2,1)}, bf16[640,256]{1,0:T(8,128)(2,1)S(1)}, u32[]{:S(2)}, u32[]{:S(2)}) collective-permute-start(bf16[640,256]{1,0:T(8,128)(2,1)} %get-tuple-element.30.refs_0_.refs_6_), channel_id=1, source_target_pairs={{0,12},{1,13},{2,14},{3,15},{4,8},{5,9},{6,10},{7,11},{8,4},{9,5},... | collective-permute-start | bytes 983048 | tf_op jit(solution)/shard_map/ppermute | solution.py:444
  7.9 15.7 %collective-permute-start.3 = (bf16[640,256]{1,0:T(8,128)(2,1)}, bf16[640,256]{1,0:T(8,128)(2,1)S(1)}, u32[]{:S(2)}, u32[]{:S(2)}) collective-permute-start(bf16[640,256]{1,0:T(8,128)(2,1)} %get-tuple-element.30.refs_0_.refs_6_), channel_id=1, source_target_pairs={{0,4},{1,5},{2,6},{3,7},{4,0},{5,1},{6,2},{7,3},{8,12},{9,13},{10,... | collective-permute-start | bytes 983048 | tf_op jit(solution)/shard_map/ppermute | solution.py:444
  7.9 15.7 %collective-permute-start.4 = (bf16[640,256]{1,0:T(8,128)(2,1)}, bf16[640,256]{1,0:T(8,128)(2,1)S(1)}, u32[]{:S(2)}, u32[]{:S(2)}) collective-permute-start(bf16[640,256]{1,0:T(8,128)(2,1)} %get-tuple-element.30.refs_0_.refs_6_), channel_id=1, source_target_pairs={{0,2},{1,3},{2,0},{3,1},{4,6},{5,7},{6,4},{7,5},{8,10},{9,11},{10,... | collective-permute-start | bytes 983048 | tf_op jit(solution)/shard_map/ppermute | solution.py:444
  9.4 1.4 %collective-permute-start.1 = (s32[16,64]{1,0:T(8,128)}, s32[16,64]{1,0:T(8,128)S(1)}, u32[]{:S(2)}, u32[]{:S(2)}) collective-permute-start(s32[16,64]{1,0:T(8,128)} %refs_2_.1), channel_id=1, source_target_pairs={{0,1},{1,0},{2,3},{3,2},{4,5},{5,4},{6,7},{7,6},{8,9},{9,8},{10,11... | collective-permute-start | bytes 12296 | tf_op jit(solution)/shard_map/ppermute | solution.py:444
  10.8 1.0 %copy-start = (f32[16,32,256]{2,1,0:T(8,128)S(1)}, f32[16,32,256]{2,1,0:T(8,128)}, u32[]{:S(2)}) copy-start(f32[16,32,256]{2,1,0:T(8,128)} %block_ref.3) | copy-start | bytes 1572868
  11.8 1.0 %copy-start.4 = (f32[16,32,256]{2,1,0:T(8,128)S(1)}, f32[16,32,256]{2,1,0:T(8,128)}, u32[]{:S(2)}) copy-start(f32[16,32,256]{2,1,0:T(8,128)} %refs_5_.1) | copy-start | bytes 1572868
  12.9 1.0 %copy-start.5 = (bf16[640,256]{1,0:T(8,128)(2,1)S(1)}, bf16[640,256]{1,0:T(8,128)(2,1)}, u32[]{:S(2)}) copy-start(bf16[640,256]{1,0:T(8,128)(2,1)} %get-tuple-element.30.refs_0_.refs_6_) | copy-start | bytes 983044
  13.9 0.7 %copy-start.7 = (f32[32,32]{1,0:T(8,128)S(1)}, f32[32,32]{1,0:T(8,128)}, u32[]{:S(2)}) copy-start(f32[32,32]{1,0:T(8,128)} %refs_6_.1) | copy-start | bytes 12292
  14.6 0.7 %copy-start.8 = (s32[16,64]{1,0:T(8,128)S(1)}, s32[16,64]{1,0:T(8,128)}, u32[]{:S(2)}) copy-start(s32[16,64]{1,0:T(8,128)} %refs_2_.1) | copy-start | bytes 12292
  15.3 3.2 %copy-start.6 = (bf16[640,256]{1,0:T(8,128)(2,1)S(1)}, bf16[640,256]{1,0:T(8,128)(2,1)}, u32[]{:S(2)}) copy-start(bf16[640,256]{1,0:T(8,128)(2,1)} %get-tuple-element.30.refs_0_.refs_6_) | copy-start | bytes 983044
  23.6 10.6 %collective-permute-start.7 = (bf16[640,256]{1,0:T(8,128)(2,1)S(1)}, bf16[640,256]{1,0:T(8,128)(2,1)S(1)}, u32[]{:S(2)}, u32[]{:S(2)}) collective-permute-start(bf16[640,256]{1,0:T(8,128)(2,1)S(1)} %collective-permute-done.2.refs_6_), channel_id=1, source_target_pairs={{0,4},{1,5},{2,6},{3,7},{4,0},{5,1},{6,2},{7,3},{8,12},{9,13},{10,... | collective-permute-start | bytes 983048 | tf_op jit(solution)/shard_map/ppermute | solution.py:444
  25.3 10.6 %collective-permute-start.8 = (bf16[640,256]{1,0:T(8,128)(2,1)S(1)}, bf16[640,256]{1,0:T(8,128)(2,1)S(1)}, u32[]{:S(2)}, u32[]{:S(2)}) collective-permute-start(bf16[640,256]{1,0:T(8,128)(2,1)S(1)} %collective-permute-done.2.refs_6_), channel_id=1, source_target_pairs={{0,2},{1,3},{2,0},{3,1},{4,6},{5,7},{6,4},{7,5},{8,10},{9,11},{10,... | collective-permute-start | bytes 983048 | tf_op jit(solution)/shard_map/ppermute | solution.py:444
  26.8 11.1 %collective-permute-start.5 = (bf16[320,256]{1,0:T(8,128)(2,1)S(1)}, bf16[320,256]{1,0:T(8,128)(2,1)S(1)}, u32[]{:S(2)}, u32[]{:S(2)}) collective-permute-start(bf16[320,256]{1,0:T(8,128)(2,1)S(1)} %slice.12), channel_id=1, source_target_pairs={{0,4},{1,5},{2,6},{3,7},{4,0},{5,1},{6,2},{7,3},{8,12},{9,13},{10,... | collective-permute-start | bytes 491528 | tf_op jit(solution)/shard_map/ppermute | solution.py:444
  27.2 12.2 %collective-permute-start.6 = (bf16[320,256]{1,0:T(8,128)(2,1)S(1)}, bf16[320,256]{1,0:T(8,128)(2,1)S(1)}, u32[]{:S(2)}, u32[]{:S(2)}) collective-permute-start(bf16[320,256]{1,0:T(8,128)(2,1)S(1)} %slice.13), channel_id=1, source_target_pairs={{0,2},{1,3},{2,0},{3,1},{4,6},{5,7},{6,4},{7,5},{8,10},{9,11},{10,... | collective-permute-start | bytes 491528 | tf_op jit(solution)/shard_map/ppermute | solution.py:444
  36.0 9.8 %collective-permute-start.10 = (bf16[320,256]{1,0:T(8,128)(2,1)S(1)}, bf16[320,256]{1,0:T(8,128)(2,1)S(1)}, u32[]{:S(2)}, u32[]{:S(2)}) collective-permute-start(bf16[320,256]{1,0:T(8,128)(2,1)S(1)} %slice.15), channel_id=1, source_target_pairs={{0,2},{1,3},{2,0},{3,1},{4,6},{5,7},{6,4},{7,5},{8,10},{9,11},{10,... | collective-permute-start | bytes 491528 | tf_op jit(solution)/shard_map/ppermute | solution.py:444
  37.6 8.2 %collective-permute-start.9 = (bf16[320,256]{1,0:T(8,128)(2,1)S(1)}, bf16[320,256]{1,0:T(8,128)(2,1)S(1)}, u32[]{:S(2)}, u32[]{:S(2)}) collective-permute-start(bf16[320,256]{1,0:T(8,128)(2,1)S(1)} %slice.14), channel_id=1, source_target_pairs={{0,4},{1,5},{2,6},{3,7},{4,0},{5,1},{6,2},{7,3},{8,12},{9,13},{10,... | collective-permute-start | bytes 491528 | tf_op jit(solution)/shard_map/ppermute | solution.py:444
  47.7 2.1 %copy-start.1 = (f32[16,32,256]{2,1,0:T(8,128)S(1)}, f32[16,32,256]{2,1,0:T(8,128)}, u32[]{:S(2)}) copy-start(f32[16,32,256]{2,1,0:T(8,128)} %block_ref.3) | copy-start | bytes 1572868
  47.7 2.1 %copy-start.2 = (bf16[16,32,256]{2,1,0:T(8,128)(2,1)S(1)}, bf16[16,32,256]{2,1,0:T(8,128)(2,1)}, u32[]{:S(2)}) copy-start(bf16[16,32,256]{2,1,0:T(8,128)(2,1)} %basis_ref.3) | copy-start | bytes 786436
  47.7 2.1 %copy-start.3 = (f32[16,32]{1,0:T(8,128)S(1)}, f32[16,32]{1,0:T(8,128)}, u32[]{:S(2)}) copy-start(f32[16,32]{1,0:T(8,128)} %scales_ref.3) | copy-start | bytes 6148
  47.7 2.1 %collective-permute-start.11 = (f32[18,32,256]{2,1,0:T(8,128)S(1)}, f32[18,32,256]{2,1,0:T(8,128)S(1)}, u32[]{:S(2)}, u32[]{:S(2)}) collective-permute-start(f32[18,32,256]{2,1,0:T(8,128)S(1)} %shard_map.117), channel_id=1, source_target_pairs={{0,1},{1,0},{2,3},{3,2},{4,5},{5,4},{6,7},{7,6},{8,9},{9,8},{10,11... | collective-permute-start | bytes 1769480 | tf_op jit(solution)/shard_map/ppermute | solution.py:444

commit v6 on v4

--- a/solution.py
+++ b/solution.py
@@ -468,27 +468,22 @@
     def fetched(values, step):
         return passed(values, parts, step)
 
-    head, tail = (fetched(half, over) for half in halved)
-    inward, sideways = fetched(message, inner), fetched(message, along)
-    token = yield
-    head, sideways = held((head, sideways), token)
-    inner_head, side_head = fetched(head, inner), fetched(head, along)
+    mirrored = fetched(message, over)
+    inward = [fetched(half, inner) for half in halved]
+    sideways = [fetched(half, along) for half in halved]
+    cut = message.shape[0] // 2
+    yield
     token = yield group_of([0], [[message]])
-    tail, inward, side_head = held((tail, inward, side_head), token)
-    side_tail, inner_tail = fetched(tail, along), fetched(tail, inner)
-    last_head = fetched(side_head, inner)
-    diagonal = fetched(inward, along)
-    token = yield group_of([over, inner, along], [[head, tail], [inward], [sideways]])
-    side_tail, diagonal, inner_head, inner_tail, last_head = held(
-        (side_tail, diagonal, inner_head, inner_tail, last_head), token
-    )
-    last_tail = fetched(side_tail, inner)
-    token = yield group_of(
-        [inner ^ along, over ^ inner, over ^ along],
-        [[diagonal], [inner_head, inner_tail], [side_head, side_tail]],
-    )
-    last_tail = held(last_tail, token)
-    yield group_of([over ^ inner ^ along], [[last_head, last_tail]])
+    mirrored, inward, sideways = held((mirrored, inward, sideways), token)
+    mirrored_inward = fetched(mirrored, inner)
+    mirrored_sideways = fetched(mirrored, along)
+    diagonal = [fetched(sideways[0], inner), fetched(inward[1], along)]
+    token = yield group_of([over, inner, along], [[mirrored], inward, sideways])
+    mirrored_inward, mirrored_sideways = held((mirrored_inward, mirrored_sideways), token)
+    last = [fetched(mirrored_sideways[:cut], inner), fetched(mirrored_inward[cut:], along)]
+    token = yield group_of([over ^ inner, over ^ along], [[mirrored_inward], [mirrored_sideways]])
+    last, diagonal = held((last, diagonal), token)
+    yield group_of([inner ^ along, over ^ inner ^ along], [diagonal, last])
 
 
 def local(

time: 70 us -> 67.7 us (0.967)
  waiting for transfers between devices: 11.8 us -> 5.42 us
  Pallas kernels: 24.5 us -> 28.8 us
  starting transfers between devices: 13.3 us -> 15.5 us
  blocking collectives: 14.5 us -> 12.7 us
    ppermute x14, waiting for transfers between devices: 11.8 us -> 5.42 us  [passed(): return lax.ppermute(values, 'clus', pairs)]
    pallas_call x8, Pallas kernels: 24.5 us -> 28.8 us  [call(): pl.pallas_call(kernel, out_shape=out_shape, in_specs=specs(len(operands),...]
    ppermute x14, starting transfers between devices: 13.3 us -> 15.5 us  [passed(): return lax.ppermute(values, 'clus', pairs)]
    all_to_all x1, blocking collectives: 14.5 us -> 12.7 us  [local(): lax.all_to_all(products, 'clus', split_axis=0, concat_axis=0, tiled=True)]
  transfers between devices with their start and end apart: 14 -> 14, of which waited for: 7 -> 5; matrix products, arithmetic and copies ran while one was open for 0% -> 0% of each run, Pallas kernels for 21% -> 25%
where the time goes in v6:
time: 67.7 us; the launch traced here: 67.6 us
  Pallas kernels  28.8 us (43%)
  starting transfers between devices  15.5 us (23%)
  blocking collectives  12.7 us (19%)
  waiting for transfers between devices  5.42 us (8%)
  local copies, waits for them, and re-layouts  4.51 us (7%)
  between operations  0.76 us (1%)
    pallas_call x8, Pallas kernels, call(): pl.pallas_call(kernel, out_shape=out_shape, in_specs=specs(len(operands),...  28.8 us
    ppermute x14, starting transfers between devices, passed(): return lax.ppermute(values, 'clus', pairs)  15.5 us
    all_to_all x1, blocking collectives, local(): lax.all_to_all(products, 'clus', split_axis=0, concat_axis=0, tiled=True)  12.7 us
    ppermute x14, waiting for transfers between devices, passed(): return lax.ppermute(values, 'clus', pairs)  5.42 us
    unnamed x18, local copies, waits for them, and re-layouts  4.48 us
  transfers between devices with their start and end apart: 14, of which 5 were waited for; matrix products, arithmetic and copies ran while one was open for 0% of the time, Pallas kernels for 25%

profile of v6, /device:TPU:0, one launch (start us, length us, event | category | flops | bytes accessed | tf_op | source)
XLA Modules:
  0.0 67.6 jit_solution(16690223259099390166)
XLA Ops:
  0.6 2.2 %shard_map.112 = (bf16[640,256]{1,0:T(8,128)(2,1)}, bf16[320,256]{1,0:T(8,128)(2,1)}, bf16[320,256]{1,0:T(8,128)(2,1)}) custom-call(f32[16,32,256]{2,1,0:T(8,128)} %block_ref.3, bf16[16,32,256]{2,1,0:T(8,128)(2,1)} %basis_ref.3, f32[16,32]{1,0:T(8,128)} %scales_ref.3, bf16[3,16,256]{2,1,0:T(8,128)(2,1)} %bitcast.3, bf16[3,16,32]{2,1,0:T(8,128)(2,1)} %bitcast.4, ...), custom_call_target="tpu_custom_call" | custom-call | bytes 1048576 | tf_op jit(solution)/shard_map/pallas_call | solution.py:428
  2.8 0.5 collective-permute-start
  3.3 4.6 %collective-permute-start.2 = (bf16[640,256]{1,0:T(8,128)(2,1)}, bf16[640,256]{1,0:T(8,128)(2,1)S(1)}, u32[]{:S(2)}, u32[]{:S(2)}) collective-permute-start(bf16[640,256]{1,0:T(8,128)(2,1)} %get-tuple-element.35.refs_0_.refs_6_), channel_id=1, source_target_pairs={{0,12},{1,13},{2,14},{3,15},{4,8},{5,9},{6,10},{7,11},{8,4},{9,5},... | collective-permute-start | bytes 983048 | tf_op jit(solution)/shard_map/ppermute | solution.py:443
  7.9 0.2 collective-permute-start.1
  8.1 1.5 %collective-permute-start.5 = (bf16[320,256]{1,0:T(8,128)(2,1)}, bf16[320,256]{1,0:T(8,128)(2,1)S(1)}, u32[]{:S(2)}, u32[]{:S(2)}) collective-permute-start(bf16[320,256]{1,0:T(8,128)(2,1)} %get-tuple-element.44), channel_id=1, source_target_pairs={{0,2},{1,3},{2,0},{3,1},{4,6},{5,7},{6,4},{7,5},{8,10},{9,11},{10,... | collective-permute-start | bytes 491528 | tf_op jit(solution)/shard_map/ppermute | solution.py:443
  9.6 2.0 %collective-permute-start.4 = (bf16[320,256]{1,0:T(8,128)(2,1)}, bf16[320,256]{1,0:T(8,128)(2,1)S(1)}, u32[]{:S(2)}, u32[]{:S(2)}) collective-permute-start(bf16[320,256]{1,0:T(8,128)(2,1)} %get-tuple-element.45), channel_id=1, source_target_pairs={{0,4},{1,5},{2,6},{3,7},{4,0},{5,1},{6,2},{7,3},{8,12},{9,13},{10,... | collective-permute-start | bytes 491528 | tf_op jit(solution)/shard_map/ppermute | solution.py:443
  11.7 0.5 collective-permute-start.6
  12.2 1.0 %copy-done = f32[16,32,256]{2,1,0:T(8,128)S(1)} copy-done((f32[16,32,256]{2,1,0:T(8,128)S(1)}, f32[16,32,256]{2,1,0:T(8,128)}, u32[]{:S(2)}) %copy-start) | copy-done | bytes 524312
  13.2 1.0 %copy-done.4 = f32[16,32,256]{2,1,0:T(8,128)S(1)} copy-done((f32[16,32,256]{2,1,0:T(8,128)S(1)}, f32[16,32,256]{2,1,0:T(8,128)}, u32[]{:S(2)}) %copy-start.4) | copy-done | bytes 524312
  14.3 1.0 %copy-done.5 = bf16[640,256]{1,0:T(8,128)(2,1)S(1)} copy-done((bf16[640,256]{1,0:T(8,128)(2,1)S(1)}, bf16[640,256]{1,0:T(8,128)(2,1)}, u32[]{:S(2)}) %copy-start.5) | copy-done | bytes 327704
  15.2 0.7 %copy-done.7 = f32[32,32]{1,0:T(8,128)S(1)} copy-done((f32[32,32]{1,0:T(8,128)S(1)}, f32[32,32]{1,0:T(8,128)}, u32[]{:S(2)}) %copy-start.7) | copy-done | bytes 4120
  16.0 0.7 %copy-done.8 = s32[16,64]{1,0:T(8,128)S(1)} copy-done((s32[16,64]{1,0:T(8,128)S(1)}, s32[16,64]{1,0:T(8,128)}, u32[]{:S(2)}) %copy-start.8) | copy-done | bytes 4120
  16.7 3.2 %shard_map.113 = (f32[33,32,256]{2,1,0:T(8,128)S(1)}, f32[4,32,256]{2,1,0:T(8,128)S(1)}, f32[32,64]{1,0:T(8,128)S(1)}, bf16[32,256,16]{2,1,0:T(8,128)(2,1)S(1)},...) custom-call(bf16[640,256]{1,0:T(8,128)(2,1)S(1)} %copy-done.5, ...), custom_call_target="tpu_custom_call" | custom-call | flops 2147483648 | bytes 1048576 | tf_op jit(solution)/shard_map/pallas_call | solution.py:428
  19.8 3.2 %shard_map.114 = (f32[33,32,256]{2,1,0:T(8,128)S(1)}, f32[4,32,256]{2,1,0:T(8,128)S(1)}) custom-call(f32[33,32,256]{2,1,0:T(8,128)S(1)} %get-tuple-element.36.refs_0_, f32[4,32,256]{2,1,0:T(8,128)S(1)} %get-tuple-element.37.refs_1_, bf16[32,256,16]{2,1,0:T(8,128)(2,1)S(1)} %get-tuple-element.38.refs_2_, bf16[4,256,16]{2,1,0:T(8,128)(2,1)S(1)} %get-tuple-element.39.refs_3_, ...), custom_call_target="tpu_custom_call" | custom-call | flops 268435456 | bytes 1048576 | tf_op jit(solution)/shard_map/pallas_call | solution.py:428
  23.0 0.6 collective-permute-done.4.refs_8_
  23.6 1.8 %collective-permute-start.7 = (bf16[640,256]{1,0:T(8,128)(2,1)S(1)}, bf16[640,256]{1,0:T(8,128)(2,1)S(1)}, u32[]{:S(2)}, u32[]{:S(2)}) collective-permute-start(bf16[640,256]{1,0:T(8,128)(2,1)S(1)} %collective-permute-done.2.refs_6_), channel_id=1, source_target_pairs={{0,4},{1,5},{2,6},{3,7},{4,0},{5,1},{6,2},{7,3},{8,12},{9,13},{10,... | collective-permute-start | bytes 983048 | tf_op jit(solution)/shard_map/ppermute | solution.py:443
  25.4 1.5 %collective-permute-start.8 = (bf16[640,256]{1,0:T(8,128)(2,1)S(1)}, bf16[640,256]{1,0:T(8,128)(2,1)S(1)}, u32[]{:S(2)}, u32[]{:S(2)}) collective-permute-start(bf16[640,256]{1,0:T(8,128)(2,1)S(1)} %collective-permute-done.2.refs_6_), channel_id=1, source_target_pairs={{0,2},{1,3},{2,0},{3,1},{4,6},{5,7},{6,4},{7,5},{8,10},{9,11},{10,... | collective-permute-start | bytes 983048 | tf_op jit(solution)/shard_map/ppermute | solution.py:443
  26.9 0.3 collective-permute-start.11
  27.2 0.5 collective-permute-start.12
  27.7 5.8 %shard_map.115 = (f32[33,32,256]{2,1,0:T(8,128)S(1)}, f32[4,32,256]{2,1,0:T(8,128)S(1)}) custom-call(f32[33,32,256]{2,1,0:T(8,128)S(1)} %get-tuple-element.42.refs_0_, f32[4,32,256]{2,1,0:T(8,128)S(1)} %get-tuple-element.43.refs_1_, bf16[32,256,16]{2,1,0:T(8,128)(2,1)S(1)} %get-tuple-element.38.refs_2_, bf16[4,256,16]{2,1,0:T(8,128)(2,1)S(1)} %get-tuple-element.39.refs_3_, ...), custom_call_target="tpu_custom_call" | custom-call | flops 805306368 | bytes 1048576 | tf_op jit(solution)/shard_map/pallas_call | solution.py:428
  33.5 0.8 %collective-permute-done.7.refs_6_ = bf16[640,256]{1,0:T(8,128)(2,1)S(1)} collective-permute-done((bf16[640,256]{1,0:T(8,128)(2,1)S(1)}, bf16[640,256]{1,0:T(8,128)(2,1)S(1)}, u32[]{:S(2)}, u32[]{:S(2)}) %collective-permute-start.7) | collective-permute-done | bytes 327712 | tf_op jit(solution)/shard_map/ppermute | solution.py:443
  34.3 1.8 %collective-permute-done.8.refs_7_ = bf16[640,256]{1,0:T(8,128)(2,1)S(1)} collective-permute-done((bf16[640,256]{1,0:T(8,128)(2,1)S(1)}, bf16[640,256]{1,0:T(8,128)(2,1)S(1)}, u32[]{:S(2)}, u32[]{:S(2)}) %collective-permute-start.8) | collective-permute-done | bytes 327712 | tf_op jit(solution)/shard_map/ppermute | solution.py:443
  36.0 1.6 %collective-permute-start.10 = (bf16[320,256]{1,0:T(8,128)(2,1)S(1)}, bf16[320,256]{1,0:T(8,128)(2,1)S(1)}, u32[]{:S(2)}, u32[]{:S(2)}) collective-permute-start(bf16[320,256]{1,0:T(8,128)(2,1)S(1)} %slice.7), channel_id=1, source_target_pairs={{0,2},{1,3},{2,0},{3,1},{4,6},{5,7},{6,4},{7,5},{8,10},{9,11},{10,... | collective-permute-start | bytes 491528 | tf_op jit(solution)/shard_map/ppermute | solution.py:443
  37.6 0.4 collective-permute-start.9
  38.0 4.7 %shard_map.116 = (f32[33,32,256]{2,1,0:T(8,128)S(1)}, f32[4,32,256]{2,1,0:T(8,128)S(1)}) custom-call(f32[33,32,256]{2,1,0:T(8,128)S(1)} %get-tuple-element.51.refs_0_, f32[4,32,256]{2,1,0:T(8,128)S(1)} %get-tuple-element.52.refs_1_, bf16[32,256,16]{2,1,0:T(8,128)(2,1)S(1)} %get-tuple-element.38.refs_2_, bf16[4,256,16]{2,1,0:T(8,128)(2,1)S(1)} %get-tuple-element.39.refs_3_, ...), custom_call_target="tpu_custom_call" | custom-call | flops 536870912 | bytes 1048576 | tf_op jit(solution)/shard_map/pallas_call | solution.py:428
  42.7 0.3 collective-permute-done.9.refs_8_
  43.0 4.7 %shard_map.117 = (f32[16,32,256]{2,1,0:T(8,128)S(1)}, f32[2,32,256]{2,1,0:T(8,128)S(1)}, f32[18,32,256]{2,1,0:T(8,128)S(1)}) custom-call(f32[33,32,256]{2,1,0:T(8,128)S(1)} %get-tuple-element.55.refs_0_, f32[4,32,256]{2,1,0:T(8,128)S(1)} %get-tuple-element.56.refs_1_, bf16[32,256,16]{2,1,0:T(8,128)(2,1)S(1)} %get-tuple-element.38.refs_2_, ...), custom_call_target="tpu_custom_call" | custom-call | flops 536870912 | bytes 1048576 | tf_op jit(solution)/shard_map/pallas_call | solution.py:428
  47.7 0.1 collective-permute-start.13
  47.8 2.0 %collective-permute-done.13.given_ref = f32[18,32,256]{2,1,0:T(8,128)S(1)} collective-permute-done((f32[18,32,256]{2,1,0:T(8,128)S(1)}, f32[18,32,256]{2,1,0:T(8,128)S(1)}, u32[]{:S(2)}, u32[]{:S(2)}) %collective-permute-start.13) | collective-permute-done | bytes 589856 | tf_op jit(solution)/shard_map/ppermute | solution.py:443
  49.8 1.3 %shard_map.118 = (f32[16,64,256]{2,1,0:T(8,128)S(1)}, f32[16,32,128]{2,1,0:T(8,128)S(1)}) custom-call(f32[16,32,256]{2,1,0:T(8,128)S(1)} %get-tuple-element.61.total_ref, f32[2,32,256]{2,1,0:T(8,128)S(1)} %get-tuple-element.62.far_ref, f32[18,32,256]{2,1,0:T(8,128)S(1)} %collective-permute-done.13.given_ref, bf16[16,32,256]{2,1,0:T(8,128)(2,1)S(1)} %copy-done.2, ...), custom_call_target="tpu_custom_call" | custom-call | flops 268435456 | bytes 1048576 | tf_op jit(solution)/shard_map/pallas_call | solution.py:428
  51.0 12.7 %all_to_all.5.products_ref = f32[16,32,128]{2,1,0:T(8,128)S(1)} all-to-all(f32[16,32,128]{2,1,0:T(8,128)S(1)} %get-tuple-element.65), channel_id=1, replica_groups=mesh['group'=2,'clus'=16] {'clus'}, dimensions={0} | all-to-all | bytes 524288 | tf_op jit(solution)/shard_map/all_to_all | solution.py:586
  63.7 3.9 %shard_map.119 = (f32[16,32,256]{2,1,0:T(8,128)}, f32[32,32]{1,0:T(8,128)}, f32[32,32]{1,0:T(8,128)}) custom-call(f32[16,32,128]{2,1,0:T(8,128)S(1)} %all_to_all.5.products_ref, f32[16,64,256]{2,1,0:T(8,128)S(1)} %get-tuple-element.66.stacked_ref), custom_call_target="tpu_custom_call" | custom-call | bytes 1048576 | tf_op jit(solution)/shard_map/pallas_call | solution.py:428
  (25 shorter events, 0.1 us)
Async XLA Ops:
  2.8 8.8 %collective-permute-start = (bf16[640,256]{1,0:T(8,128)(2,1)}, bf16[640,256]{1,0:T(8,128)(2,1)S(1)}, u32[]{:S(2)}, u32[]{:S(2)}) collective-permute-start(bf16[640,256]{1,0:T(8,128)(2,1)} %get-tuple-element.35.refs_0_.refs_6_), channel_id=1, source_target_pairs={{0,1},{1,0},{2,3},{3,2},{4,5},{5,4},{6,7},{7,6},{8,9},{9,8},{10,11... | collective-permute-start | bytes 983048 | tf_op jit(solution)/shard_map/ppermute | solution.py:443
  3.3 20.3 %collective-permute-start.2 = (bf16[640,256]{1,0:T(8,128)(2,1)}, bf16[640,256]{1,0:T(8,128)(2,1)S(1)}, u32[]{:S(2)}, u32[]{:S(2)}) collective-permute-start(bf16[640,256]{1,0:T(8,128)(2,1)} %get-tuple-element.35.refs_0_.refs_6_), channel_id=1, source_target_pairs={{0,12},{1,13},{2,14},{3,15},{4,8},{5,9},{6,10},{7,11},{8,4},{9,5},... | collective-permute-start | bytes 983048 | tf_op jit(solution)/shard_map/ppermute | solution.py:443
  7.9 1.8 %collective-permute-start.1 = (s32[16,64]{1,0:T(8,128)}, s32[16,64]{1,0:T(8,128)S(1)}, u32[]{:S(2)}, u32[]{:S(2)}) collective-permute-start(s32[16,64]{1,0:T(8,128)} %refs_2_.1), channel_id=1, source_target_pairs={{0,1},{1,0},{2,3},{3,2},{4,5},{5,4},{6,7},{7,6},{8,9},{9,8},{10,11... | collective-permute-start | bytes 12296 | tf_op jit(solution)/shard_map/ppermute | solution.py:443
  8.1 14.9 %collective-permute-start.3 = (bf16[320,256]{1,0:T(8,128)(2,1)}, bf16[320,256]{1,0:T(8,128)(2,1)S(1)}, u32[]{:S(2)}, u32[]{:S(2)}) collective-permute-start(bf16[320,256]{1,0:T(8,128)(2,1)} %get-tuple-element.44), channel_id=1, source_target_pairs={{0,4},{1,5},{2,6},{3,7},{4,0},{5,1},{6,2},{7,3},{8,12},{9,13},{10,... | collective-permute-start | bytes 491528 | tf_op jit(solution)/shard_map/ppermute | solution.py:443
  8.1 15.5 %collective-permute-start.5 = (bf16[320,256]{1,0:T(8,128)(2,1)}, bf16[320,256]{1,0:T(8,128)(2,1)S(1)}, u32[]{:S(2)}, u32[]{:S(2)}) collective-permute-start(bf16[320,256]{1,0:T(8,128)(2,1)} %get-tuple-element.44), channel_id=1, source_target_pairs={{0,2},{1,3},{2,0},{3,1},{4,6},{5,7},{6,4},{7,5},{8,10},{9,11},{10,... | collective-permute-start | bytes 491528 | tf_op jit(solution)/shard_map/ppermute | solution.py:443
  9.6 14.0 %collective-permute-start.4 = (bf16[320,256]{1,0:T(8,128)(2,1)}, bf16[320,256]{1,0:T(8,128)(2,1)S(1)}, u32[]{:S(2)}, u32[]{:S(2)}) collective-permute-start(bf16[320,256]{1,0:T(8,128)(2,1)} %get-tuple-element.45), channel_id=1, source_target_pairs={{0,4},{1,5},{2,6},{3,7},{4,0},{5,1},{6,2},{7,3},{8,12},{9,13},{10,... | collective-permute-start | bytes 491528 | tf_op jit(solution)/shard_map/ppermute | solution.py:443
  11.7 11.9 %collective-permute-start.6 = (bf16[320,256]{1,0:T(8,128)(2,1)}, bf16[320,256]{1,0:T(8,128)(2,1)S(1)}, u32[]{:S(2)}, u32[]{:S(2)}) collective-permute-start(bf16[320,256]{1,0:T(8,128)(2,1)} %get-tuple-element.45), channel_id=1, source_target_pairs={{0,2},{1,3},{2,0},{3,1},{4,6},{5,7},{6,4},{7,5},{8,10},{9,11},{10,... | collective-permute-start | bytes 491528 | tf_op jit(solution)/shard_map/ppermute | solution.py:443
  12.2 1.0 %copy-start = (f32[16,32,256]{2,1,0:T(8,128)S(1)}, f32[16,32,256]{2,1,0:T(8,128)}, u32[]{:S(2)}) copy-start(f32[16,32,256]{2,1,0:T(8,128)} %block_ref.3) | copy-start | bytes 1572868
  13.2 1.0 %copy-start.4 = (f32[16,32,256]{2,1,0:T(8,128)S(1)}, f32[16,32,256]{2,1,0:T(8,128)}, u32[]{:S(2)}) copy-start(f32[16,32,256]{2,1,0:T(8,128)} %refs_5_.1) | copy-start | bytes 1572868
  14.3 1.0 %copy-start.5 = (bf16[640,256]{1,0:T(8,128)(2,1)S(1)}, bf16[640,256]{1,0:T(8,128)(2,1)}, u32[]{:S(2)}) copy-start(bf16[640,256]{1,0:T(8,128)(2,1)} %get-tuple-element.35.refs_0_.refs_6_) | copy-start | bytes 983044
  15.2 0.7 %copy-start.7 = (f32[32,32]{1,0:T(8,128)S(1)}, f32[32,32]{1,0:T(8,128)}, u32[]{:S(2)}) copy-start(f32[32,32]{1,0:T(8,128)} %refs_6_.1) | copy-start | bytes 12292
  16.0 0.7 %copy-start.8 = (s32[16,64]{1,0:T(8,128)S(1)}, s32[16,64]{1,0:T(8,128)}, u32[]{:S(2)}) copy-start(s32[16,64]{1,0:T(8,128)} %refs_2_.1) | copy-start | bytes 12292
  16.6 3.2 %copy-start.6 = (bf16[640,256]{1,0:T(8,128)(2,1)S(1)}, bf16[640,256]{1,0:T(8,128)(2,1)}, u32[]{:S(2)}) copy-start(bf16[640,256]{1,0:T(8,128)(2,1)} %get-tuple-element.35.refs_0_.refs_6_) | copy-start | bytes 983044
  23.6 10.6 %collective-permute-start.7 = (bf16[640,256]{1,0:T(8,128)(2,1)S(1)}, bf16[640,256]{1,0:T(8,128)(2,1)S(1)}, u32[]{:S(2)}, u32[]{:S(2)}) collective-permute-start(bf16[640,256]{1,0:T(8,128)(2,1)S(1)} %collective-permute-done.2.refs_6_), channel_id=1, source_target_pairs={{0,4},{1,5},{2,6},{3,7},{4,0},{5,1},{6,2},{7,3},{8,12},{9,13},{10,... | collective-permute-start | bytes 983048 | tf_op jit(solution)/shard_map/ppermute | solution.py:443
  25.4 10.6 %collective-permute-start.8 = (bf16[640,256]{1,0:T(8,128)(2,1)S(1)}, bf16[640,256]{1,0:T(8,128)(2,1)S(1)}, u32[]{:S(2)}, u32[]{:S(2)}) collective-permute-start(bf16[640,256]{1,0:T(8,128)(2,1)S(1)} %collective-permute-done.2.refs_6_), channel_id=1, source_target_pairs={{0,2},{1,3},{2,0},{3,1},{4,6},{5,7},{6,4},{7,5},{8,10},{9,11},{10,... | collective-permute-start | bytes 983048 | tf_op jit(solution)/shard_map/ppermute | solution.py:443
  26.9 15.8 %collective-permute-start.11 = (bf16[320,256]{1,0:T(8,128)(2,1)S(1)}, bf16[320,256]{1,0:T(8,128)(2,1)S(1)}, u32[]{:S(2)}, u32[]{:S(2)}) collective-permute-start(bf16[320,256]{1,0:T(8,128)(2,1)S(1)} %collective-permute-done.5.refs_9_), channel_id=1, source_target_pairs={{0,4},{1,5},{2,6},{3,7},{4,0},{5,1},{6,2},{7,3},{8,12},{9,13},{10,... | collective-permute-start | bytes 491528 | tf_op jit(solution)/shard_map/ppermute | solution.py:443
  27.2 15.5 %collective-permute-start.12 = (bf16[320,256]{1,0:T(8,128)(2,1)S(1)}, bf16[320,256]{1,0:T(8,128)(2,1)S(1)}, u32[]{:S(2)}, u32[]{:S(2)}) collective-permute-start(bf16[320,256]{1,0:T(8,128)(2,1)S(1)} %collective-permute-done.4.refs_8_), channel_id=1, source_target_pairs={{0,2},{1,3},{2,0},{3,1},{4,6},{5,7},{6,4},{7,5},{8,10},{9,11},{10,... | collective-permute-start | bytes 491528 | tf_op jit(solution)/shard_map/ppermute | solution.py:443
  36.0 6.7 %collective-permute-start.10 = (bf16[320,256]{1,0:T(8,128)(2,1)S(1)}, bf16[320,256]{1,0:T(8,128)(2,1)S(1)}, u32[]{:S(2)}, u32[]{:S(2)}) collective-permute-start(bf16[320,256]{1,0:T(8,128)(2,1)S(1)} %slice.7), channel_id=1, source_target_pairs={{0,2},{1,3},{2,0},{3,1},{4,6},{5,7},{6,4},{7,5},{8,10},{9,11},{10,... | collective-permute-start | bytes 491528 | tf_op jit(solution)/shard_map/ppermute | solution.py:443
  37.6 5.4 %collective-permute-start.9 = (bf16[320,256]{1,0:T(8,128)(2,1)S(1)}, bf16[320,256]{1,0:T(8,128)(2,1)S(1)}, u32[]{:S(2)}, u32[]{:S(2)}) collective-permute-start(bf16[320,256]{1,0:T(8,128)(2,1)S(1)} %slice.6), channel_id=1, source_target_pairs={{0,4},{1,5},{2,6},{3,7},{4,0},{5,1},{6,2},{7,3},{8,12},{9,13},{10,... | collective-permute-start | bytes 491528 | tf_op jit(solution)/shard_map/ppermute | solution.py:443
  43.0 6.8 %copy-start.1 = (f32[16,32,256]{2,1,0:T(8,128)S(1)}, f32[16,32,256]{2,1,0:T(8,128)}, u32[]{:S(2)}) copy-start(f32[16,32,256]{2,1,0:T(8,128)} %block_ref.3) | copy-start | bytes 1572868
  43.0 6.8 %copy-start.2 = (bf16[16,32,256]{2,1,0:T(8,128)(2,1)S(1)}, bf16[16,32,256]{2,1,0:T(8,128)(2,1)}, u32[]{:S(2)}) copy-start(bf16[16,32,256]{2,1,0:T(8,128)(2,1)} %basis_ref.3) | copy-start | bytes 786436
  43.0 6.8 %copy-start.3 = (f32[16,32]{1,0:T(8,128)S(1)}, f32[16,32]{1,0:T(8,128)}, u32[]{:S(2)}) copy-start(f32[16,32]{1,0:T(8,128)} %scales_ref.3) | copy-start | bytes 6148
  47.7 2.1 %collective-permute-start.13 = (f32[18,32,256]{2,1,0:T(8,128)S(1)}, f32[18,32,256]{2,1,0:T(8,128)S(1)}, u32[]{:S(2)}, u32[]{:S(2)}) collective-permute-start(f32[18,32,256]{2,1,0:T(8,128)S(1)} %get-tuple-element.63), channel_id=1, source_target_pairs={{0,1},{1,0},{2,3},{3,2},{4,5},{5,4},{6,7},{7,6},{8,9},{9,8},{10,11... | collective-permute-start | bytes 1769480 | tf_op jit(solution)/shard_map/ppermute | solution.py:443

commit v7 on v6

--- a/solution.py
+++ b/solution.py
@@ -244,7 +244,7 @@
     copy = pltpu.make_async_copy(ids_ref, ids_scalar_ref, copied)
     copy.start()
 
-    pair = 2 if devices % 2 == 0 else 1
+    pair = 2 if targets == 1 and devices % 2 == 0 else 1
 
     def far_step(turn, carry):
         terms = []

time: 67.7 us -> 67.5 us (level)
  Pallas kernels: 28.8 us -> 28 us
    pallas_call x8, Pallas kernels: 28.8 us -> 28 us  [call(): pl.pallas_call(kernel, out_shape=out_shape, in_specs=specs(len(operands),...]
  transfers between devices with their start and end apart: 14 -> 14, of which waited for: 5 -> 5; matrix products, arithmetic and copies ran while one was open for 0% -> 0% of each run, Pallas kernels for 25% -> 24%
where the time goes in v7:
time: 67.5 us; the launch traced here: 67.2 us
  Pallas kernels  28 us (41%)
  starting transfers between devices  15.5 us (23%)
  blocking collectives  12.6 us (19%)
  waiting for transfers between devices  5.81 us (9%)
  local copies, waits for them, and re-layouts  4.51 us (7%)
  between operations  0.76 us (1%)
    pallas_call x8, Pallas kernels, call(): pl.pallas_call(kernel, out_shape=out_shape, in_specs=specs(len(operands),...  28 us
    ppermute x14, starting transfers between devices, passed(): return lax.ppermute(values, 'clus', pairs)  15.5 us
    all_to_all x1, blocking collectives, local(): lax.all_to_all(products, 'clus', split_axis=0, concat_axis=0, tiled=True)  12.6 us
    ppermute x14, waiting for transfers between devices, passed(): return lax.ppermute(values, 'clus', pairs)  5.81 us
    unnamed x18, local copies, waits for them, and re-layouts  4.48 us
  transfers between devices with their start and end apart: 14, of which 5 were waited for; matrix products, arithmetic and copies ran while one was open for 0% of the time, Pallas kernels for 24%

profile of v7, /device:TPU:0, one launch (start us, length us, event | category | flops | bytes accessed | tf_op | source)
XLA Modules:
  0.0 67.2 jit_solution(9388362770039657596)
XLA Ops:
  0.6 2.2 %shard_map.112 = (bf16[640,256]{1,0:T(8,128)(2,1)}, bf16[320,256]{1,0:T(8,128)(2,1)}, bf16[320,256]{1,0:T(8,128)(2,1)}) custom-call(f32[16,32,256]{2,1,0:T(8,128)} %block_ref.3, bf16[16,32,256]{2,1,0:T(8,128)(2,1)} %basis_ref.3, f32[16,32]{1,0:T(8,128)} %scales_ref.3, bf16[3,16,256]{2,1,0:T(8,128)(2,1)} %bitcast.3, bf16[3,16,32]{2,1,0:T(8,128)(2,1)} %bitcast.4, ...), custom_call_target="tpu_custom_call" | custom-call | bytes 1048576 | tf_op jit(solution)/shard_map/pallas_call | solution.py:428
  2.8 0.5 collective-permute-start
  3.3 4.6 %collective-permute-start.2 = (bf16[640,256]{1,0:T(8,128)(2,1)}, bf16[640,256]{1,0:T(8,128)(2,1)S(1)}, u32[]{:S(2)}, u32[]{:S(2)}) collective-permute-start(bf16[640,256]{1,0:T(8,128)(2,1)} %get-tuple-element.35.refs_0_.refs_6_), channel_id=1, source_target_pairs={{0,12},{1,13},{2,14},{3,15},{4,8},{5,9},{6,10},{7,11},{8,4},{9,5},... | collective-permute-start | bytes 983048 | tf_op jit(solution)/shard_map/ppermute | solution.py:443
  7.9 0.2 collective-permute-start.1
  8.1 1.5 %collective-permute-start.5 = (bf16[320,256]{1,0:T(8,128)(2,1)}, bf16[320,256]{1,0:T(8,128)(2,1)S(1)}, u32[]{:S(2)}, u32[]{:S(2)}) collective-permute-start(bf16[320,256]{1,0:T(8,128)(2,1)} %get-tuple-element.44), channel_id=1, source_target_pairs={{0,2},{1,3},{2,0},{3,1},{4,6},{5,7},{6,4},{7,5},{8,10},{9,11},{10,... | collective-permute-start | bytes 491528 | tf_op jit(solution)/shard_map/ppermute | solution.py:443
  9.6 2.0 %collective-permute-start.4 = (bf16[320,256]{1,0:T(8,128)(2,1)}, bf16[320,256]{1,0:T(8,128)(2,1)S(1)}, u32[]{:S(2)}, u32[]{:S(2)}) collective-permute-start(bf16[320,256]{1,0:T(8,128)(2,1)} %get-tuple-element.45), channel_id=1, source_target_pairs={{0,4},{1,5},{2,6},{3,7},{4,0},{5,1},{6,2},{7,3},{8,12},{9,13},{10,... | collective-permute-start | bytes 491528 | tf_op jit(solution)/shard_map/ppermute | solution.py:443
  11.7 0.5 collective-permute-start.6
  12.2 1.0 %copy-done = f32[16,32,256]{2,1,0:T(8,128)S(1)} copy-done((f32[16,32,256]{2,1,0:T(8,128)S(1)}, f32[16,32,256]{2,1,0:T(8,128)}, u32[]{:S(2)}) %copy-start) | copy-done | bytes 524312
  13.2 1.0 %copy-done.4 = f32[16,32,256]{2,1,0:T(8,128)S(1)} copy-done((f32[16,32,256]{2,1,0:T(8,128)S(1)}, f32[16,32,256]{2,1,0:T(8,128)}, u32[]{:S(2)}) %copy-start.4) | copy-done | bytes 524312
  14.3 1.0 %copy-done.5 = bf16[640,256]{1,0:T(8,128)(2,1)S(1)} copy-done((bf16[640,256]{1,0:T(8,128)(2,1)S(1)}, bf16[640,256]{1,0:T(8,128)(2,1)}, u32[]{:S(2)}) %copy-start.5) | copy-done | bytes 327704
  15.2 0.7 %copy-done.7 = f32[32,32]{1,0:T(8,128)S(1)} copy-done((f32[32,32]{1,0:T(8,128)S(1)}, f32[32,32]{1,0:T(8,128)}, u32[]{:S(2)}) %copy-start.7) | copy-done | bytes 4120
  16.0 0.7 %copy-done.8 = s32[16,64]{1,0:T(8,128)S(1)} copy-done((s32[16,64]{1,0:T(8,128)S(1)}, s32[16,64]{1,0:T(8,128)}, u32[]{:S(2)}) %copy-start.8) | copy-done | bytes 4120
  16.7 3.2 %shard_map.113 = (f32[33,32,256]{2,1,0:T(8,128)S(1)}, f32[4,32,256]{2,1,0:T(8,128)S(1)}, f32[32,64]{1,0:T(8,128)S(1)}, bf16[32,256,16]{2,1,0:T(8,128)(2,1)S(1)},...) custom-call(bf16[640,256]{1,0:T(8,128)(2,1)S(1)} %copy-done.5, ...), custom_call_target="tpu_custom_call" | custom-call | flops 2147483648 | bytes 1048576 | tf_op jit(solution)/shard_map/pallas_call | solution.py:428
  19.8 3.2 %shard_map.114 = (f32[33,32,256]{2,1,0:T(8,128)S(1)}, f32[4,32,256]{2,1,0:T(8,128)S(1)}) custom-call(f32[33,32,256]{2,1,0:T(8,128)S(1)} %get-tuple-element.36.refs_0_, f32[4,32,256]{2,1,0:T(8,128)S(1)} %get-tuple-element.37.refs_1_, bf16[32,256,16]{2,1,0:T(8,128)(2,1)S(1)} %get-tuple-element.38.refs_2_, bf16[4,256,16]{2,1,0:T(8,128)(2,1)S(1)} %get-tuple-element.39.refs_3_, ...), custom_call_target="tpu_custom_call" | custom-call | flops 268435456 | bytes 1048576 | tf_op jit(solution)/shard_map/pallas_call | solution.py:428
  23.0 0.6 collective-permute-done.4.refs_8_
  23.6 1.8 %collective-permute-start.7 = (bf16[640,256]{1,0:T(8,128)(2,1)S(1)}, bf16[640,256]{1,0:T(8,128)(2,1)S(1)}, u32[]{:S(2)}, u32[]{:S(2)}) collective-permute-start(bf16[640,256]{1,0:T(8,128)(2,1)S(1)} %collective-permute-done.2.refs_6_), channel_id=1, source_target_pairs={{0,4},{1,5},{2,6},{3,7},{4,0},{5,1},{6,2},{7,3},{8,12},{9,13},{10,... | collective-permute-start | bytes 983048 | tf_op jit(solution)/shard_map/ppermute | solution.py:443
  25.4 1.5 %collective-permute-start.8 = (bf16[640,256]{1,0:T(8,128)(2,1)S(1)}, bf16[640,256]{1,0:T(8,128)(2,1)S(1)}, u32[]{:S(2)}, u32[]{:S(2)}) collective-permute-start(bf16[640,256]{1,0:T(8,128)(2,1)S(1)} %collective-permute-done.2.refs_6_), channel_id=1, source_target_pairs={{0,2},{1,3},{2,0},{3,1},{4,6},{5,7},{6,4},{7,5},{8,10},{9,11},{10,... | collective-permute-start | bytes 983048 | tf_op jit(solution)/shard_map/ppermute | solution.py:443
  26.9 0.3 collective-permute-start.11
  27.2 0.5 collective-permute-start.12
  27.7 6.3 %shard_map.115 = (f32[33,32,256]{2,1,0:T(8,128)S(1)}, f32[4,32,256]{2,1,0:T(8,128)S(1)}) custom-call(f32[33,32,256]{2,1,0:T(8,128)S(1)} %get-tuple-element.42.refs_0_, f32[4,32,256]{2,1,0:T(8,128)S(1)} %get-tuple-element.43.refs_1_, bf16[32,256,16]{2,1,0:T(8,128)(2,1)S(1)} %get-tuple-element.38.refs_2_, bf16[4,256,16]{2,1,0:T(8,128)(2,1)S(1)} %get-tuple-element.39.refs_3_, ...), custom_call_target="tpu_custom_call" | custom-call | flops 805306368 | bytes 1048576 | tf_op jit(solution)/shard_map/pallas_call | solution.py:428
  34.0 0.2 collective-permute-done.7.refs_6_
  34.3 1.8 %collective-permute-done.8.refs_7_ = bf16[640,256]{1,0:T(8,128)(2,1)S(1)} collective-permute-done((bf16[640,256]{1,0:T(8,128)(2,1)S(1)}, bf16[640,256]{1,0:T(8,128)(2,1)S(1)}, u32[]{:S(2)}, u32[]{:S(2)}) %collective-permute-start.8) | collective-permute-done | bytes 327712 | tf_op jit(solution)/shard_map/ppermute | solution.py:443
  36.0 1.6 %collective-permute-start.10 = (bf16[320,256]{1,0:T(8,128)(2,1)S(1)}, bf16[320,256]{1,0:T(8,128)(2,1)S(1)}, u32[]{:S(2)}, u32[]{:S(2)}) collective-permute-start(bf16[320,256]{1,0:T(8,128)(2,1)S(1)} %slice.7), channel_id=1, source_target_pairs={{0,2},{1,3},{2,0},{3,1},{4,6},{5,7},{6,4},{7,5},{8,10},{9,11},{10,... | collective-permute-start | bytes 491528 | tf_op jit(solution)/shard_map/ppermute | solution.py:443
  37.6 0.4 collective-permute-start.9
  38.0 3.8 %shard_map.116 = (f32[33,32,256]{2,1,0:T(8,128)S(1)}, f32[4,32,256]{2,1,0:T(8,128)S(1)}) custom-call(f32[33,32,256]{2,1,0:T(8,128)S(1)} %get-tuple-element.51.refs_0_, f32[4,32,256]{2,1,0:T(8,128)S(1)} %get-tuple-element.52.refs_1_, bf16[32,256,16]{2,1,0:T(8,128)(2,1)S(1)} %get-tuple-element.38.refs_2_, bf16[4,256,16]{2,1,0:T(8,128)(2,1)S(1)} %get-tuple-element.39.refs_3_, ...), custom_call_target="tpu_custom_call" | custom-call | flops 536870912 | bytes 1048576 | tf_op jit(solution)/shard_map/pallas_call | solution.py:428
  41.8 1.2 %collective-permute-done.9.refs_8_ = bf16[320,256]{1,0:T(8,128)(2,1)S(1)} collective-permute-done((bf16[320,256]{1,0:T(8,128)(2,1)S(1)}, bf16[320,256]{1,0:T(8,128)(2,1)S(1)}, u32[]{:S(2)}, u32[]{:S(2)}) %collective-permute-start.9) | collective-permute-done | bytes 163872 | tf_op jit(solution)/shard_map/ppermute | solution.py:443
  43.0 4.3 %shard_map.117 = (f32[16,32,256]{2,1,0:T(8,128)S(1)}, f32[2,32,256]{2,1,0:T(8,128)S(1)}, f32[18,32,256]{2,1,0:T(8,128)S(1)}) custom-call(f32[33,32,256]{2,1,0:T(8,128)S(1)} %get-tuple-element.55.refs_0_, f32[4,32,256]{2,1,0:T(8,128)S(1)} %get-tuple-element.56.refs_1_, bf16[32,256,16]{2,1,0:T(8,128)(2,1)S(1)} %get-tuple-element.38.refs_2_, ...), custom_call_target="tpu_custom_call" | custom-call | flops 536870912 | bytes 1048576 | tf_op jit(solution)/shard_map/pallas_call | solution.py:428
  47.3 0.1 collective-permute-start.13
  47.4 2.0 %collective-permute-done.13.given_ref = f32[18,32,256]{2,1,0:T(8,128)S(1)} collective-permute-done((f32[18,32,256]{2,1,0:T(8,128)S(1)}, f32[18,32,256]{2,1,0:T(8,128)S(1)}, u32[]{:S(2)}, u32[]{:S(2)}) %collective-permute-start.13) | collective-permute-done | bytes 589856 | tf_op jit(solution)/shard_map/ppermute | solution.py:443
  49.4 1.3 %shard_map.118 = (f32[16,64,256]{2,1,0:T(8,128)S(1)}, f32[16,32,128]{2,1,0:T(8,128)S(1)}) custom-call(f32[16,32,256]{2,1,0:T(8,128)S(1)} %get-tuple-element.61.total_ref, f32[2,32,256]{2,1,0:T(8,128)S(1)} %get-tuple-element.62.far_ref, f32[18,32,256]{2,1,0:T(8,128)S(1)} %collective-permute-done.13.given_ref, bf16[16,32,256]{2,1,0:T(8,128)(2,1)S(1)} %copy-done.2, ...), custom_call_target="tpu_custom_call" | custom-call | flops 268435456 | bytes 1048576 | tf_op jit(solution)/shard_map/pallas_call | solution.py:428
  50.7 12.6 %all_to_all.5.products_ref = f32[16,32,128]{2,1,0:T(8,128)S(1)} all-to-all(f32[16,32,128]{2,1,0:T(8,128)S(1)} %get-tuple-element.65), channel_id=1, replica_groups=mesh['group'=2,'clus'=16] {'clus'}, dimensions={0} | all-to-all | bytes 524288 | tf_op jit(solution)/shard_map/all_to_all | solution.py:586
  63.3 3.9 %shard_map.119 = (f32[16,32,256]{2,1,0:T(8,128)}, f32[32,32]{1,0:T(8,128)}, f32[32,32]{1,0:T(8,128)}) custom-call(f32[16,32,128]{2,1,0:T(8,128)S(1)} %all_to_all.5.products_ref, f32[16,64,256]{2,1,0:T(8,128)S(1)} %get-tuple-element.66.stacked_ref), custom_call_target="tpu_custom_call" | custom-call | bytes 1048576 | tf_op jit(solution)/shard_map/pallas_call | solution.py:428
  (25 shorter events, 0.1 us)
Async XLA Ops:
  2.8 8.8 %collective-permute-start = (bf16[640,256]{1,0:T(8,128)(2,1)}, bf16[640,256]{1,0:T(8,128)(2,1)S(1)}, u32[]{:S(2)}, u32[]{:S(2)}) collective-permute-start(bf16[640,256]{1,0:T(8,128)(2,1)} %get-tuple-element.35.refs_0_.refs_6_), channel_id=1, source_target_pairs={{0,1},{1,0},{2,3},{3,2},{4,5},{5,4},{6,7},{7,6},{8,9},{9,8},{10,11... | collective-permute-start | bytes 983048 | tf_op jit(solution)/shard_map/ppermute | solution.py:443
  3.3 20.3 %collective-permute-start.2 = (bf16[640,256]{1,0:T(8,128)(2,1)}, bf16[640,256]{1,0:T(8,128)(2,1)S(1)}, u32[]{:S(2)}, u32[]{:S(2)}) collective-permute-start(bf16[640,256]{1,0:T(8,128)(2,1)} %get-tuple-element.35.refs_0_.refs_6_), channel_id=1, source_target_pairs={{0,12},{1,13},{2,14},{3,15},{4,8},{5,9},{6,10},{7,11},{8,4},{9,5},... | collective-permute-start | bytes 983048 | tf_op jit(solution)/shard_map/ppermute | solution.py:443
  7.9 1.8 %collective-permute-start.1 = (s32[16,64]{1,0:T(8,128)}, s32[16,64]{1,0:T(8,128)S(1)}, u32[]{:S(2)}, u32[]{:S(2)}) collective-permute-start(s32[16,64]{1,0:T(8,128)} %refs_2_.1), channel_id=1, source_target_pairs={{0,1},{1,0},{2,3},{3,2},{4,5},{5,4},{6,7},{7,6},{8,9},{9,8},{10,11... | collective-permute-start | bytes 12296 | tf_op jit(solution)/shard_map/ppermute | solution.py:443
  8.1 14.9 %collective-permute-start.3 = (bf16[320,256]{1,0:T(8,128)(2,1)}, bf16[320,256]{1,0:T(8,128)(2,1)S(1)}, u32[]{:S(2)}, u32[]{:S(2)}) collective-permute-start(bf16[320,256]{1,0:T(8,128)(2,1)} %get-tuple-element.44), channel_id=1, source_target_pairs={{0,4},{1,5},{2,6},{3,7},{4,0},{5,1},{6,2},{7,3},{8,12},{9,13},{10,... | collective-permute-start | bytes 491528 | tf_op jit(solution)/shard_map/ppermute | solution.py:443
  8.1 15.5 %collective-permute-start.5 = (bf16[320,256]{1,0:T(8,128)(2,1)}, bf16[320,256]{1,0:T(8,128)(2,1)S(1)}, u32[]{:S(2)}, u32[]{:S(2)}) collective-permute-start(bf16[320,256]{1,0:T(8,128)(2,1)} %get-tuple-element.44), channel_id=1, source_target_pairs={{0,2},{1,3},{2,0},{3,1},{4,6},{5,7},{6,4},{7,5},{8,10},{9,11},{10,... | collective-permute-start | bytes 491528 | tf_op jit(solution)/shard_map/ppermute | solution.py:443
  9.6 14.0 %collective-permute-start.4 = (bf16[320,256]{1,0:T(8,128)(2,1)}, bf16[320,256]{1,0:T(8,128)(2,1)S(1)}, u32[]{:S(2)}, u32[]{:S(2)}) collective-permute-start(bf16[320,256]{1,0:T(8,128)(2,1)} %get-tuple-element.45), channel_id=1, source_target_pairs={{0,4},{1,5},{2,6},{3,7},{4,0},{5,1},{6,2},{7,3},{8,12},{9,13},{10,... | collective-permute-start | bytes 491528 | tf_op jit(solution)/shard_map/ppermute | solution.py:443
  11.7 11.9 %collective-permute-start.6 = (bf16[320,256]{1,0:T(8,128)(2,1)}, bf16[320,256]{1,0:T(8,128)(2,1)S(1)}, u32[]{:S(2)}, u32[]{:S(2)}) collective-permute-start(bf16[320,256]{1,0:T(8,128)(2,1)} %get-tuple-element.45), channel_id=1, source_target_pairs={{0,2},{1,3},{2,0},{3,1},{4,6},{5,7},{6,4},{7,5},{8,10},{9,11},{10,... | collective-permute-start | bytes 491528 | tf_op jit(solution)/shard_map/ppermute | solution.py:443
  12.2 1.0 %copy-start = (f32[16,32,256]{2,1,0:T(8,128)S(1)}, f32[16,32,256]{2,1,0:T(8,128)}, u32[]{:S(2)}) copy-start(f32[16,32,256]{2,1,0:T(8,128)} %block_ref.3) | copy-start | bytes 1572868
  13.2 1.0 %copy-start.4 = (f32[16,32,256]{2,1,0:T(8,128)S(1)}, f32[16,32,256]{2,1,0:T(8,128)}, u32[]{:S(2)}) copy-start(f32[16,32,256]{2,1,0:T(8,128)} %refs_5_.1) | copy-start | bytes 1572868
  14.3 1.0 %copy-start.5 = (bf16[640,256]{1,0:T(8,128)(2,1)S(1)}, bf16[640,256]{1,0:T(8,128)(2,1)}, u32[]{:S(2)}) copy-start(bf16[640,256]{1,0:T(8,128)(2,1)} %get-tuple-element.35.refs_0_.refs_6_) | copy-start | bytes 983044
  15.2 0.7 %copy-start.7 = (f32[32,32]{1,0:T(8,128)S(1)}, f32[32,32]{1,0:T(8,128)}, u32[]{:S(2)}) copy-start(f32[32,32]{1,0:T(8,128)} %refs_6_.1) | copy-start | bytes 12292
  16.0 0.7 %copy-start.8 = (s32[16,64]{1,0:T(8,128)S(1)}, s32[16,64]{1,0:T(8,128)}, u32[]{:S(2)}) copy-start(s32[16,64]{1,0:T(8,128)} %refs_2_.1) | copy-start | bytes 12292
  16.6 3.2 %copy-start.6 = (bf16[640,256]{1,0:T(8,128)(2,1)S(1)}, bf16[640,256]{1,0:T(8,128)(2,1)}, u32[]{:S(2)}) copy-start(bf16[640,256]{1,0:T(8,128)(2,1)} %get-tuple-element.35.refs_0_.refs_6_) | copy-start | bytes 983044
  23.6 10.6 %collective-permute-start.7 = (bf16[640,256]{1,0:T(8,128)(2,1)S(1)}, bf16[640,256]{1,0:T(8,128)(2,1)S(1)}, u32[]{:S(2)}, u32[]{:S(2)}) collective-permute-start(bf16[640,256]{1,0:T(8,128)(2,1)S(1)} %collective-permute-done.2.refs_6_), channel_id=1, source_target_pairs={{0,4},{1,5},{2,6},{3,7},{4,0},{5,1},{6,2},{7,3},{8,12},{9,13},{10,... | collective-permute-start | bytes 983048 | tf_op jit(solution)/shard_map/ppermute | solution.py:443
  25.4 10.6 %collective-permute-start.8 = (bf16[640,256]{1,0:T(8,128)(2,1)S(1)}, bf16[640,256]{1,0:T(8,128)(2,1)S(1)}, u32[]{:S(2)}, u32[]{:S(2)}) collective-permute-start(bf16[640,256]{1,0:T(8,128)(2,1)S(1)} %collective-permute-done.2.refs_6_), channel_id=1, source_target_pairs={{0,2},{1,3},{2,0},{3,1},{4,6},{5,7},{6,4},{7,5},{8,10},{9,11},{10,... | collective-permute-start | bytes 983048 | tf_op jit(solution)/shard_map/ppermute | solution.py:443
  26.9 14.9 %collective-permute-start.11 = (bf16[320,256]{1,0:T(8,128)(2,1)S(1)}, bf16[320,256]{1,0:T(8,128)(2,1)S(1)}, u32[]{:S(2)}, u32[]{:S(2)}) collective-permute-start(bf16[320,256]{1,0:T(8,128)(2,1)S(1)} %collective-permute-done.5.refs_9_), channel_id=1, source_target_pairs={{0,4},{1,5},{2,6},{3,7},{4,0},{5,1},{6,2},{7,3},{8,12},{9,13},{10,... | collective-permute-start | bytes 491528 | tf_op jit(solution)/shard_map/ppermute | solution.py:443
  27.2 14.5 %collective-permute-start.12 = (bf16[320,256]{1,0:T(8,128)(2,1)S(1)}, bf16[320,256]{1,0:T(8,128)(2,1)S(1)}, u32[]{:S(2)}, u32[]{:S(2)}) collective-permute-start(bf16[320,256]{1,0:T(8,128)(2,1)S(1)} %collective-permute-done.4.refs_8_), channel_id=1, source_target_pairs={{0,2},{1,3},{2,0},{3,1},{4,6},{5,7},{6,4},{7,5},{8,10},{9,11},{10,... | collective-permute-start | bytes 491528 | tf_op jit(solution)/shard_map/ppermute | solution.py:443
  36.0 5.8 %collective-permute-start.10 = (bf16[320,256]{1,0:T(8,128)(2,1)S(1)}, bf16[320,256]{1,0:T(8,128)(2,1)S(1)}, u32[]{:S(2)}, u32[]{:S(2)}) collective-permute-start(bf16[320,256]{1,0:T(8,128)(2,1)S(1)} %slice.7), channel_id=1, source_target_pairs={{0,2},{1,3},{2,0},{3,1},{4,6},{5,7},{6,4},{7,5},{8,10},{9,11},{10,... | collective-permute-start | bytes 491528 | tf_op jit(solution)/shard_map/ppermute | solution.py:443
  37.6 5.4 %collective-permute-start.9 = (bf16[320,256]{1,0:T(8,128)(2,1)S(1)}, bf16[320,256]{1,0:T(8,128)(2,1)S(1)}, u32[]{:S(2)}, u32[]{:S(2)}) collective-permute-start(bf16[320,256]{1,0:T(8,128)(2,1)S(1)} %slice.6), channel_id=1, source_target_pairs={{0,4},{1,5},{2,6},{3,7},{4,0},{5,1},{6,2},{7,3},{8,12},{9,13},{10,... | collective-permute-start | bytes 491528 | tf_op jit(solution)/shard_map/ppermute | solution.py:443
  43.0 6.4 %copy-start.1 = (f32[16,32,256]{2,1,0:T(8,128)S(1)}, f32[16,32,256]{2,1,0:T(8,128)}, u32[]{:S(2)}) copy-start(f32[16,32,256]{2,1,0:T(8,128)} %block_ref.3) | copy-start | bytes 1572868
  43.0 6.4 %copy-start.2 = (bf16[16,32,256]{2,1,0:T(8,128)(2,1)S(1)}, bf16[16,32,256]{2,1,0:T(8,128)(2,1)}, u32[]{:S(2)}) copy-start(bf16[16,32,256]{2,1,0:T(8,128)(2,1)} %basis_ref.3) | copy-start | bytes 786436
  43.0 6.4 %copy-start.3 = (f32[16,32]{1,0:T(8,128)S(1)}, f32[16,32]{1,0:T(8,128)}, u32[]{:S(2)}) copy-start(f32[16,32]{1,0:T(8,128)} %scales_ref.3) | copy-start | bytes 6148
  47.3 2.1 %collective-permute-start.13 = (f32[18,32,256]{2,1,0:T(8,128)S(1)}, f32[18,32,256]{2,1,0:T(8,128)S(1)}, u32[]{:S(2)}, u32[]{:S(2)}) collective-permute-start(f32[18,32,256]{2,1,0:T(8,128)S(1)} %get-tuple-element.63), channel_id=1, source_target_pairs={{0,1},{1,0},{2,3},{3,2},{4,5},{5,4},{6,7},{7,6},{8,9},{9,8},{10,11... | collective-permute-start | bytes 1769480 | tf_op jit(solution)/shard_map/ppermute | solution.py:443
